TPU v7x, 128 devices: a whole 4x4x4 slice. The times are simulated.
128 devices in a mesh: dp: 16 (over z, x_lo, core), head: 8 (over y, x_hi).
Axes of the slice: x: 4 (x_hi: 2, x_lo: 2; x = x_hi * 2 + x_lo), y: 4, z: 4, core: 2. Of those that a mesh axis runs over, the one named last changes fastest.
Arguments:
- query: bfloat16 [16384, 4096], P(('dp', 'head')), may hold values from -6 to 6
- key_states: bfloat16 [16384, 1024], P(('dp', 'head')), may hold values from -6 to 6
- value_states: bfloat16 [16384, 1024], P(('dp', 'head')), may hold values from -6 to 6
- grad_attended: bfloat16 [16384, 4096], P(('dp', 'head')), may hold values from -6 to 6
- query_gain: float32 [128], replicated, may hold values from 0.6 to 5.5
- key_gain: float32 [128], replicated, may hold values from 0.6 to 5.5
- doc_lengths: int32 [16, 8], replicated, may hold values from 1 to 512, 1024 in all within a row
Outputs:
- attended: bfloat16 [16384, 4096], P(('dp', 'head'))
- grad_query: bfloat16 [16384, 4096], P(('dp', 'head'))
- grad_key: bfloat16 [16384, 1024], P(('dp', 'head'))
- grad_value: bfloat16 [16384, 1024], P(('dp', 'head'))
- grad_query_gain: float32 [128], replicated
- grad_key_gain: float32 [128], replicated
Inputs may be any that keep to these rules, and one draw needn't show every extreme that they name: `doc_lengths`: each row sums to 1024.
All inputs are finite; a program needn't handle non-finite values.
Results may differ from a plain program's by a relative error of at most 0.007.
The roundings to bfloat16 on the way count: a program that leaves them out, or rounds other values in their place, can miss the bound.
Values may be sent and summed in bfloat16 or wider, within the bound.
No kernel may reach another device: no remote copies, remote signals or barrier semaphores. Data moves between devices by JAX's collectives and lax.ppermute only.
A program may use at most 192 MiB of HBM per device.

v0:
```python
import functools
import math

import jax
import jax.numpy as jnp
from jax import lax
from jax.experimental import pallas as pl
from jax.experimental.pallas import tpu as pltpu
from jax.sharding import PartitionSpec as P

H = 32
KVH = 8
HD = 128
GROUP = H // KVH
MOST_DOC = 512
BLK = 128
WINDOWS = MOST_DOC // BLK + 1
EPS = 1e-06
FACTOR = HD ** (-0.5)
EXP2_FACTOR = FACTOR * math.log2(math.e)
CHUNKS = ((0, 4),)
F32 = jnp.float32
BF16 = jnp.bfloat16


def dot(left, right, contract):
    return lax.dot_general(left, right, ((contract[:1], contract[1:]), ((), ())), preferred_element_type=F32)


def copies_kernel(plan, n_in, *refs):
    sems = refs[-1]
    moves = []
    for i, (src, src_at, dst, dst_at) in enumerate(plan):
        moves.append(pltpu.make_async_copy(refs[src].at[src_at], refs[n_in + dst].at[dst_at], sems.at[i]))
    for move in moves:
        move.start()
    for move in moves:
        move.wait()


def run_copies(plan, arrays, shapes, sources, targets):
    return pl.pallas_call(
        functools.partial(copies_kernel, plan, len(arrays)),
        out_shape=[jax.ShapeDtypeStruct(s, BF16) for s in shapes],
        in_specs=[pl.BlockSpec(memory_space=sources)] * len(arrays),
        out_specs=[pl.BlockSpec(memory_space=targets)] * len(shapes),
        scratch_shapes=[pltpu.SemaphoreType.DMA((len(plan),))],
        compiler_params=pltpu.CompilerParams(vmem_limit_bytes=32 * 1024 * 1024),
    )(*arrays)


def cols(first, width):
    return pl.ds(first, width)


def pack(query, key_states, value_states, grad_attended, chunk, first, members):
    rows = query.shape[0]
    start, count = chunk
    width = count * HD
    plan = []
    allrows = pl.ds(0, rows)
    base = 2 * HD if first else 0
    for m in range(members):
        if first:
            plan.append((0, (allrows, cols(m * HD, HD)), 0, (m, allrows, cols(0, HD))))
            plan.append((1, (allrows, cols(m * HD, HD)), 0, (m, allrows, cols(HD, HD))))
        at = (m * GROUP + start) * HD
        plan.append((2, (allrows, cols(at, width)), 0, (m, allrows, cols(base, width))))
        plan.append((3, (allrows, cols(at, width)), 0, (m, allrows, cols(base + width, width))))
    shape = (members, rows, base + 2 * width)
    return run_copies(
        plan, (key_states, value_states, query, grad_attended), [shape], pl.ANY, pltpu.VMEM
    )[0]


def unpack(parts, members, rows):
    plan = []
    allrows = pl.ds(0, rows)
    for index, (start, count) in enumerate(CHUNKS):
        width = count * HD
        for m in range(members):
            at = (m * GROUP + start) * HD
            plan.append((index, (m, allrows, cols(0, width)), 0, (allrows, cols(at, width))))
            plan.append((index, (m, allrows, cols(width, width)), 1, (allrows, cols(at, width))))
            if index == len(CHUNKS) - 1:
                plan.append((index, (m, allrows, cols(2 * width, HD)), 2, (allrows, cols(m * HD, HD))))
                plan.append((index, (m, allrows, cols(2 * width + HD, HD)), 3, (allrows, cols(m * HD, HD))))
    shapes = [(rows, H * HD), (rows, H * HD), (rows, KVH * HD), (rows, KVH * HD)]
    return run_copies(plan, parts, shapes, pltpu.VMEM, pl.ANY)


def unit_of(raw):
    values = raw.astype(F32)
    inverse = lax.rsqrt(jnp.mean(values * values, axis=-1, keepdims=True) + EPS)
    return values * inverse, inverse


def attend_kernel(count, first, last, *refs):
    refs = list(refs)
    lengths_ref, q_gain_ref, k_gain_ref, kv_ref = refs[:4]
    del refs[:4]
    x_ref = kv_ref if first else refs.pop(0)
    if not first:
        dk_in, dv_in, gains_in = refs[:3]
        del refs[:3]
    y_ref = refs.pop(0)
    if not last:
        dk_ref, dv_ref = refs[:2]
        del refs[:2]
    gains_ref = refs.pop(0)
    if last:
        dk_ref, dv_ref = refs[:2]
        del refs[:2]
    kn_ref, qn_ref, g_ref, out_ref, dq_ref, bias_ref = refs
    base = 2 * HD if first else 0
    width = count * HD
    span = kv_ref.shape[0]
    replica = lax.axis_index("dp")
    q_gain = q_gain_ref[...]
    k_gain = k_gain_ref[...]

    k_unit, _ = unit_of(kv_ref[:, :HD])
    kn_ref[...] = (k_unit * k_gain).astype(BF16)
    if first:
        dk_ref[...] = jnp.zeros_like(dk_ref)
        dv_ref[...] = jnp.zeros_like(dv_ref)
        gains_ref[...] = jnp.zeros_like(gains_ref)
    else:
        dk_ref[...] = dk_in[...]
        dv_ref[...] = dv_in[...]
        gains_ref[...] = gains_in[...]
    ends = []
    total = jnp.int32(0)
    for d in range(lengths_ref.shape[1]):
        total = total + lengths_ref[replica, d]
        ends.append(total)

    def block(i, carry):
        row0 = pl.multiple_of(i * BLK, BLK)
        rows = pl.ds(row0, BLK)
        places = row0 + lax.broadcasted_iota(jnp.int32, (BLK, BLK), 0)
        begins = jnp.zeros((BLK, BLK), jnp.int32)
        begin0 = jnp.int32(0)
        for end in ends:
            begins = jnp.where(end <= places, end, begins)
            begin0 = jnp.where(end <= row0, end, begin0)
        first_block = begin0 // BLK
        needed = i - first_block + 1
        units = []
        for h in range(count):
            unit, inverse = unit_of(x_ref[rows, base + h * HD : base + (h + 1) * HD])
            units.append((unit, inverse))
            qn_ref[h * BLK : (h + 1) * BLK, :] = (unit * q_gain).astype(BF16)
            g_ref[h * BLK : (h + 1) * BLK, :] = x_ref[
                rows, base + width + h * HD : base + width + (h + 1) * HD
            ]
        for blocks in range(1, WINDOWS + 1):

            @pl.when(needed == blocks)
            def _():
                keys = blocks * BLK
                k0 = pl.multiple_of(first_block * BLK, BLK)
                window = pl.ds(k0, keys)
                lane = k0 + lax.broadcasted_iota(jnp.int32, (BLK, BLK), 1)
                for t in range(blocks):
                    place = lane + t * BLK
                    seen = place >= begins
                    if t == blocks - 1:
                        seen = seen & (place <= places)
                    bias_ref[:, t * BLK : (t + 1) * BLK] = jnp.where(seen, 0.0, -1e30)
                qn = qn_ref[...]
                g = g_ref[...]
                kn = kn_ref[window, :]
                v = kv_ref[window, HD : 2 * HD]
                bias = bias_ref[:, :keys]
                scores = dot(qn, kn, (1, 1)).reshape(count, BLK, keys) + bias[None]
                scores = scores.reshape(count * BLK, keys)
                peak = jnp.max(scores, axis=1, keepdims=True)
                raised = jnp.exp2((scores - peak) * EXP2_FACTOR)
                weights = raised * (1.0 / jnp.sum(raised, axis=1, keepdims=True))
                rounded = weights.astype(BF16)
                out = dot(rounded, v, (1, 0))
                out_ref[...] = out
                dv_ref[window, :] += dot(rounded, g, (0, 0))
                dweights = dot(g, v, (1, 1))
                delta = jnp.sum(g.astype(F32) * out, axis=1, keepdims=True)
                dscores = (weights * (dweights - delta) * FACTOR).astype(BF16)
                dq_ref[...] = dot(dscores, kn, (1, 0))
                dk_ref[window, :] += dot(dscores, qn, (0, 0))

        part = jnp.zeros((8, HD), F32)
        for h in range(count):
            unit, inverse = units[h]
            here = slice(h * BLK, (h + 1) * BLK)
            y_ref[rows, h * HD : (h + 1) * HD] = out_ref[here, :].astype(BF16)
            dq = dq_ref[here, :]
            scaled = dq * q_gain
            back = inverse * (scaled - unit * jnp.mean(scaled * unit, axis=-1, keepdims=True))
            y_ref[rows, width + h * HD : width + (h + 1) * HD] = back.astype(BF16)
            part = part + jnp.sum((dq * unit).reshape(BLK // 8, 8, HD), axis=0)
        gains_ref[0:8, :] += part
        return carry

    lax.fori_loop(0, span // BLK, block, 0)

    if last:
        for r in range(0, span, BLK):
            rows = slice(r, r + BLK)
            unit, inverse = unit_of(kv_ref[rows, :HD])
            dk = dk_ref[rows, :]
            scaled = dk * k_gain
            back = inverse * (scaled - unit * jnp.mean(scaled * unit, axis=-1, keepdims=True))
            y_ref[rows, 2 * width : 2 * width + HD] = back.astype(BF16)
            y_ref[rows, 2 * width + HD : 2 * width + 2 * HD] = dv_ref[rows, :].astype(BF16)
            gains_ref[8:16, :] += jnp.sum((dk * unit).reshape(BLK // 8, 8, HD), axis=0)


def run_attend(lengths, q_gain, k_gain, kv, x, before, count, last):
    first = x is None
    span = kv.shape[0]
    vmem = pl.BlockSpec(memory_space=pltpu.VMEM)
    args = [lengths, q_gain, k_gain, kv]
    if not first:
        args += [x, *before]
    sums = jax.ShapeDtypeStruct((span, HD), F32)
    out_shape = [jax.ShapeDtypeStruct((span, 2 * count * HD + (2 * HD if last else 0)), BF16)]
    if not last:
        out_shape += [sums, sums]
    out_shape += [jax.ShapeDtypeStruct((16, HD), F32)]
    scratch = [pltpu.VMEM((span, HD), F32)] * 2 if last else []
    scratch += [
        pltpu.VMEM((span, HD), BF16),
        pltpu.VMEM((count * BLK, HD), BF16),
        pltpu.VMEM((count * BLK, HD), BF16),
        pltpu.VMEM((count * BLK, HD), F32),
        pltpu.VMEM((count * BLK, HD), F32),
        pltpu.VMEM((BLK, WINDOWS * BLK), F32),
    ]
    return pl.pallas_call(
        functools.partial(attend_kernel, count, first, last),
        out_shape=out_shape,
        in_specs=[pl.BlockSpec(memory_space=pltpu.SMEM)] + [vmem] * (len(args) - 1),
        out_specs=[vmem] * len(out_shape),
        scratch_shapes=scratch,
        compiler_params=pltpu.CompilerParams(vmem_limit_bytes=48 * 1024 * 1024),
        cost_estimate=pl.CostEstimate(
            flops=5 * 2 * count * span * 384 * HD, bytes_accessed=4 * span * count * HD * 2, transcendentals=count * span * 384
        ),
    )(*args)


def sum_everywhere(x):
    for axis, bits in (("dp", (0, 2, 3, 1)), ("head", (0, 1, 2))):
        size = lax.axis_size(axis)
        for bit in bits:
            x = x + lax.ppermute(x, axis, [(i, i ^ 1 << bit) for i in range(size)])
    return x


def on_device(query, key_states, value_states, grad_attended, query_gain, key_gain, doc_lengths):
    replicas = lax.axis_size("dp")
    members = lax.axis_size("head")
    rows = query.shape[0]
    span = rows * members
    q_gain = query_gain.reshape(1, HD)
    k_gain = key_gain.reshape(1, HD)
    arrived = []
    for index, chunk in enumerate(CHUNKS):
        packed = pack(query, key_states, value_states, grad_attended, chunk, index == 0, members)
        moved = lax.all_to_all(packed, "head", split_axis=0, concat_axis=0, tiled=True)
        arrived.append(moved.reshape(span, packed.shape[2]))
    before = None
    results = []
    for index, (_, count) in enumerate(CHUNKS):
        last = index == len(CHUNKS) - 1
        x = None if index == 0 else arrived[index]
        y, *before = run_attend(doc_lengths, q_gain, k_gain, arrived[0], x, before, count, last)
        results.append(
            lax.all_to_all(
                y.reshape(members, rows, y.shape[1]), "head", split_axis=0, concat_axis=0, tiled=True
            )
        )
    gains = before[-1]
    totals = sum_everywhere(
        jnp.stack([jnp.sum(gains[:8], axis=0), jnp.sum(gains[8:], axis=0)])
    )
    finals = unpack(results, members, rows)
    all_tokens = rows * replicas * members
    return (
        *finals,
        totals[0] * (all_tokens * H) ** (-0.5),
        totals[1] * (all_tokens * KVH) ** (-0.5),
    )


def solution(mesh):
    rows = P(("dp", "head"), None)
    in_specs = (rows, rows, rows, rows, P(), P(), P())
    out_specs = (rows, rows, rows, rows, P(), P())
    return jax.shard_map(
        on_device, mesh=mesh, in_specs=in_specs, out_specs=out_specs, check_vma=False
    )
```

profile of v0, /device:TPU:0, one launch (start us, length us, event | category | flops | bytes accessed | tf_op | source)
XLA Modules:
  0.0 113.2 jit_solution(114281046912927836)
XLA Ops:
  0.6 0.0 copy-start.1
  0.6 1.2 %copy-done.1 = bf16[128,4096]{1,0:T(8,128)(2,1)S(1)} copy-done((bf16[128,4096]{1,0:T(8,128)(2,1)S(1)}, bf16[128,4096]{1,0:T(8,128)(2,1)}, u32[]{:S(2)}) %copy-start.1) | copy-done | bytes 1048600
  1.9 0.0 copy-start.2
  1.9 1.2 %copy-done.2 = bf16[128,4096]{1,0:T(8,128)(2,1)S(1)} copy-done((bf16[128,4096]{1,0:T(8,128)(2,1)S(1)}, bf16[128,4096]{1,0:T(8,128)(2,1)}, u32[]{:S(2)}) %copy-start.2) | copy-done | bytes 1048600
  3.1 0.0 copy-start.3
  3.1 0.9 copy-done.3
  4.0 0.0 copy-start.4
  4.0 0.9 copy-done.4
  5.0 2.3 %shard_map.118 = bf16[8,128,1280]{2,1,0:T(8,128)(2,1)} custom-call(bf16[128,1024]{1,0:T(8,128)(2,1)S(1)} %copy-done.3, bf16[128,1024]{1,0:T(8,128)(2,1)S(1)} %copy-done.4, bf16[128,4096]{1,0:T(8,128)(2,1)S(1)} %copy-done.1, bf16[128,4096]{1,0:T(8,128)(2,1)S(1)} %copy-done.2), custom_call_target="tpu_custom_call" | custom-call | tf_op jit(solution)/shard_map/pallas_call | solution.py:42
  7.3 0.0 copy-start.7
  7.3 0.0 copy-start.5
  7.3 0.0 copy-start.6
  7.3 7.2 %all-to-all-start = ((bf16[8,128,1280]{2,1,0:T(8,128)(2,1)}), bf16[8,128,1280]{2,1,0:T(8,128)(2,1)S(1)}, u32[]{:S(2)}, u32[]{:S(2)}) async-start(bf16[8,128,1280]{2,1,0:T(8,128)(2,1)} %shard_map.118), calls=%async_computation | async-start | bytes 5242880 | tf_op jit(solution)/shard_map/all_to_all | solution.py:270
  14.5 0.0 copy-done.7
  14.5 0.1 copy.13.refs_0_
  14.5 34.0 %all-to-all-done = bf16[8,128,1280]{2,1,0:T(8,128)(2,1)S(1)} async-done(((bf16[8,128,1280]{2,1,0:T(8,128)(2,1)}), bf16[8,128,1280]{2,1,0:T(8,128)(2,1)S(1)}, u32[]{:S(2)}, u32[]{:S(2)}) %all-to-all-start) | async-done | bytes 2621472 | tf_op jit(solution)/shard_map/all_to_all | solution.py:270
  48.6 0.0 copy-done.5
  48.6 0.0 copy-done.6
  48.6 13.8 %shard_map.119 = (bf16[1024,1280]{1,0:T(8,128)(2,1)S(1)}, f32[16,128]{1,0:T(8,128)S(1)}) custom-call(s32[16,8]{1,0:T(8,128)S(1)} %copy.13.refs_0_, f32[1,128]{1,0:T(1,128)S(1)} %bitcast.12, f32[1,128]{1,0:T(1,128)S(1)} %bitcast.13, bf16[1024,1280]{1,0:T(8,128)(2,1)S(1)} %bitcast.11), custom_call_target="tpu_custom_call" | custom-call | flops 2013265920 | bytes 4194304 | tf_op jit(solution)/shard_map/pallas_call | solution.py:239
  62.4 0.0 copy-start
  62.4 1.5 %copy-done = bf16[1024,1280]{1,0:T(8,128)(2,1)} copy-done((bf16[1024,1280]{1,0:T(8,128)(2,1)}, bf16[1024,1280]{1,0:T(8,128)(2,1)S(1)}, u32[]{:S(2)}) %copy-start) | copy-done | bytes 2621464
  63.9 3.6 %all-to-all-start.1 = ((bf16[8,128,1280]{2,1,0:T(8,128)(2,1)}), bf16[8,128,1280]{2,1,0:T(8,128)(2,1)S(1)}, u32[]{:S(2)}, u32[]{:S(2)}) async-start(bf16[8,128,1280]{2,1,0:T(8,128)(2,1)} %bitcast.10), calls=%async_computation.1 | async-start | bytes 5242880 | tf_op jit(solution)/shard_map/all_to_all | solution.py:279
  67.5 0.1 collective-permute-start
  67.6 1.1 collective-permute-done
  68.8 1.9 %collective-permute-start.1 = (f32[2,128]{1,0:T(2,128)S(1)}, f32[2,128]{1,0:T(2,128)S(1)}, u32[]{:S(2)}, u32[]{:S(2)}) collective-permute-start(f32[2,128]{1,0:T(2,128)S(1)} %fusion), channel_id=1, source_target_pairs={{0,32},{8,40},{16,48},{24,56},{32,0},{40,8},{48,16},{56,24},{64,96... | collective-permute-start | bytes 3080 | tf_op jit(solution)/shard_map/ppermute | solution.py:256
  70.7 1.7 %collective-permute-done.1 = f32[2,128]{1,0:T(2,128)S(1)} collective-permute-done((f32[2,128]{1,0:T(2,128)S(1)}, f32[2,128]{1,0:T(2,128)S(1)}, u32[]{:S(2)}, u32[]{:S(2)}) %collective-permute-start.1) | collective-permute-done | bytes 1056 | tf_op jit(solution)/shard_map/ppermute | solution.py:256
  72.4 3.9 %collective-permute-start.2 = (f32[2,128]{1,0:T(2,128)S(1)}, f32[2,128]{1,0:T(2,128)S(1)}, u32[]{:S(2)}, u32[]{:S(2)}) collective-permute-start(f32[2,128]{1,0:T(2,128)S(1)} %fusion.1), channel_id=1, source_target_pairs={{0,64},{8,72},{16,80},{24,88},{32,96},{40,104},{48,112},{56,120},{... | collective-permute-start | bytes 3080 | tf_op jit(solution)/shard_map/ppermute | solution.py:256
  76.3 1.5 %collective-permute-done.2 = f32[2,128]{1,0:T(2,128)S(1)} collective-permute-done((f32[2,128]{1,0:T(2,128)S(1)}, f32[2,128]{1,0:T(2,128)S(1)}, u32[]{:S(2)}, u32[]{:S(2)}) %collective-permute-start.2) | collective-permute-done | bytes 1056 | tf_op jit(solution)/shard_map/ppermute | solution.py:256
  77.9 0.6 collective-permute-start.3
  78.5 17.8 %collective-permute-done.3 = f32[2,128]{1,0:T(2,128)S(1)} collective-permute-done((f32[2,128]{1,0:T(2,128)S(1)}, f32[2,128]{1,0:T(2,128)S(1)}, u32[]{:S(2)}, u32[]{:S(2)}) %collective-permute-start.3) | collective-permute-done | bytes 1056 | tf_op jit(solution)/shard_map/ppermute | solution.py:256
  96.2 4.5 %collective-permute-start.4 = (f32[2,128]{1,0:T(2,128)S(1)}, f32[2,128]{1,0:T(2,128)S(1)}, u32[]{:S(2)}, u32[]{:S(2)}) collective-permute-start(f32[2,128]{1,0:T(2,128)S(1)} %add.24), channel_id=1, source_target_pairs={{0,1},{1,0},{2,3},{3,2},{4,5},{5,4},{6,7},{7,6},{8,9},{9,8},{10,11... | collective-permute-start | bytes 3080 | tf_op jit(solution)/shard_map/ppermute | solution.py:256
  100.7 1.5 %collective-permute-done.4 = f32[2,128]{1,0:T(2,128)S(1)} collective-permute-done((f32[2,128]{1,0:T(2,128)S(1)}, f32[2,128]{1,0:T(2,128)S(1)}, u32[]{:S(2)}, u32[]{:S(2)}) %collective-permute-start.4) | collective-permute-done | bytes 1056 | tf_op jit(solution)/shard_map/ppermute | solution.py:256
  102.3 0.6 collective-permute-start.5
  102.9 3.0 %collective-permute-done.5 = f32[2,128]{1,0:T(2,128)S(1)} collective-permute-done((f32[2,128]{1,0:T(2,128)S(1)}, f32[2,128]{1,0:T(2,128)S(1)}, u32[]{:S(2)}, u32[]{:S(2)}) %collective-permute-start.5) | collective-permute-done | bytes 1056 | tf_op jit(solution)/shard_map/ppermute | solution.py:256
  105.9 2.7 %collective-permute-start.6 = (f32[2,128]{1,0:T(2,128)S(1)}, f32[2,128]{1,0:T(2,128)S(1)}, u32[]{:S(2)}, u32[]{:S(2)}) collective-permute-start(f32[2,128]{1,0:T(2,128)S(1)} %add.26), channel_id=1, source_target_pairs={{0,4},{1,5},{2,6},{3,7},{4,0},{5,1},{6,2},{7,3},{8,12},{9,13},{10,... | collective-permute-start | bytes 3080 | tf_op jit(solution)/shard_map/ppermute | solution.py:256
  108.5 2.4 %collective-permute-done.6 = f32[2,128]{1,0:T(2,128)S(1)} collective-permute-done((f32[2,128]{1,0:T(2,128)S(1)}, f32[2,128]{1,0:T(2,128)S(1)}, u32[]{:S(2)}, u32[]{:S(2)}) %collective-permute-start.6) | collective-permute-done | bytes 1056 | tf_op jit(solution)/shard_map/ppermute | solution.py:256
  110.9 0.5 multiply_bitcast_fusion
  111.5 0.0 all-to-all-done.1.refs_0_
  111.5 1.7 %shard_map.120 = (bf16[128,4096]{1,0:T(8,128)(2,1)}, bf16[128,4096]{1,0:T(8,128)(2,1)}, bf16[128,1024]{1,0:T(8,128)(2,1)}, bf16[128,1024]{1,0:T(8,128)(2,1)}) custom-call(bf16[8,128,1280]{2,1,0:T(8,128)(2,1)S(1)} %all-to-all-done.1.refs_0_), custom_call_target="tpu_custom_call" | custom-call | tf_op jit(solution)/shard_map/pallas_call | solution.py:42
  (9 shorter events, 0.1 us)
Async XLA Ops:
  0.6 1.2 %copy-start.1 = (bf16[128,4096]{1,0:T(8,128)(2,1)S(1)}, bf16[128,4096]{1,0:T(8,128)(2,1)}, u32[]{:S(2)}) copy-start(bf16[128,4096]{1,0:T(8,128)(2,1)} %refs_2_.1) | copy-start | bytes 3145732
  1.9 1.2 %copy-start.2 = (bf16[128,4096]{1,0:T(8,128)(2,1)S(1)}, bf16[128,4096]{1,0:T(8,128)(2,1)}, u32[]{:S(2)}) copy-start(bf16[128,4096]{1,0:T(8,128)(2,1)} %refs_3_.1) | copy-start | bytes 3145732
  3.1 0.9 copy-start.3
  4.0 0.9 copy-start.4
  7.3 7.2 %copy-start.7 = (s32[16,8]{0,1:T(8,128)S(1)}, s32[16,8]{0,1:T(8,128)}, u32[]{:S(2)}) copy-start(s32[16,8]{0,1:T(8,128)} %param.13) | copy-start | bytes 1540
  7.3 41.3 %copy-start.5 = (f32[128]{0:T(128)S(1)}, f32[128]{0:T(128)}, u32[]{:S(2)}) copy-start(f32[128]{0:T(128)} %param.11) | copy-start | bytes 1540
  7.3 41.3 %copy-start.6 = (f32[128]{0:T(128)S(1)}, f32[128]{0:T(128)}, u32[]{:S(2)}) copy-start(f32[128]{0:T(128)} %param.12) | copy-start | bytes 1540
  7.3 41.3 %all-to-all-start = ((bf16[8,128,1280]{2,1,0:T(8,128)(2,1)}), bf16[8,128,1280]{2,1,0:T(8,128)(2,1)S(1)}, u32[]{:S(2)}, u32[]{:S(2)}) async-start(bf16[8,128,1280]{2,1,0:T(8,128)(2,1)} %shard_map.118), calls=%async_computation | async-start | bytes 5242880 | tf_op jit(solution)/shard_map/all_to_all | solution.py:270
  62.4 1.5 %copy-start = (bf16[1024,1280]{1,0:T(8,128)(2,1)}, bf16[1024,1280]{1,0:T(8,128)(2,1)S(1)}, u32[]{:S(2)}) copy-start(bf16[1024,1280]{1,0:T(8,128)(2,1)S(1)} %get-tuple-element.12) | copy-start | bytes 7864324
  63.9 47.6 %all-to-all-start.1 = ((bf16[8,128,1280]{2,1,0:T(8,128)(2,1)}), bf16[8,128,1280]{2,1,0:T(8,128)(2,1)S(1)}, u32[]{:S(2)}, u32[]{:S(2)}) async-start(bf16[8,128,1280]{2,1,0:T(8,128)(2,1)} %bitcast.10), calls=%async_computation.1 | async-start | bytes 5242880 | tf_op jit(solution)/shard_map/all_to_all | solution.py:279
  67.5 1.2 %collective-permute-start = (f32[2,128]{1,0:T(2,128)S(1)}, f32[2,128]{1,0:T(2,128)S(1)}, u32[]{:S(2)}, u32[]{:S(2)}) collective-permute-start(f32[2,128]{1,0:T(2,128)S(1)} %pad_maximum_fusion), channel_id=1, source_target_pairs={{0,8},{8,0},{16,24},{24,16},{32,40},{40,32},{48,56},{56,48},{64,72... | collective-permute-start | bytes 3080 | tf_op jit(solution)/shard_map/ppermute | solution.py:256
  68.8 3.6 %collective-permute-start.1 = (f32[2,128]{1,0:T(2,128)S(1)}, f32[2,128]{1,0:T(2,128)S(1)}, u32[]{:S(2)}, u32[]{:S(2)}) collective-permute-start(f32[2,128]{1,0:T(2,128)S(1)} %fusion), channel_id=1, source_target_pairs={{0,32},{8,40},{16,48},{24,56},{32,0},{40,8},{48,16},{56,24},{64,96... | collective-permute-start | bytes 3080 | tf_op jit(solution)/shard_map/ppermute | solution.py:256
  72.4 5.4 %collective-permute-start.2 = (f32[2,128]{1,0:T(2,128)S(1)}, f32[2,128]{1,0:T(2,128)S(1)}, u32[]{:S(2)}, u32[]{:S(2)}) collective-permute-start(f32[2,128]{1,0:T(2,128)S(1)} %fusion.1), channel_id=1, source_target_pairs={{0,64},{8,72},{16,80},{24,88},{32,96},{40,104},{48,112},{56,120},{... | collective-permute-start | bytes 3080 | tf_op jit(solution)/shard_map/ppermute | solution.py:256
  77.9 18.4 %collective-permute-start.3 = (f32[2,128]{1,0:T(2,128)S(1)}, f32[2,128]{1,0:T(2,128)S(1)}, u32[]{:S(2)}, u32[]{:S(2)}) collective-permute-start(f32[2,128]{1,0:T(2,128)S(1)} %add.23), channel_id=1, source_target_pairs={{0,16},{8,24},{16,0},{24,8},{32,48},{40,56},{48,32},{56,40},{64,80... | collective-permute-start | bytes 3080 | tf_op jit(solution)/shard_map/ppermute | solution.py:256
  96.2 6.0 %collective-permute-start.4 = (f32[2,128]{1,0:T(2,128)S(1)}, f32[2,128]{1,0:T(2,128)S(1)}, u32[]{:S(2)}, u32[]{:S(2)}) collective-permute-start(f32[2,128]{1,0:T(2,128)S(1)} %add.24), channel_id=1, source_target_pairs={{0,1},{1,0},{2,3},{3,2},{4,5},{5,4},{6,7},{7,6},{8,9},{9,8},{10,11... | collective-permute-start | bytes 3080 | tf_op jit(solution)/shard_map/ppermute | solution.py:256
  102.3 3.6 %collective-permute-start.5 = (f32[2,128]{1,0:T(2,128)S(1)}, f32[2,128]{1,0:T(2,128)S(1)}, u32[]{:S(2)}, u32[]{:S(2)}) collective-permute-start(f32[2,128]{1,0:T(2,128)S(1)} %add.25), channel_id=1, source_target_pairs={{0,2},{1,3},{2,0},{3,1},{4,6},{5,7},{6,4},{7,5},{8,10},{9,11},{10,... | collective-permute-start | bytes 3080 | tf_op jit(solution)/shard_map/ppermute | solution.py:256
  105.9 5.1 %collective-permute-start.6 = (f32[2,128]{1,0:T(2,128)S(1)}, f32[2,128]{1,0:T(2,128)S(1)}, u32[]{:S(2)}, u32[]{:S(2)}) collective-permute-start(f32[2,128]{1,0:T(2,128)S(1)} %add.26), channel_id=1, source_target_pairs={{0,4},{1,5},{2,6},{3,7},{4,0},{5,1},{6,2},{7,3},{8,12},{9,13},{10,... | collective-permute-start | bytes 3080 | tf_op jit(solution)/shard_map/ppermute | solution.py:256
where the time goes:
time: 114 us; the launch traced here: 113 us
  waiting for transfers between devices  63.1 us (55%)
  starting transfers between devices  25 us (22%)
  Pallas kernels  17.8 us (16%)
  local copies, waits for them, and re-layouts  5.92 us (5%)
    all_to_all x1, waiting for transfers between devices, on_device(): lax.all_to_all(packed, 'head', split_axis=0, concat_axis=0, tiled=True)  34 us
    ppermute x7, waiting for transfers between devices, sum_everywhere(): x = x + lax.ppermute(x, axis, [(i, i ^ 1 << bit) for i in range(size)])  29.1 us
    ppermute x7, starting transfers between devices, sum_everywhere(): x = x + lax.ppermute(x, axis, [(i, i ^ 1 << bit) for i in range(size)])  14.2 us
    pallas_call x1, Pallas kernels, run_attend(): pl.pallas_call(functools.partial(attend_kernel, count, first, last), out_...  13.8 us
    all_to_all x1, starting transfers between devices, on_device(): lax.all_to_all(packed, 'head', split_axis=0, concat_axis=0, tiled=True)  7.16 us
    unnamed x17, local copies, waits for them, and re-layouts  5.92 us
    pallas_call x2, Pallas kernels, run_copies(): pl.pallas_call(functools.partial(copies_kernel, plan, len(arrays)), out_s...  4.02 us
    all_to_all x1, starting transfers between devices, on_device(): lax.all_to_all(y.reshape(members, rows, y.shape[1]), 'head', split_axis=0...  3.63 us
  transfers between devices with their start and end apart: 9, of which 8 were waited for; matrix products, arithmetic and copies ran while one was open for 1% of the time, Pallas kernels for 0%

commit v1 on v0

v1 whole, which is shorter than its diff:
```python
import functools
import math

import jax
import jax.numpy as jnp
from jax import lax
from jax.experimental import pallas as pl
from jax.experimental.pallas import tpu as pltpu
from jax.sharding import PartitionSpec as P

H = 32
KVH = 8
HD = 128
GROUP = H // KVH
MOST_DOC = 512
BLK = 128
WINDOWS = MOST_DOC // BLK + 1
YS = 4
PARTS = KVH // YS
WIDTH = GROUP * HD
TAIL = 16
EPS = 1e-06
FACTOR = HD ** (-0.5)
EXP2_FACTOR = FACTOR * math.log2(math.e)
F32 = jnp.float32
BF16 = jnp.bfloat16
HBM = pltpu.HBM
VMEM = pltpu.VMEM
PACK_LIMIT = pltpu.CompilerParams(vmem_limit_bytes=60 * 1024 * 1024)
LIMIT = pltpu.CompilerParams(vmem_limit_bytes=20 * 1024 * 1024)


def dot(left, right, contract):
    return lax.dot_general(left, right, ((contract[:1], contract[1:]), ((), ())), preferred_element_type=F32)


def specs(spaces):
    return [pl.BlockSpec(memory_space=space) for space in spaces]


def shape(rows, columns, kind=BF16):
    return jax.ShapeDtypeStruct((rows, columns), kind)


def my_y():
    return lax.axis_index("head") // 2


def ahead(step):
    return lax.rem(my_y() + step, YS)


def behind(step):
    return lax.rem(my_y() + (YS - step), YS)


def block_rows(index):
    return pl.ds(pl.multiple_of(index * BLK, BLK), BLK)


def do_copies(moves, sems):
    started = [pltpu.make_async_copy(a, b, sems.at[i]) for i, (a, b) in enumerate(moves)]
    for move in started:
        move.start()
    for move in started:
        move.wait()


def pack_kv_kernel(k_ref, v_ref, *refs):
    kv, sems = refs[:YS], refs[YS]
    wide = PARTS * HD
    moves = []
    for step in range(YS):
        at = pl.ds(pl.multiple_of(ahead(step) * wide, wide), wide)
        moves.append((k_ref.at[:, at], kv[step].at[:, pl.ds(0, wide)]))
        moves.append((v_ref.at[:, at], kv[step].at[:, pl.ds(wide, wide)]))
    do_copies(moves, sems)


def pack_qg_kernel(q_ref, g_ref, _, *refs):
    soon, qg, sems = refs[0], refs[1 : 1 + YS], refs[1 + YS]
    moves = []
    for y in range(YS):
        at = pl.ds(y * (PARTS * WIDTH), WIDTH)
        moves.append((q_ref.at[:, at], soon.at[y, :, pl.ds(0, WIDTH)]))
        moves.append((g_ref.at[:, at], soon.at[y, :, pl.ds(WIDTH, WIDTH)]))
    for step in range(YS):
        at = pl.ds(pl.multiple_of(ahead(step) * (PARTS * WIDTH) + WIDTH, WIDTH), WIDTH)
        moves.append((q_ref.at[:, at], qg[step].at[:, pl.ds(0, WIDTH)]))
        moves.append((g_ref.at[:, at], qg[step].at[:, pl.ds(WIDTH, WIDTH)]))
    do_copies(moves, sems)


def after_kernel(*refs):
    pass


def after(x, first):
    return pl.pallas_call(
        after_kernel,
        out_shape=jax.ShapeDtypeStruct(x.shape, x.dtype),
        in_specs=specs([pl.ANY] * 2),
        out_specs=specs([pl.ANY])[0],
        input_output_aliases={0: 0},
    )(x, first)


def gather_kv_kernel(q_gain_ref, k_gain_ref, *refs):
    out, gains_ref = refs[YS:]
    gains_ref[0:1, :] = q_gain_ref[...]
    gains_ref[1:2, :] = k_gain_ref[...]
    for step in range(YS):
        out[block_rows(behind(step)), :] = refs[step][...]


def unit_of(raw):
    values = raw.astype(F32)
    inverse = lax.rsqrt(jnp.mean(values * values, axis=-1, keepdims=True) + EPS)
    return values * inverse, inverse


def norm_back(grad, unit, inverse, gain):
    scaled = grad * gain
    return inverse * (scaled - unit * jnp.mean(scaled * unit, axis=-1, keepdims=True))


def fold(x):
    return jnp.sum(x.reshape(x.shape[0] // 8, 8, x.shape[1]), axis=0)


def attend_kernel(part, *refs):
    refs = list(refs)
    lengths_ref, both_gains_ref, own_ref, far_ref = refs[:4]
    del refs[:4]
    if part == 0:
        qg_ref, y_ref, far_out, own_out, gains_ref = refs[:5]
        del refs[:5]
    else:
        pieces = refs[:YS]
        y_before, far_before, own_before, gains_before = refs[YS : YS + 4]
        del refs[: YS + 4]
        outs = refs[:YS]
        far_out, own_out, gains_ref = refs[YS : YS + 3]
        del refs[: YS + 3]
        qg_ref = refs.pop()
        y_ref = refs.pop()
    kn_ref, v_ref, dk_ref, dv_ref, qn_ref, g_ref, out_ref, dq_ref, bias_ref = refs
    replica = lax.axis_index("dp")
    column = lax.rem(lax.axis_index("head"), 2)
    q_gain = both_gains_ref[0:1, :]
    k_gain = both_gains_ref[1:2, :]
    k_at = slice(part * HD, (part + 1) * HD)
    v_at = slice((PARTS + part) * HD, (PARTS + part + 1) * HD)
    for j in range(YS):
        local = slice(j * BLK, (j + 1) * BLK)
        for ref, col in ((own_ref, column), (far_ref, 1 - column)):
            place = block_rows(2 * j + col)
            unit, _ = unit_of(ref[local, k_at])
            kn_ref[place, :] = (unit * k_gain).astype(BF16)
            v_ref[place, :] = ref[local, v_at]
    if part > 0:
        for step in range(YS):
            qg_ref[block_rows(behind(step)), :] = pieces[step][...]
    dk_ref[...] = jnp.zeros_like(dk_ref)
    dv_ref[...] = jnp.zeros_like(dv_ref)
    ends = []
    total = jnp.int32(0)
    for d in range(lengths_ref.shape[1]):
        total = total + lengths_ref[replica, d]
        ends.append(total)

    def block(j, q_sum):
        here = block_rows(j)
        i = 2 * j + column
        row0 = i * BLK
        places = row0 + lax.broadcasted_iota(jnp.int32, (BLK, BLK), 0)
        begins = jnp.zeros((BLK, BLK), jnp.int32)
        begin0 = jnp.int32(0)
        for end in ends:
            begins = jnp.where(end <= places, end, begins)
            begin0 = jnp.where(end <= row0, end, begin0)
        first_block = begin0 // BLK
        needed = i - first_block + 1
        units = []
        for h in range(GROUP):
            unit, inverse = unit_of(qg_ref[here, h * HD : (h + 1) * HD])
            units.append((unit, inverse))
            qn_ref[h * BLK : (h + 1) * BLK, :] = (unit * q_gain).astype(BF16)
            g_ref[h * BLK : (h + 1) * BLK, :] = qg_ref[here, WIDTH + h * HD : WIDTH + (h + 1) * HD]
        for blocks in range(1, WINDOWS + 1):

            @pl.when(needed == blocks)
            def _():
                keys = blocks * BLK
                k0 = pl.multiple_of(first_block * BLK, BLK)
                window = pl.ds(k0, keys)
                lane = k0 + lax.broadcasted_iota(jnp.int32, (BLK, BLK), 1)
                for t in range(blocks):
                    place = lane + t * BLK
                    seen = place >= begins
                    if t == blocks - 1:
                        seen = seen & (place <= places)
                    bias_ref[:, t * BLK : (t + 1) * BLK] = jnp.where(seen, 0.0, -1e30)
                qn = qn_ref[...]
                g = g_ref[...]
                kn = kn_ref[window, :]
                v = v_ref[window, :]
                bias = bias_ref[:, :keys]
                scores = dot(qn, kn, (1, 1)).reshape(GROUP, BLK, keys) + bias[None]
                scores = scores.reshape(GROUP * BLK, keys)
                peak = jnp.max(scores, axis=1, keepdims=True)
                raised = jnp.exp2((scores - peak) * EXP2_FACTOR)
                weights = raised * (1.0 / jnp.sum(raised, axis=1, keepdims=True))
                rounded = weights.astype(BF16)
                out = dot(rounded, v, (1, 0))
                out_ref[...] = out
                dv_ref[window, :] += dot(rounded, g, (0, 0))
                dweights = dot(g, v, (1, 1))
                delta = jnp.sum(g.astype(F32) * out, axis=1, keepdims=True)
                dscores = (weights * (dweights - delta) * FACTOR).astype(BF16)
                dq_ref[...] = dot(dscores, kn, (1, 0))
                dk_ref[window, :] += dot(dscores, qn, (0, 0))

        for h in range(GROUP):
            unit, inverse = units[h]
            local = slice(h * BLK, (h + 1) * BLK)
            y_ref[here, h * HD : (h + 1) * HD] = out_ref[local, :].astype(BF16)
            dq = dq_ref[local, :]
            back = norm_back(dq, unit, inverse, q_gain)
            y_ref[here, WIDTH + h * HD : WIDTH + (h + 1) * HD] = back.astype(BF16)
            q_sum = q_sum + fold(dq * unit)
        return q_sum

    q_sum = lax.fori_loop(0, YS, block, jnp.zeros((8, HD), F32))
    k_sum = jnp.zeros((8, HD), F32)
    for j in range(YS):
        local = slice(j * BLK, (j + 1) * BLK)
        for ref, col in ((own_ref, column), (far_ref, 1 - column)):
            place = block_rows(2 * j + col)
            unit, _ = unit_of(ref[local, k_at])
            dk = dk_ref[place, :]
            dv = dv_ref[place, :]
            k_sum = k_sum + fold(dk * unit)
            target = own_out if ref is own_ref else far_out
            target[local, k_at] = dk.astype(target.dtype)
            target[local, v_at] = dv.astype(target.dtype)
    if part > 0:
        for before, target in ((far_before, far_out), (own_before, own_out)):
            for p in range(part):
                for at in (p, PARTS + p):
                    target[:, at * HD : (at + 1) * HD] = before[:, at * HD : (at + 1) * HD]
    sums = jnp.concatenate(
        [jnp.sum(q_sum, axis=0, keepdims=True), jnp.sum(k_sum, axis=0, keepdims=True)], axis=0
    )
    if part == 0:
        gains_ref[...] = sums
    else:
        gains_ref[...] = jnp.broadcast_to((gains_before[...] + sums)[None], gains_ref.shape)
        for step in range(YS):
            rows = block_rows(ahead(step))
            for p, ref in enumerate((y_before, y_ref)):
                outs[step][:, p * WIDTH : (p + 1) * WIDTH] = ref[rows, :WIDTH]
                outs[step][:, (PARTS + p) * WIDTH : (PARTS + p + 1) * WIDTH] = ref[rows, WIDTH:]


def attend(part, lengths, both_gains, own, far, pieces, before, others):
    span = 2 * YS * BLK
    args = [lengths, both_gains, own, far, *pieces, *before]
    half = own.shape[0]
    sums = [shape(half, 2 * PARTS * HD), shape(half, 2 * PARTS * HD, F32)]
    if part == 0:
        out_shape = [shape(half, 2 * WIDTH), *sums, shape(2, HD, F32)]
    else:
        out_shape = [shape(BLK, 2 * PARTS * WIDTH)] * YS + sums
        out_shape += [jax.ShapeDtypeStruct((others, 2, HD), F32)]
    scratch = [
        pltpu.VMEM((span, HD), BF16),
        pltpu.VMEM((span, HD), BF16),
        pltpu.VMEM((span, HD), F32),
        pltpu.VMEM((span, HD), F32),
        pltpu.VMEM((WIDTH, HD), BF16),
        pltpu.VMEM((WIDTH, HD), BF16),
        pltpu.VMEM((WIDTH, HD), F32),
        pltpu.VMEM((WIDTH, HD), F32),
        pltpu.VMEM((BLK, WINDOWS * BLK), F32),
    ]
    if part > 0:
        scratch += [pltpu.VMEM((half, 2 * WIDTH), BF16)] * 2
    return pl.pallas_call(
        functools.partial(attend_kernel, part),
        out_shape=out_shape,
        in_specs=specs([pltpu.SMEM] + [VMEM] * (len(args) - 1)),
        out_specs=specs([VMEM] * len(out_shape)),
        scratch_shapes=scratch,
        compiler_params=LIMIT,
        cost_estimate=pl.CostEstimate(
            flops=10 * 2 * GROUP * half * 384 * HD, bytes_accessed=4 << 20, transcendentals=GROUP * half * 384
        ),
    )(*args)


def finish_kv_kernel(both_gains_ref, kv_ref, own_ref, far_ref, gains_ref, *refs):
    outs = refs[:YS]
    y_ref = refs[YS]
    k_gain = both_gains_ref[1:2, :]
    for p in range(PARTS):
        k_at = slice(p * HD, (p + 1) * HD)
        v_at = slice((PARTS + p) * HD, (PARTS + p + 1) * HD)
        unit, inverse = unit_of(kv_ref[:, k_at])
        dk = own_ref[:, k_at] + far_ref[:, k_at].astype(F32)
        y_ref[:, k_at] = norm_back(dk, unit, inverse, k_gain).astype(BF16)
        y_ref[:, v_at] = (own_ref[:, v_at] + far_ref[:, v_at].astype(F32)).astype(BF16)
    rest = jnp.concatenate([jnp.sum(gains_ref[...], axis=0), jnp.zeros((TAIL - 2, HD), F32)], axis=0)
    for step in range(YS):
        outs[step][:BLK, :] = y_ref[block_rows(ahead(step)), :]
        outs[step][BLK:, 3 * HD :] = jnp.zeros((TAIL, HD), BF16)
    for n in range(3):
        term = rest.astype(BF16)
        rest = rest - term.astype(F32)
        for step in range(YS):
            outs[step][BLK:, n * HD : (n + 1) * HD] = term


def unpack_moves(half, pieces, results):
    moves = []
    for step in range(YS):
        for n, result in enumerate(results):
            at = pl.ds(pl.multiple_of(behind(step) * half, half), half)
            moves.append((pieces[step].at[pl.ds(0, BLK), pl.ds(n * half, half)], result.at[:, at]))
    return moves


def unpack_qg_kernel(*refs):
    do_copies(unpack_moves(PARTS * WIDTH, refs[:YS], refs[YS:-1]), refs[-1])


def unpack_kv_kernel(scales, *refs):
    pieces = refs[:YS]
    dk_ref, dv_ref, q_ref, k_ref, sums_ref, sems = refs[YS:]
    for step in range(YS):
        tail = pieces[step][BLK:, :].astype(F32)
        whole = (tail[:, :HD] + tail[:, HD : 2 * HD]) + tail[:, 2 * HD : 3 * HD]
        sums_ref[pl.ds(behind(step), 1)] = whole[None]
    total = (sums_ref[0] + sums_ref[1]) + (sums_ref[2] + sums_ref[3])
    q_ref[...] = total[0:1] * scales[0]
    k_ref[...] = total[1:2] * scales[1]
    do_copies(unpack_moves(PARTS * HD, pieces, (dk_ref, dv_ref)), sems)


def over_y(pieces):
    moved = [pieces[0]]
    for step in range(1, YS):
        moved.append(
            lax.ppermute(
                pieces[step],
                "head",
                [(2 * y + c, 2 * ((y + step) % YS) + c) for y in range(YS) for c in range(2)],
            )
        )
    return moved


def over_x(x):
    return lax.ppermute(x, "head", [(i, i ^ 1) for i in range(2 * YS)])


def on_device(query, key_states, value_states, grad_attended, query_gain, key_gain, doc_lengths):
    replicas = lax.axis_size("dp")
    members = lax.axis_size("head")
    rows = query.shape[0]
    half = YS * rows
    wide = 2 * PARTS * HD

    pieces = pl.pallas_call(
        pack_kv_kernel,
        out_shape=[shape(rows, wide)] * YS,
        in_specs=specs([HBM] * 2),
        out_specs=specs([VMEM] * YS),
        scratch_shapes=[pltpu.SemaphoreType.DMA((2 * YS,))],
        compiler_params=PACK_LIMIT,
    )(key_states, value_states)
    kv_moved = over_y(pieces)
    soon, *pieces = pl.pallas_call(
        pack_qg_kernel,
        out_shape=[jax.ShapeDtypeStruct((YS, rows, 2 * WIDTH), BF16)] + [shape(rows, 2 * WIDTH)] * YS,
        in_specs=specs([HBM] * 2 + [VMEM]),
        out_specs=specs([VMEM] * (1 + YS)),
        scratch_shapes=[pltpu.SemaphoreType.DMA((4 * YS,))],
        compiler_params=LIMIT,
    )(query, grad_attended, kv_moved[1])
    qg_moved = over_y(pieces)
    own, both_gains = pl.pallas_call(
        gather_kv_kernel,
        out_shape=[shape(half, wide), shape(2, HD, F32)],
        in_specs=specs([VMEM] * (2 + YS)),
        out_specs=specs([VMEM] * 2),
        compiler_params=LIMIT,
    )(query_gain.reshape(1, HD), key_gain.reshape(1, HD), *kv_moved)
    far = over_x(own)
    groups = [[2 * y + c for y in range(YS)] for c in range(2)]
    soon = after(soon, both_gains)
    soon = lax.all_to_all(soon, "head", split_axis=0, concat_axis=0, tiled=True, axis_index_groups=groups)
    qg_parts = [[soon.reshape(half, 2 * WIDTH)], qg_moved]

    before = ()
    for part in range(PARTS):
        before = attend(
            part, doc_lengths, both_gains, own, far, qg_parts[part], before, 2 * replicas
        )
    *outs, far_sum, own_sum, gains = before
    far_back = over_x(far_sum)
    outs = over_y(outs)
    same_y = [[d * members + 2 * y + c for d in range(replicas) for c in range(2)] for y in range(YS)]
    gains = lax.all_to_all(
        gains, ("dp", "head"), split_axis=0, concat_axis=0, tiled=True, axis_index_groups=same_y
    )
    kv_back = pl.pallas_call(
        finish_kv_kernel,
        out_shape=[shape(rows + TAIL, wide)] * YS,
        in_specs=specs([VMEM] * 5),
        out_specs=specs([VMEM] * YS),
        scratch_shapes=[pltpu.VMEM((half, wide), BF16)],
        compiler_params=LIMIT,
    )(both_gains, own, own_sum, far_back, gains)
    kv_back = over_y(kv_back)
    out, dq = pl.pallas_call(
        unpack_qg_kernel,
        out_shape=[shape(rows, H * HD)] * 2,
        in_specs=specs([VMEM] * YS),
        out_specs=specs([HBM] * 2),
        scratch_shapes=[pltpu.SemaphoreType.DMA((2 * YS,))],
        compiler_params=LIMIT,
    )(*outs)
    all_tokens = rows * replicas * members
    scales = ((all_tokens * H) ** (-0.5), (all_tokens * KVH) ** (-0.5))
    dk, dv, q_total, k_total = pl.pallas_call(
        functools.partial(unpack_kv_kernel, scales),
        out_shape=[shape(rows, KVH * HD)] * 2 + [shape(1, HD, F32)] * 2,
        in_specs=specs([VMEM] * YS),
        out_specs=specs([HBM] * 2 + [VMEM] * 2),
        scratch_shapes=[pltpu.VMEM((YS, TAIL, HD), F32), pltpu.SemaphoreType.DMA((2 * YS,))],
        compiler_params=LIMIT,
    )(*kv_back)
    return out, dq, dk, dv, q_total.reshape(HD), k_total.reshape(HD)


def solution(mesh):
    rows = P(("dp", "head"), None)
    in_specs = (rows, rows, rows, rows, P(), P(), P())
    out_specs = (rows, rows, rows, rows, P(), P())
    return jax.shard_map(
        on_device, mesh=mesh, in_specs=in_specs, out_specs=out_specs, check_vma=False
    )
```

time: 114 us -> 88 us (0.77)
  waiting for transfers between devices: 63.1 us -> 13.6 us
  blocking collectives: 0 us -> 14.6 us
  starting transfers between devices: 25 us -> 34.1 us
  Pallas kernels: 17.8 us -> 19.9 us
  local copies, waits for them, and re-layouts: 5.92 us -> 4.72 us
    all_to_all x2 -> x1, waiting for transfers between devices: 34 us -> 4.59 us  [on_device(): lax.all_to_all(soon, 'head', split_axis=0, concat_axis=0, tiled=True, axi...]
    ppermute x7 -> x14, waiting for transfers between devices: 29.1 us -> 8.98 us  [the longest x12 6.17 us: over_y(): lax.ppermute(pieces[step], 'head', [(2 * y + c, 2 * ((y + step) % YS) + c...]
    all_to_all x0 -> x1, blocking collectives: none -> 14.6 us  [on_device(): lax.all_to_all(gains, ('dp', 'head'), split_axis=0, concat_axis=0, tiled=...]
    ppermute x7 -> x14, starting transfers between devices: 14.2 us -> 28.2 us  [the longest x12 20.8 us: over_y(): lax.ppermute(pieces[step], 'head', [(2 * y + c, 2 * ((y + step) % YS) + c...]
    all_to_all x2 -> x1, starting transfers between devices: 10.8 us -> 5.93 us  [on_device(): lax.all_to_all(soon, 'head', split_axis=0, concat_axis=0, tiled=True, axi...]
    pallas_call x3 -> x9, Pallas kernels: 17.8 us -> 19.9 us  [the longest x2 14.2 us: attend(): pl.pallas_call(functools.partial(attend_kernel, part), out_shape=out_shap...]
    unnamed x17 -> x19, local copies, waits for them, and re-layouts: 5.92 us -> 4.72 us
  transfers between devices with their start and end apart: 9 -> 15, of which waited for: 8 -> 7; matrix products, arithmetic and copies ran while one was open for 1% -> 0% of each run, Pallas kernels for 0% -> 10%
where the time goes in v1:
time: 88 us; the launch traced here: 87.8 us
  starting transfers between devices  34.1 us (39%)
  Pallas kernels  19.9 us (23%)
  blocking collectives  14.6 us (17%)
  waiting for transfers between devices  13.6 us (15%)
  local copies, waits for them, and re-layouts  4.72 us (5%)
  between operations  0.92 us (1%)
    ppermute x12, starting transfers between devices, over_y(): lax.ppermute(pieces[step], 'head', [(2 * y + c, 2 * ((y + step) % YS) + c...  20.8 us
    all_to_all x1, blocking collectives, on_device(): lax.all_to_all(gains, ('dp', 'head'), split_axis=0, concat_axis=0, tiled=...  14.6 us
    pallas_call x2, Pallas kernels, attend(): pl.pallas_call(functools.partial(attend_kernel, part), out_shape=out_shap...  14.2 us
    ppermute x2, starting transfers between devices, over_x(): return lax.ppermute(x, 'head', [(i, i ^ 1) for i in range(2 * YS)])  7.34 us
    ppermute x12, waiting for transfers between devices, over_y(): lax.ppermute(pieces[step], 'head', [(2 * y + c, 2 * ((y + step) % YS) + c...  6.17 us
    all_to_all x1, starting transfers between devices, on_device(): lax.all_to_all(soon, 'head', split_axis=0, concat_axis=0, tiled=True, axi...  5.93 us
    unnamed x19, local copies, waits for them, and re-layouts  4.72 us
    all_to_all x1, waiting for transfers between devices, on_device(): lax.all_to_all(soon, 'head', split_axis=0, concat_axis=0, tiled=True, axi...  4.59 us
  transfers between devices with their start and end apart: 15, of which 7 were waited for; matrix products, arithmetic and copies ran while one was open for 0% of the time, Pallas kernels for 10%

profile of v1, /device:TPU:0, one launch (start us, length us, event | category | flops | bytes accessed | tf_op | source)
XLA Modules:
  0.0 87.8 jit_solution(6524041647835030660)
XLA Ops:
  0.6 1.9 %shard_map.118 = (bf16[128,512]{1,0:T(8,128)(2,1)}, bf16[128,512]{1,0:T(8,128)(2,1)}, bf16[128,512]{1,0:T(8,128)(2,1)}, bf16[128,512]{1,0:T(8,128)(2,1)}) custom-call(bf16[128,1024]{1,0:T(8,128)(2,1)} %k_ref.1, bf16[128,1024]{1,0:T(8,128)(2,1)} %v_ref.1), custom_call_target="tpu_custom_call" | custom-call | tf_op jit(solution)/shard_map/pallas_call | solution.py:374
  2.6 1.7 %collective-permute-start = (bf16[128,512]{1,0:T(8,128)(2,1)}, bf16[128,512]{1,0:T(8,128)(2,1)S(1)}, u32[]{:S(2)}, u32[]{:S(2)}) collective-permute-start(bf16[128,512]{1,0:T(8,128)(2,1)} %get-tuple-element.39), channel_id=1, source_target_pairs={{0,2},{1,3},{2,4},{3,5},{4,6},{5,7},{6,0},{7,1},{8,10},{9,11},{10,... | collective-permute-start | bytes 393224 | tf_op jit(solution)/shard_map/ppermute | solution.py:354
  4.3 2.9 %collective-permute-start.1 = (bf16[128,512]{1,0:T(8,128)(2,1)}, bf16[128,512]{1,0:T(8,128)(2,1)S(1)}, u32[]{:S(2)}, u32[]{:S(2)}) collective-permute-start(bf16[128,512]{1,0:T(8,128)(2,1)} %get-tuple-element.40), channel_id=1, source_target_pairs={{0,4},{1,5},{2,6},{3,7},{4,0},{5,1},{6,2},{7,3},{8,12},{9,13},{10,... | collective-permute-start | bytes 393224 | tf_op jit(solution)/shard_map/ppermute | solution.py:354
  7.2 1.3 %collective-permute-start.2 = (bf16[128,512]{1,0:T(8,128)(2,1)}, bf16[128,512]{1,0:T(8,128)(2,1)S(1)}, u32[]{:S(2)}, u32[]{:S(2)}) collective-permute-start(bf16[128,512]{1,0:T(8,128)(2,1)} %get-tuple-element.41), channel_id=1, source_target_pairs={{0,6},{1,7},{2,0},{3,1},{4,2},{5,3},{6,4},{7,5},{8,14},{9,15},{10,... | collective-permute-start | bytes 393224 | tf_op jit(solution)/shard_map/ppermute | solution.py:354
  8.6 0.9 %collective-permute-done.refs_1_._ = bf16[128,512]{1,0:T(8,128)(2,1)S(1)} collective-permute-done((bf16[128,512]{1,0:T(8,128)(2,1)}, bf16[128,512]{1,0:T(8,128)(2,1)S(1)}, u32[]{:S(2)}, u32[]{:S(2)}) %collective-permute-start) | collective-permute-done | bytes 131104 | tf_op jit(solution)/shard_map/ppermute | solution.py:354
  9.5 1.2 %copy-done.1 = bf16[128,4096]{1,0:T(8,128)(2,1)S(1)} copy-done((bf16[128,4096]{1,0:T(8,128)(2,1)S(1)}, bf16[128,4096]{1,0:T(8,128)(2,1)}, u32[]{:S(2)}) %copy-start.1) | copy-done | bytes 1048600
  10.7 1.2 %copy-done.2 = bf16[128,4096]{1,0:T(8,128)(2,1)S(1)} copy-done((bf16[128,4096]{1,0:T(8,128)(2,1)S(1)}, bf16[128,4096]{1,0:T(8,128)(2,1)}, u32[]{:S(2)}) %copy-start.2) | copy-done | bytes 1048600
  11.9 0.5 shard_map.120
  12.4 0.0 copy-start
  12.4 1.0 %copy-done = bf16[4,128,1024]{2,1,0:T(8,128)(2,1)} copy-done((bf16[4,128,1024]{2,1,0:T(8,128)(2,1)}, bf16[4,128,1024]{2,1,0:T(8,128)(2,1)S(1)}, u32[]{:S(2)}) %copy-start) | copy-done | bytes 1048600
  13.4 0.1 collective-permute-done.1.refs_2_
  13.4 0.0 collective-permute-done.2.refs_3_
  13.4 0.0 copy-done.3
  13.5 0.6 copy-done.6
  14.1 0.0 copy-done.7
  14.2 0.0 copy-start.4
  14.2 0.6 copy-done.4
  14.7 5.9 %all-to-all-start = ((bf16[4,128,1024]{2,1,0:T(8,128)(2,1)}), bf16[4,128,1024]{2,1,0:T(8,128)(2,1)S(1)}, u32[]{:S(2)}, u32[]{:S(2)}) async-start(bf16[4,128,1024]{2,1,0:T(8,128)(2,1)} %shard_map.121), calls=%async_computation | async-start | bytes 2097152 | tf_op jit(solution)/shard_map/all_to_all | solution.py:402
  20.7 3.0 %collective-permute-start.3 = (bf16[512,512]{1,0:T(8,128)(2,1)S(1)}, bf16[512,512]{1,0:T(8,128)(2,1)S(1)}, u32[]{:S(2)}, u32[]{:S(2)}) collective-permute-start(bf16[512,512]{1,0:T(8,128)(2,1)S(1)} %get-tuple-element.43.refs_2_.kv_ref), channel_id=1, source_target_pairs={{0,1},{1,0},{2,3},{3,2},{4,5},{5,4},{6,7},{7,6},{8,9},{9,8},{10,11... | collective-permute-start | bytes 1572872 | tf_op jit(solution)/shard_map/ppermute | solution.py:364
  23.7 2.0 %collective-permute-start.4 = (bf16[128,1024]{1,0:T(8,128)(2,1)S(1)}, bf16[128,1024]{1,0:T(8,128)(2,1)S(1)}, u32[]{:S(2)}, u32[]{:S(2)}) collective-permute-start(bf16[128,1024]{1,0:T(8,128)(2,1)S(1)} %get-tuple-element.45), channel_id=1, source_target_pairs={{0,2},{1,3},{2,4},{3,5},{4,6},{5,7},{6,0},{7,1},{8,10},{9,11},{10,... | collective-permute-start | bytes 786440 | tf_op jit(solution)/shard_map/ppermute | solution.py:354
  25.7 2.7 %collective-permute-start.5 = (bf16[128,1024]{1,0:T(8,128)(2,1)S(1)}, bf16[128,1024]{1,0:T(8,128)(2,1)}, u32[]{:S(2)}, u32[]{:S(2)}) collective-permute-start(bf16[128,1024]{1,0:T(8,128)(2,1)S(1)} %get-tuple-element.46), channel_id=1, source_target_pairs={{0,4},{1,5},{2,6},{3,7},{4,0},{5,1},{6,2},{7,3},{8,12},{9,13},{10,... | collective-permute-start | bytes 786440 | tf_op jit(solution)/shard_map/ppermute | solution.py:354
  28.4 1.5 %collective-permute-start.6 = (bf16[128,1024]{1,0:T(8,128)(2,1)S(1)}, bf16[128,1024]{1,0:T(8,128)(2,1)}, u32[]{:S(2)}, u32[]{:S(2)}) collective-permute-start(bf16[128,1024]{1,0:T(8,128)(2,1)S(1)} %get-tuple-element.47), channel_id=1, source_target_pairs={{0,6},{1,7},{2,0},{3,1},{4,2},{5,3},{6,4},{7,5},{8,14},{9,15},{10,... | collective-permute-start | bytes 786440 | tf_op jit(solution)/shard_map/ppermute | solution.py:354
  29.9 0.1 copy.15.refs_0_
  29.9 2.8 %collective-permute-done.3.refs_3_ = bf16[512,512]{1,0:T(8,128)(2,1)S(1)} collective-permute-done((bf16[512,512]{1,0:T(8,128)(2,1)S(1)}, bf16[512,512]{1,0:T(8,128)(2,1)S(1)}, u32[]{:S(2)}, u32[]{:S(2)}) %collective-permute-start.3) | collective-permute-done | bytes 524320 | tf_op jit(solution)/shard_map/ppermute | solution.py:364
  32.8 4.6 %all-to-all-done = bf16[4,128,1024]{2,1,0:T(8,128)(2,1)S(1)} async-done(((bf16[4,128,1024]{2,1,0:T(8,128)(2,1)}), bf16[4,128,1024]{2,1,0:T(8,128)(2,1)S(1)}, u32[]{:S(2)}, u32[]{:S(2)}) %all-to-all-start) | async-done | bytes 1048608 | tf_op jit(solution)/shard_map/all_to_all | solution.py:402
  37.3 6.7 %shard_map.122 = (bf16[512,1024]{1,0:T(8,128)(2,1)S(1)}, bf16[512,512]{1,0:T(8,128)(2,1)S(1)}, f32[512,512]{1,0:T(8,128)S(1)}, f32[2,128]{1,0:T(2,128)S(1)}) custom-call(s32[16,8]{1,0:T(8,128)S(1)} %copy.15.refs_0_, f32[2,128]{1,0:T(2,128)S(1)} %copy-done.5, bf16[512,512]{1,0:T(8,128)(2,1)S(1)} %get-tuple-element.43.refs_2_.kv_ref, ...), custom_call_target="tpu_custom_call" | custom-call | flops 2013265920 | bytes 4194304 | tf_op jit(solution)/shard_map/pallas_call | solution.py:289
  44.1 0.0 collective-permute-done.4.refs_5_
  44.1 0.2 collective-permute-done.5.refs_6_
  44.3 0.0 collective-permute-done.6.refs_7_
  44.3 7.4 %shard_map.123 = (bf16[128,2048]{1,0:T(8,128)(2,1)S(1)}, bf16[128,2048]{1,0:T(8,128)(2,1)S(1)}, bf16[128,2048]{1,0:T(8,128)(2,1)S(1)}, bf16[128,2048]{1,0:T(8,12...) custom-call(s32[16,8]{1,0:T(8,128)S(1)} %copy.15.refs_0_, ...), custom_call_target="tpu_custom_call" | custom-call | flops 2013265920 | bytes 4194304 | tf_op jit(solution)/shard_map/pallas_call | solution.py:289
  51.7 4.3 %collective-permute-start.10 = (bf16[512,512]{1,0:T(8,128)(2,1)S(1)}, bf16[512,512]{1,0:T(8,128)(2,1)S(1)}, u32[]{:S(2)}, u32[]{:S(2)}) collective-permute-start(bf16[512,512]{1,0:T(8,128)(2,1)S(1)} %get-tuple-element.60), channel_id=1, source_target_pairs={{0,1},{1,0},{2,3},{3,2},{4,5},{5,4},{6,7},{7,6},{8,9},{9,8},{10,11... | collective-permute-start | bytes 1572872 | tf_op jit(solution)/shard_map/ppermute | solution.py:364
  56.0 1.5 %collective-permute-start.7 = (bf16[128,2048]{1,0:T(8,128)(2,1)S(1)}, bf16[128,2048]{1,0:T(8,128)(2,1)S(1)}, u32[]{:S(2)}, u32[]{:S(2)}) collective-permute-start(bf16[128,2048]{1,0:T(8,128)(2,1)S(1)} %get-tuple-element.54), channel_id=1, source_target_pairs={{0,2},{1,3},{2,4},{3,5},{4,6},{5,7},{6,0},{7,1},{8,10},{9,11},{10,... | collective-permute-start | bytes 1572872 | tf_op jit(solution)/shard_map/ppermute | solution.py:354
  57.5 3.1 %collective-permute-start.8 = (bf16[128,2048]{1,0:T(8,128)(2,1)S(1)}, bf16[128,2048]{1,0:T(8,128)(2,1)S(1)}, u32[]{:S(2)}, u32[]{:S(2)}) collective-permute-start(bf16[128,2048]{1,0:T(8,128)(2,1)S(1)} %get-tuple-element.55), channel_id=1, source_target_pairs={{0,4},{1,5},{2,6},{3,7},{4,0},{5,1},{6,2},{7,3},{8,12},{9,13},{10,... | collective-permute-start | bytes 1572872 | tf_op jit(solution)/shard_map/ppermute | solution.py:354
  60.6 0.0 collective-permute-start.9
  60.6 14.6 %all_to_all.10.gains_ref = f32[32,2,128]{2,1,0:T(2,128)S(1)} all-to-all(f32[32,2,128]{2,1,0:T(2,128)S(1)} %get-tuple-element.61), channel_id=1, replica_groups={{0,1,8,9,16,17,24,25,32,33,40,41,48,49,56,57,64,65,72,73,80,81,88,89,96..., dimensions={0} | all-to-all | bytes 65536 | tf_op jit(solution)/shard_map/all_to_all | solution.py:414
  75.2 0.0 collective-permute-done.10.far_ref
  75.2 0.5 shard_map.125
  75.7 1.4 %collective-permute-start.11 = (bf16[144,512]{1,0:T(8,128)(2,1)S(1)}, bf16[144,512]{1,0:T(8,128)(2,1)S(1)}, u32[]{:S(2)}, u32[]{:S(2)}) collective-permute-start(bf16[144,512]{1,0:T(8,128)(2,1)S(1)} %get-tuple-element.63), channel_id=1, source_target_pairs={{0,2},{1,3},{2,4},{3,5},{4,6},{5,7},{6,0},{7,1},{8,10},{9,11},{10,... | collective-permute-start | bytes 442376 | tf_op jit(solution)/shard_map/ppermute | solution.py:354
  77.1 1.6 %collective-permute-start.12 = (bf16[144,512]{1,0:T(8,128)(2,1)S(1)}, bf16[144,512]{1,0:T(8,128)(2,1)S(1)}, u32[]{:S(2)}, u32[]{:S(2)}) collective-permute-start(bf16[144,512]{1,0:T(8,128)(2,1)S(1)} %get-tuple-element.64), channel_id=1, source_target_pairs={{0,4},{1,5},{2,6},{3,7},{4,0},{5,1},{6,2},{7,3},{8,12},{9,13},{10,... | collective-permute-start | bytes 442376 | tf_op jit(solution)/shard_map/ppermute | solution.py:354
  78.7 0.0 collective-permute-done.7.refs_1_
  78.7 1.2 %collective-permute-start.13 = (bf16[144,512]{1,0:T(8,128)(2,1)S(1)}, bf16[144,512]{1,0:T(8,128)(2,1)S(1)}, u32[]{:S(2)}, u32[]{:S(2)}) collective-permute-start(bf16[144,512]{1,0:T(8,128)(2,1)S(1)} %get-tuple-element.65), channel_id=1, source_target_pairs={{0,6},{1,7},{2,0},{3,1},{4,2},{5,3},{6,4},{7,5},{8,14},{9,15},{10,... | collective-permute-start | bytes 442376 | tf_op jit(solution)/shard_map/ppermute | solution.py:354
  79.8 0.0 collective-permute-done.8.refs_2_
  79.9 0.0 collective-permute-done.9.refs_3_
  79.9 1.4 %shard_map.124 = (bf16[128,4096]{1,0:T(8,128)(2,1)}, bf16[128,4096]{1,0:T(8,128)(2,1)}) custom-call(bf16[128,2048]{1,0:T(8,128)(2,1)S(1)} %get-tuple-element.53.refs_0_, bf16[128,2048]{1,0:T(8,128)(2,1)S(1)} %collective-permute-done.7.refs_1_, bf16[128,2048]{1,0:T(8,128)(2,1)S(1)} %collective-permute-done.8.refs_2_, ...), custom_call_target="tpu_custom_call" | custom-call | tf_op jit(solution)/shard_map/pallas_call | solution.py:426
  81.2 4.5 %collective-permute-done.11.refs_1_ = bf16[144,512]{1,0:T(8,128)(2,1)S(1)} collective-permute-done((bf16[144,512]{1,0:T(8,128)(2,1)S(1)}, bf16[144,512]{1,0:T(8,128)(2,1)S(1)}, u32[]{:S(2)}, u32[]{:S(2)}) %collective-permute-start.11) | collective-permute-done | bytes 147488 | tf_op jit(solution)/shard_map/ppermute | solution.py:354
  85.7 0.0 collective-permute-done.12.refs_2_
  85.7 0.6 collective-permute-done.13.refs_3_
  86.3 1.4 %shard_map.126 = (bf16[128,1024]{1,0:T(8,128)(2,1)}, bf16[128,1024]{1,0:T(8,128)(2,1)}, f32[1,128]{1,0:T(1,128)}, f32[1,128]{1,0:T(1,128)}) custom-call(bf16[144,512]{1,0:T(8,128)(2,1)S(1)} %get-tuple-element.62.refs_0_, bf16[144,512]{1,0:T(8,128)(2,1)S(1)} %collective-permute-done.11.refs_1_, bf16[144,512]{1,0:T(8,128)(2,1)S(1)} %collective-permute-done.12.refs_2_, ...), custom_call_target="tpu_custom_call" | custom-call | tf_op jit(solution)/shard_map/pallas_call | solution.py:436
  (11 shorter events, 0.1 us)
Async XLA Ops:
  2.6 6.9 %collective-permute-start = (bf16[128,512]{1,0:T(8,128)(2,1)}, bf16[128,512]{1,0:T(8,128)(2,1)S(1)}, u32[]{:S(2)}, u32[]{:S(2)}) collective-permute-start(bf16[128,512]{1,0:T(8,128)(2,1)} %get-tuple-element.39), channel_id=1, source_target_pairs={{0,2},{1,3},{2,4},{3,5},{4,6},{5,7},{6,0},{7,1},{8,10},{9,11},{10,... | collective-permute-start | bytes 393224 | tf_op jit(solution)/shard_map/ppermute | solution.py:354
  4.3 9.1 %collective-permute-start.1 = (bf16[128,512]{1,0:T(8,128)(2,1)}, bf16[128,512]{1,0:T(8,128)(2,1)S(1)}, u32[]{:S(2)}, u32[]{:S(2)}) collective-permute-start(bf16[128,512]{1,0:T(8,128)(2,1)} %get-tuple-element.40), channel_id=1, source_target_pairs={{0,4},{1,5},{2,6},{3,7},{4,0},{5,1},{6,2},{7,3},{8,12},{9,13},{10,... | collective-permute-start | bytes 393224 | tf_op jit(solution)/shard_map/ppermute | solution.py:354
  7.2 6.2 %collective-permute-start.2 = (bf16[128,512]{1,0:T(8,128)(2,1)}, bf16[128,512]{1,0:T(8,128)(2,1)S(1)}, u32[]{:S(2)}, u32[]{:S(2)}) collective-permute-start(bf16[128,512]{1,0:T(8,128)(2,1)} %get-tuple-element.41), channel_id=1, source_target_pairs={{0,6},{1,7},{2,0},{3,1},{4,2},{5,3},{6,4},{7,5},{8,14},{9,15},{10,... | collective-permute-start | bytes 393224 | tf_op jit(solution)/shard_map/ppermute | solution.py:354
  9.5 1.2 %copy-start.1 = (bf16[128,4096]{1,0:T(8,128)(2,1)S(1)}, bf16[128,4096]{1,0:T(8,128)(2,1)}, u32[]{:S(2)}) copy-start(bf16[128,4096]{1,0:T(8,128)(2,1)} %q_ref.1) | copy-start | bytes 3145732
  10.7 1.2 %copy-start.2 = (bf16[128,4096]{1,0:T(8,128)(2,1)S(1)}, bf16[128,4096]{1,0:T(8,128)(2,1)}, u32[]{:S(2)}) copy-start(bf16[128,4096]{1,0:T(8,128)(2,1)} %g_ref.1) | copy-start | bytes 3145732
  11.9 1.5 %copy-start.3 = (bf16[128,512]{1,0:T(8,128)(2,1)S(1)}, bf16[128,512]{1,0:T(8,128)(2,1)}, u32[]{:S(2)}) copy-start(bf16[128,512]{1,0:T(8,128)(2,1)} %get-tuple-element.38.refs_0_) | copy-start | bytes 393220
  12.4 1.0 %copy-start = (bf16[4,128,1024]{2,1,0:T(8,128)(2,1)}, bf16[4,128,1024]{2,1,0:T(8,128)(2,1)S(1)}, u32[]{:S(2)}) copy-start(bf16[4,128,1024]{2,1,0:T(8,128)(2,1)S(1)} %get-tuple-element.48.refs_0_) | copy-start | bytes 3145732
  13.4 0.7 copy-start.6
  13.4 0.7 copy-start.7
  14.2 0.6 copy-start.4
  14.7 22.6 %all-to-all-start = ((bf16[4,128,1024]{2,1,0:T(8,128)(2,1)}), bf16[4,128,1024]{2,1,0:T(8,128)(2,1)S(1)}, u32[]{:S(2)}, u32[]{:S(2)}) async-start(bf16[4,128,1024]{2,1,0:T(8,128)(2,1)} %shard_map.121), calls=%async_computation | async-start | bytes 2097152 | tf_op jit(solution)/shard_map/all_to_all | solution.py:402
  20.7 9.2 %copy-start.8 = (s32[16,8]{0,1:T(8,128)S(1)}, s32[16,8]{0,1:T(8,128)}, u32[]{:S(2)}) copy-start(s32[16,8]{0,1:T(8,128)} %param.13) | copy-start | bytes 1540
  20.7 12.1 %collective-permute-start.3 = (bf16[512,512]{1,0:T(8,128)(2,1)S(1)}, bf16[512,512]{1,0:T(8,128)(2,1)S(1)}, u32[]{:S(2)}, u32[]{:S(2)}) collective-permute-start(bf16[512,512]{1,0:T(8,128)(2,1)S(1)} %get-tuple-element.43.refs_2_.kv_ref), channel_id=1, source_target_pairs={{0,1},{1,0},{2,3},{3,2},{4,5},{5,4},{6,7},{7,6},{8,9},{9,8},{10,11... | collective-permute-start | bytes 1572872 | tf_op jit(solution)/shard_map/ppermute | solution.py:364
  23.7 20.4 %collective-permute-start.4 = (bf16[128,1024]{1,0:T(8,128)(2,1)S(1)}, bf16[128,1024]{1,0:T(8,128)(2,1)S(1)}, u32[]{:S(2)}, u32[]{:S(2)}) collective-permute-start(bf16[128,1024]{1,0:T(8,128)(2,1)S(1)} %get-tuple-element.45), channel_id=1, source_target_pairs={{0,2},{1,3},{2,4},{3,5},{4,6},{5,7},{6,0},{7,1},{8,10},{9,11},{10,... | collective-permute-start | bytes 786440 | tf_op jit(solution)/shard_map/ppermute | solution.py:354
  25.7 18.5 %collective-permute-start.5 = (bf16[128,1024]{1,0:T(8,128)(2,1)S(1)}, bf16[128,1024]{1,0:T(8,128)(2,1)}, u32[]{:S(2)}, u32[]{:S(2)}) collective-permute-start(bf16[128,1024]{1,0:T(8,128)(2,1)S(1)} %get-tuple-element.46), channel_id=1, source_target_pairs={{0,4},{1,5},{2,6},{3,7},{4,0},{5,1},{6,2},{7,3},{8,12},{9,13},{10,... | collective-permute-start | bytes 786440 | tf_op jit(solution)/shard_map/ppermute | solution.py:354
  28.4 15.9 %collective-permute-start.6 = (bf16[128,1024]{1,0:T(8,128)(2,1)S(1)}, bf16[128,1024]{1,0:T(8,128)(2,1)}, u32[]{:S(2)}, u32[]{:S(2)}) collective-permute-start(bf16[128,1024]{1,0:T(8,128)(2,1)S(1)} %get-tuple-element.47), channel_id=1, source_target_pairs={{0,6},{1,7},{2,0},{3,1},{4,2},{5,3},{6,4},{7,5},{8,14},{9,15},{10,... | collective-permute-start | bytes 786440 | tf_op jit(solution)/shard_map/ppermute | solution.py:354
  29.9 7.4 %copy-start.5 = (f32[2,128]{1,0:T(2,128)S(1)}, f32[2,128]{1,0:T(2,128)}, u32[]{:S(2)}) copy-start(f32[2,128]{1,0:T(2,128)} %copy-done.4) | copy-start | bytes 3076
  51.7 23.5 %collective-permute-start.10 = (bf16[512,512]{1,0:T(8,128)(2,1)S(1)}, bf16[512,512]{1,0:T(8,128)(2,1)S(1)}, u32[]{:S(2)}, u32[]{:S(2)}) collective-permute-start(bf16[512,512]{1,0:T(8,128)(2,1)S(1)} %get-tuple-element.60), channel_id=1, source_target_pairs={{0,1},{1,0},{2,3},{3,2},{4,5},{5,4},{6,7},{7,6},{8,9},{9,8},{10,11... | collective-permute-start | bytes 1572872 | tf_op jit(solution)/shard_map/ppermute | solution.py:364
  56.0 22.6 %collective-permute-start.7 = (bf16[128,2048]{1,0:T(8,128)(2,1)S(1)}, bf16[128,2048]{1,0:T(8,128)(2,1)S(1)}, u32[]{:S(2)}, u32[]{:S(2)}) collective-permute-start(bf16[128,2048]{1,0:T(8,128)(2,1)S(1)} %get-tuple-element.54), channel_id=1, source_target_pairs={{0,2},{1,3},{2,4},{3,5},{4,6},{5,7},{6,0},{7,1},{8,10},{9,11},{10,... | collective-permute-start | bytes 1572872 | tf_op jit(solution)/shard_map/ppermute | solution.py:354
  57.5 22.4 %collective-permute-start.8 = (bf16[128,2048]{1,0:T(8,128)(2,1)S(1)}, bf16[128,2048]{1,0:T(8,128)(2,1)S(1)}, u32[]{:S(2)}, u32[]{:S(2)}) collective-permute-start(bf16[128,2048]{1,0:T(8,128)(2,1)S(1)} %get-tuple-element.55), channel_id=1, source_target_pairs={{0,4},{1,5},{2,6},{3,7},{4,0},{5,1},{6,2},{7,3},{8,12},{9,13},{10,... | collective-permute-start | bytes 1572872 | tf_op jit(solution)/shard_map/ppermute | solution.py:354
  60.6 19.3 %collective-permute-start.9 = (bf16[128,2048]{1,0:T(8,128)(2,1)S(1)}, bf16[128,2048]{1,0:T(8,128)(2,1)S(1)}, u32[]{:S(2)}, u32[]{:S(2)}) collective-permute-start(bf16[128,2048]{1,0:T(8,128)(2,1)S(1)} %get-tuple-element.56), channel_id=1, source_target_pairs={{0,6},{1,7},{2,0},{3,1},{4,2},{5,3},{6,4},{7,5},{8,14},{9,15},{10,... | collective-permute-start | bytes 1572872 | tf_op jit(solution)/shard_map/ppermute | solution.py:354
  75.7 10.0 %collective-permute-start.11 = (bf16[144,512]{1,0:T(8,128)(2,1)S(1)}, bf16[144,512]{1,0:T(8,128)(2,1)S(1)}, u32[]{:S(2)}, u32[]{:S(2)}) collective-permute-start(bf16[144,512]{1,0:T(8,128)(2,1)S(1)} %get-tuple-element.63), channel_id=1, source_target_pairs={{0,2},{1,3},{2,4},{3,5},{4,6},{5,7},{6,0},{7,1},{8,10},{9,11},{10,... | collective-permute-start | bytes 442376 | tf_op jit(solution)/shard_map/ppermute | solution.py:354
  77.1 8.6 %collective-permute-start.12 = (bf16[144,512]{1,0:T(8,128)(2,1)S(1)}, bf16[144,512]{1,0:T(8,128)(2,1)S(1)}, u32[]{:S(2)}, u32[]{:S(2)}) collective-permute-start(bf16[144,512]{1,0:T(8,128)(2,1)S(1)} %get-tuple-element.64), channel_id=1, source_target_pairs={{0,4},{1,5},{2,6},{3,7},{4,0},{5,1},{6,2},{7,3},{8,12},{9,13},{10,... | collective-permute-start | bytes 442376 | tf_op jit(solution)/shard_map/ppermute | solution.py:354
  78.7 7.6 %collective-permute-start.13 = (bf16[144,512]{1,0:T(8,128)(2,1)S(1)}, bf16[144,512]{1,0:T(8,128)(2,1)S(1)}, u32[]{:S(2)}, u32[]{:S(2)}) collective-permute-start(bf16[144,512]{1,0:T(8,128)(2,1)S(1)} %get-tuple-element.65), channel_id=1, source_target_pairs={{0,6},{1,7},{2,0},{3,1},{4,2},{5,3},{6,4},{7,5},{8,14},{9,15},{10,... | collective-permute-start | bytes 442376 | tf_op jit(solution)/shard_map/ppermute | solution.py:354

commit v2 on v1

--- a/solution.py
+++ b/solution.py
@@ -19,6 +19,7 @@
 PARTS = KVH // YS
 WIDTH = GROUP * HD
 TAIL = 16
+PAIR = 2
 EPS = 1e-06
 FACTOR = HD ** (-0.5)
 EXP2_FACTOR = FACTOR * math.log2(math.e)
@@ -144,7 +145,7 @@
         del refs[: YS + 3]
         qg_ref = refs.pop()
         y_ref = refs.pop()
-    kn_ref, v_ref, dk_ref, dv_ref, qn_ref, g_ref, out_ref, dq_ref, bias_ref = refs
+    kn_ref, v_ref, dk_ref, dv_ref, unit_ref, inv_ref, qn_ref, g_ref, dq_ref = refs
     replica = lax.axis_index("dp")
     column = lax.rem(lax.axis_index("head"), 2)
     q_gain = both_gains_ref[0:1, :]
@@ -163,83 +164,108 @@
             qg_ref[block_rows(behind(step)), :] = pieces[step][...]
     dk_ref[...] = jnp.zeros_like(dk_ref)
     dv_ref[...] = jnp.zeros_like(dv_ref)
+    for h in range(GROUP):
+        unit, inverse = unit_of(qg_ref[:, h * HD : (h + 1) * HD])
+        unit_ref[h] = unit
+        inv_ref[h] = jnp.broadcast_to(inverse, unit.shape)
+        normed = (unit * q_gain).astype(BF16)
+        g = qg_ref[:, WIDTH + h * HD : WIDTH + (h + 1) * HD]
+        for j in range(YS):
+            to = slice(j * WIDTH + h * BLK, j * WIDTH + (h + 1) * BLK)
+            qn_ref[to, :] = normed[j * BLK : (j + 1) * BLK]
+            g_ref[to, :] = g[j * BLK : (j + 1) * BLK]
     ends = []
     total = jnp.int32(0)
     for d in range(lengths_ref.shape[1]):
         total = total + lengths_ref[replica, d]
         ends.append(total)
 
-    def block(j, q_sum):
-        here = block_rows(j)
-        i = 2 * j + column
-        row0 = i * BLK
-        places = row0 + lax.broadcasted_iota(jnp.int32, (BLK, BLK), 0)
-        begins = jnp.zeros((BLK, BLK), jnp.int32)
-        begin0 = jnp.int32(0)
-        for end in ends:
-            begins = jnp.where(end <= places, end, begins)
-            begin0 = jnp.where(end <= row0, end, begin0)
-        first_block = begin0 // BLK
-        needed = i - first_block + 1
-        units = []
-        for h in range(GROUP):
-            unit, inverse = unit_of(qg_ref[here, h * HD : (h + 1) * HD])
-            units.append((unit, inverse))
-            qn_ref[h * BLK : (h + 1) * BLK, :] = (unit * q_gain).astype(BF16)
-            g_ref[h * BLK : (h + 1) * BLK, :] = qg_ref[here, WIDTH + h * HD : WIDTH + (h + 1) * HD]
-        for blocks in range(1, WINDOWS + 1):
-
-            @pl.when(needed == blocks)
+    def steps(count, first):
+        blocks = []
+        needed = jnp.int32(1)
+        for n in range(count):
+            j = first + n
+            i = 2 * j + column
+            begin0 = jnp.int32(0)
+            for end in ends:
+                begin0 = jnp.where(end <= i * BLK, end, begin0)
+            needed = jnp.maximum(needed, i - begin0 // BLK + 1)
+            blocks.append((j, i))
+
+        def attend_window(tiles):
+            keys = tiles * BLK
+            rows = [pl.ds(pl.multiple_of(j * WIDTH, WIDTH), WIDTH) for j, _ in blocks]
+            starts = [jnp.maximum(i - (tiles - 1), 0) * BLK for _, i in blocks]
+            windows = [pl.ds(pl.multiple_of(k0, BLK), keys) for k0 in starts]
+            qn = [qn_ref[at, :] for at in rows]
+            g = [g_ref[at, :] for at in rows]
+            kn = [kn_ref[at, :] for at in windows]
+            v = [v_ref[at, :] for at in windows]
+            scores = [dot(a, b, (1, 1)) for a, b in zip(qn, kn)]
+            dweights = [dot(a, b, (1, 1)) for a, b in zip(g, v)]
+            biases = []
+            for (j, i), k0 in zip(blocks, starts):
+                places = i * BLK + lax.broadcasted_iota(jnp.int32, (BLK, BLK), 0)
+                begins = jnp.zeros((BLK, BLK), jnp.int32)
+                for end in ends:
+                    begins = jnp.where(end <= places, end, begins)
+                lane = k0 + lax.broadcasted_iota(jnp.int32, (BLK, BLK), 1)
+                biases.append(
+                    jnp.concatenate(
+                        [
+                            jnp.where((lane + t * BLK >= begins) & (lane + t * BLK <= places), 0.0, -1e30)
+                            for t in range(tiles)
+                        ],
+                        axis=1,
+                    )
+                )
+            scores = [
+                (x.reshape(GROUP, BLK, keys) + bias[None]).reshape(WIDTH, keys) for x, bias in zip(scores, biases)
+            ]
+            raised = [jnp.exp2((x - jnp.max(x, axis=1, keepdims=True)) * EXP2_FACTOR) for x in scores]
+            weights = [x * (1.0 / jnp.sum(x, axis=1, keepdims=True)) for x in raised]
+            rounded = [x.astype(BF16) for x in weights]
+            out = [dot(x, b, (1, 0)) for x, b in zip(rounded, v)]
+            delta = [jnp.sum(a.astype(F32) * x, axis=1, keepdims=True) for a, x in zip(g, out)]
+            dscores = [
+                (w * (dw - d) * FACTOR).astype(BF16) for w, dw, d in zip(weights, dweights, delta)
+            ]
+            for n, (j, _) in enumerate(blocks):
+                dq_ref[rows[n], :] = dot(dscores[n], kn[n], (1, 0))
+                dv_ref[n, windows[n], :] += dot(rounded[n], g[n], (0, 0))
+                dk_ref[n, windows[n], :] += dot(dscores[n], qn[n], (0, 0))
+                here = block_rows(j)
+                for h in range(GROUP):
+                    y_ref[here, h * HD : (h + 1) * HD] = out[n][h * BLK : (h + 1) * BLK, :].astype(BF16)
+
+        for tiles in range(1, WINDOWS + 1):
+
+            @pl.when(needed == tiles)
             def _():
-                keys = blocks * BLK
-                k0 = pl.multiple_of(first_block * BLK, BLK)
-                window = pl.ds(k0, keys)
-                lane = k0 + lax.broadcasted_iota(jnp.int32, (BLK, BLK), 1)
-                for t in range(blocks):
-                    place = lane + t * BLK
-                    seen = place >= begins
-                    if t == blocks - 1:
-                        seen = seen & (place <= places)
-                    bias_ref[:, t * BLK : (t + 1) * BLK] = jnp.where(seen, 0.0, -1e30)
-                qn = qn_ref[...]
-                g = g_ref[...]
-                kn = kn_ref[window, :]
-                v = v_ref[window, :]
-                bias = bias_ref[:, :keys]
-                scores = dot(qn, kn, (1, 1)).reshape(GROUP, BLK, keys) + bias[None]
-                scores = scores.reshape(GROUP * BLK, keys)
-                peak = jnp.max(scores, axis=1, keepdims=True)
-                raised = jnp.exp2((scores - peak) * EXP2_FACTOR)
-                weights = raised * (1.0 / jnp.sum(raised, axis=1, keepdims=True))
-                rounded = weights.astype(BF16)
-                out = dot(rounded, v, (1, 0))
-                out_ref[...] = out
-                dv_ref[window, :] += dot(rounded, g, (0, 0))
-                dweights = dot(g, v, (1, 1))
-                delta = jnp.sum(g.astype(F32) * out, axis=1, keepdims=True)
-                dscores = (weights * (dweights - delta) * FACTOR).astype(BF16)
-                dq_ref[...] = dot(dscores, kn, (1, 0))
-                dk_ref[window, :] += dot(dscores, qn, (0, 0))
-
-        for h in range(GROUP):
-            unit, inverse = units[h]
-            local = slice(h * BLK, (h + 1) * BLK)
-            y_ref[here, h * HD : (h + 1) * HD] = out_ref[local, :].astype(BF16)
-            dq = dq_ref[local, :]
-            back = norm_back(dq, unit, inverse, q_gain)
-            y_ref[here, WIDTH + h * HD : WIDTH + (h + 1) * HD] = back.astype(BF16)
+                attend_window(tiles)
+
+    def pair(p, carry):
+        steps(PAIR, PAIR * p)
+        return carry
+
+    lax.fori_loop(0, YS // PAIR, pair, 0)
+    q_sum = jnp.zeros((8, HD), F32)
+    for h in range(GROUP):
+        for j in range(YS):
+            local = slice(j * BLK, (j + 1) * BLK)
+            unit = unit_ref[h, local, :]
+            dq = dq_ref[j * WIDTH + h * BLK : j * WIDTH + (h + 1) * BLK, :]
+            back = norm_back(dq, unit, inv_ref[h, local, :], q_gain)
+            y_ref[local, WIDTH + h * HD : WIDTH + (h + 1) * HD] = back.astype(BF16)
             q_sum = q_sum + fold(dq * unit)
-        return q_sum
-
-    q_sum = lax.fori_loop(0, YS, block, jnp.zeros((8, HD), F32))
     k_sum = jnp.zeros((8, HD), F32)
     for j in range(YS):
         local = slice(j * BLK, (j + 1) * BLK)
         for ref, col in ((own_ref, column), (far_ref, 1 - column)):
             place = block_rows(2 * j + col)
             unit, _ = unit_of(ref[local, k_at])
-            dk = dk_ref[place, :]
-            dv = dv_ref[place, :]
+            dk = sum(dk_ref[n, place, :] for n in range(PAIR))
+            dv = sum(dv_ref[n, place, :] for n in range(PAIR))
             k_sum = k_sum + fold(dk * unit)
             target = own_out if ref is own_ref else far_out
             target[local, k_at] = dk.astype(target.dtype)
@@ -276,13 +302,13 @@
     scratch = [
         pltpu.VMEM((span, HD), BF16),
         pltpu.VMEM((span, HD), BF16),
-        pltpu.VMEM((span, HD), F32),
-        pltpu.VMEM((span, HD), F32),
-        pltpu.VMEM((WIDTH, HD), BF16),
-        pltpu.VMEM((WIDTH, HD), BF16),
-        pltpu.VMEM((WIDTH, HD), F32),
-        pltpu.VMEM((WIDTH, HD), F32),
-        pltpu.VMEM((BLK, WINDOWS * BLK), F32),
+        pltpu.VMEM((PAIR, span, HD), F32),
+        pltpu.VMEM((PAIR, span, HD), F32),
+        pltpu.VMEM((GROUP, half, HD), F32),
+        pltpu.VMEM((GROUP, half, HD), F32),
+        pltpu.VMEM((GROUP * half, HD), BF16),
+        pltpu.VMEM((GROUP * half, HD), BF16),
+        pltpu.VMEM((GROUP * half, HD), F32),
     ]
     if part > 0:
         scratch += [pltpu.VMEM((half, 2 * WIDTH), BF16)] * 2

time: 88 us -> 85.7 us (0.974)
  starting transfers between devices: 34.1 us -> 31.9 us
  Pallas kernels: 19.9 us -> 18.4 us
  waiting for transfers between devices: 13.6 us -> 14.5 us
    ppermute x2, starting transfers between devices: 7.34 us -> 5.87 us  [over_x(): return lax.ppermute(x, 'head', [(i, i ^ 1) for i in range(2 * YS)])]
    pallas_call x2, Pallas kernels: 14.2 us -> 12.7 us  [attend(): pl.pallas_call(functools.partial(attend_kernel, part), out_shape=out_shap...]
where the time goes in v2:
time: 85.7 us; the launch traced here: 85.3 us
  starting transfers between devices  31.9 us (37%)
  Pallas kernels  18.4 us (21%)
  blocking collectives  14.9 us (17%)
  waiting for transfers between devices  14.5 us (17%)
  local copies, waits for them, and re-layouts  4.72 us (6%)
  between operations  0.92 us (1%)
    ppermute x12, starting transfers between devices, over_y(): lax.ppermute(pieces[step], 'head', [(2 * y + c, 2 * ((y + step) % YS) + c...  20.1 us
    all_to_all x1, blocking collectives, on_device(): lax.all_to_all(gains, ('dp', 'head'), split_axis=0, concat_axis=0, tiled=...  14.9 us
    pallas_call x2, Pallas kernels, attend(): pl.pallas_call(functools.partial(attend_kernel, part), out_shape=out_shap...  12.7 us
    ppermute x12, waiting for transfers between devices, over_y(): lax.ppermute(pieces[step], 'head', [(2 * y + c, 2 * ((y + step) % YS) + c...  7.04 us
    all_to_all x1, starting transfers between devices, on_device(): lax.all_to_all(soon, 'head', split_axis=0, concat_axis=0, tiled=True, axi...  5.93 us
    ppermute x2, starting transfers between devices, over_x(): return lax.ppermute(x, 'head', [(i, i ^ 1) for i in range(2 * YS)])  5.87 us
    unnamed x19, local copies, waits for them, and re-layouts  4.72 us
    all_to_all x1, waiting for transfers between devices, on_device(): lax.all_to_all(soon, 'head', split_axis=0, concat_axis=0, tiled=True, axi...  4.59 us
  transfers between devices with their start and end apart: 15, of which 7 were waited for; matrix products, arithmetic and copies ran while one was open for 0% of the time, Pallas kernels for 10%

profile of v2, /device:TPU:0, one launch (start us, length us, event | category | flops | bytes accessed | tf_op | source)
XLA Modules:
  0.0 85.3 jit_solution(9901957834791099262)
XLA Ops:
  0.6 1.9 %shard_map.118 = (bf16[128,512]{1,0:T(8,128)(2,1)}, bf16[128,512]{1,0:T(8,128)(2,1)}, bf16[128,512]{1,0:T(8,128)(2,1)}, bf16[128,512]{1,0:T(8,128)(2,1)}) custom-call(bf16[128,1024]{1,0:T(8,128)(2,1)} %k_ref.1, bf16[128,1024]{1,0:T(8,128)(2,1)} %v_ref.1), custom_call_target="tpu_custom_call" | custom-call | tf_op jit(solution)/shard_map/pallas_call | solution.py:400
  2.6 1.7 %collective-permute-start = (bf16[128,512]{1,0:T(8,128)(2,1)}, bf16[128,512]{1,0:T(8,128)(2,1)S(1)}, u32[]{:S(2)}, u32[]{:S(2)}) collective-permute-start(bf16[128,512]{1,0:T(8,128)(2,1)} %get-tuple-element.39), channel_id=1, source_target_pairs={{0,2},{1,3},{2,4},{3,5},{4,6},{5,7},{6,0},{7,1},{8,10},{9,11},{10,... | collective-permute-start | bytes 393224 | tf_op jit(solution)/shard_map/ppermute | solution.py:380
  4.3 2.9 %collective-permute-start.1 = (bf16[128,512]{1,0:T(8,128)(2,1)}, bf16[128,512]{1,0:T(8,128)(2,1)S(1)}, u32[]{:S(2)}, u32[]{:S(2)}) collective-permute-start(bf16[128,512]{1,0:T(8,128)(2,1)} %get-tuple-element.40), channel_id=1, source_target_pairs={{0,4},{1,5},{2,6},{3,7},{4,0},{5,1},{6,2},{7,3},{8,12},{9,13},{10,... | collective-permute-start | bytes 393224 | tf_op jit(solution)/shard_map/ppermute | solution.py:380
  7.2 1.3 %collective-permute-start.2 = (bf16[128,512]{1,0:T(8,128)(2,1)}, bf16[128,512]{1,0:T(8,128)(2,1)S(1)}, u32[]{:S(2)}, u32[]{:S(2)}) collective-permute-start(bf16[128,512]{1,0:T(8,128)(2,1)} %get-tuple-element.41), channel_id=1, source_target_pairs={{0,6},{1,7},{2,0},{3,1},{4,2},{5,3},{6,4},{7,5},{8,14},{9,15},{10,... | collective-permute-start | bytes 393224 | tf_op jit(solution)/shard_map/ppermute | solution.py:380
  8.6 0.9 %collective-permute-done.refs_1_._ = bf16[128,512]{1,0:T(8,128)(2,1)S(1)} collective-permute-done((bf16[128,512]{1,0:T(8,128)(2,1)}, bf16[128,512]{1,0:T(8,128)(2,1)S(1)}, u32[]{:S(2)}, u32[]{:S(2)}) %collective-permute-start) | collective-permute-done | bytes 131104 | tf_op jit(solution)/shard_map/ppermute | solution.py:380
  9.5 1.2 %copy-done.1 = bf16[128,4096]{1,0:T(8,128)(2,1)S(1)} copy-done((bf16[128,4096]{1,0:T(8,128)(2,1)S(1)}, bf16[128,4096]{1,0:T(8,128)(2,1)}, u32[]{:S(2)}) %copy-start.1) | copy-done | bytes 1048600
  10.7 1.2 %copy-done.2 = bf16[128,4096]{1,0:T(8,128)(2,1)S(1)} copy-done((bf16[128,4096]{1,0:T(8,128)(2,1)S(1)}, bf16[128,4096]{1,0:T(8,128)(2,1)}, u32[]{:S(2)}) %copy-start.2) | copy-done | bytes 1048600
  11.9 0.5 shard_map.120
  12.4 0.0 copy-start
  12.4 1.0 %copy-done = bf16[4,128,1024]{2,1,0:T(8,128)(2,1)} copy-done((bf16[4,128,1024]{2,1,0:T(8,128)(2,1)}, bf16[4,128,1024]{2,1,0:T(8,128)(2,1)S(1)}, u32[]{:S(2)}) %copy-start) | copy-done | bytes 1048600
  13.4 0.1 collective-permute-done.1.refs_2_
  13.4 0.0 collective-permute-done.2.refs_3_
  13.5 0.6 copy-done.6
  14.1 0.0 copy-done.7
  14.2 0.0 copy-start.4
  14.2 0.6 copy-done.4
  14.7 5.9 %all-to-all-start = ((bf16[4,128,1024]{2,1,0:T(8,128)(2,1)}), bf16[4,128,1024]{2,1,0:T(8,128)(2,1)S(1)}, u32[]{:S(2)}, u32[]{:S(2)}) async-start(bf16[4,128,1024]{2,1,0:T(8,128)(2,1)} %shard_map.121), calls=%async_computation | async-start | bytes 2097152 | tf_op jit(solution)/shard_map/all_to_all | solution.py:428
  20.7 3.0 %collective-permute-start.3 = (bf16[512,512]{1,0:T(8,128)(2,1)S(1)}, bf16[512,512]{1,0:T(8,128)(2,1)S(1)}, u32[]{:S(2)}, u32[]{:S(2)}) collective-permute-start(bf16[512,512]{1,0:T(8,128)(2,1)S(1)} %get-tuple-element.43.refs_2_.kv_ref), channel_id=1, source_target_pairs={{0,1},{1,0},{2,3},{3,2},{4,5},{5,4},{6,7},{7,6},{8,9},{9,8},{10,11... | collective-permute-start | bytes 1572872 | tf_op jit(solution)/shard_map/ppermute | solution.py:390
  23.7 2.0 %collective-permute-start.4 = (bf16[128,1024]{1,0:T(8,128)(2,1)S(1)}, bf16[128,1024]{1,0:T(8,128)(2,1)S(1)}, u32[]{:S(2)}, u32[]{:S(2)}) collective-permute-start(bf16[128,1024]{1,0:T(8,128)(2,1)S(1)} %get-tuple-element.45), channel_id=1, source_target_pairs={{0,2},{1,3},{2,4},{3,5},{4,6},{5,7},{6,0},{7,1},{8,10},{9,11},{10,... | collective-permute-start | bytes 786440 | tf_op jit(solution)/shard_map/ppermute | solution.py:380
  25.7 2.7 %collective-permute-start.5 = (bf16[128,1024]{1,0:T(8,128)(2,1)S(1)}, bf16[128,1024]{1,0:T(8,128)(2,1)}, u32[]{:S(2)}, u32[]{:S(2)}) collective-permute-start(bf16[128,1024]{1,0:T(8,128)(2,1)S(1)} %get-tuple-element.46), channel_id=1, source_target_pairs={{0,4},{1,5},{2,6},{3,7},{4,0},{5,1},{6,2},{7,3},{8,12},{9,13},{10,... | collective-permute-start | bytes 786440 | tf_op jit(solution)/shard_map/ppermute | solution.py:380
  28.4 1.5 %collective-permute-start.6 = (bf16[128,1024]{1,0:T(8,128)(2,1)S(1)}, bf16[128,1024]{1,0:T(8,128)(2,1)}, u32[]{:S(2)}, u32[]{:S(2)}) collective-permute-start(bf16[128,1024]{1,0:T(8,128)(2,1)S(1)} %get-tuple-element.47), channel_id=1, source_target_pairs={{0,6},{1,7},{2,0},{3,1},{4,2},{5,3},{6,4},{7,5},{8,14},{9,15},{10,... | collective-permute-start | bytes 786440 | tf_op jit(solution)/shard_map/ppermute | solution.py:380
  29.9 0.1 copy.15.refs_0_
  29.9 2.8 %collective-permute-done.3.refs_3_ = bf16[512,512]{1,0:T(8,128)(2,1)S(1)} collective-permute-done((bf16[512,512]{1,0:T(8,128)(2,1)S(1)}, bf16[512,512]{1,0:T(8,128)(2,1)S(1)}, u32[]{:S(2)}, u32[]{:S(2)}) %collective-permute-start.3) | collective-permute-done | bytes 524320 | tf_op jit(solution)/shard_map/ppermute | solution.py:390
  32.8 4.6 %all-to-all-done = bf16[4,128,1024]{2,1,0:T(8,128)(2,1)S(1)} async-done(((bf16[4,128,1024]{2,1,0:T(8,128)(2,1)}), bf16[4,128,1024]{2,1,0:T(8,128)(2,1)S(1)}, u32[]{:S(2)}, u32[]{:S(2)}) %all-to-all-start) | async-done | bytes 1048608 | tf_op jit(solution)/shard_map/all_to_all | solution.py:428
  37.3 0.0 copy-done.5
  37.3 5.8 %shard_map.122 = (bf16[512,1024]{1,0:T(8,128)(2,1)S(1)}, bf16[512,512]{1,0:T(8,128)(2,1)S(1)}, f32[512,512]{1,0:T(8,128)S(1)}, f32[2,128]{1,0:T(2,128)S(1)}) custom-call(s32[16,8]{1,0:T(8,128)S(1)} %copy.15.refs_0_, f32[2,128]{1,0:T(2,128)S(1)} %copy-done.5, bf16[512,512]{1,0:T(8,128)(2,1)S(1)} %get-tuple-element.43.refs_2_.kv_ref, ...), custom_call_target="tpu_custom_call" | custom-call | flops 2013265920 | bytes 4194304 | tf_op jit(solution)/shard_map/pallas_call | solution.py:315
  43.2 0.0 collective-permute-done.4.refs_5_
  43.2 1.1 %collective-permute-done.5.refs_6_ = bf16[128,1024]{1,0:T(8,128)(2,1)} collective-permute-done((bf16[128,1024]{1,0:T(8,128)(2,1)S(1)}, bf16[128,1024]{1,0:T(8,128)(2,1)}, u32[]{:S(2)}, u32[]{:S(2)}) %collective-permute-start.5) | collective-permute-done | bytes 262176 | tf_op jit(solution)/shard_map/ppermute | solution.py:380
  44.3 0.0 collective-permute-done.6.refs_7_
  44.3 6.9 %shard_map.123 = (bf16[128,2048]{1,0:T(8,128)(2,1)S(1)}, bf16[128,2048]{1,0:T(8,128)(2,1)S(1)}, bf16[128,2048]{1,0:T(8,128)(2,1)S(1)}, bf16[128,2048]{1,0:T(8,12...) custom-call(s32[16,8]{1,0:T(8,128)S(1)} %copy.15.refs_0_, ...), custom_call_target="tpu_custom_call" | custom-call | flops 2013265920 | bytes 4194304 | tf_op jit(solution)/shard_map/pallas_call | solution.py:315
  51.1 2.8 %collective-permute-start.10 = (bf16[512,512]{1,0:T(8,128)(2,1)S(1)}, bf16[512,512]{1,0:T(8,128)(2,1)S(1)}, u32[]{:S(2)}, u32[]{:S(2)}) collective-permute-start(bf16[512,512]{1,0:T(8,128)(2,1)S(1)} %get-tuple-element.60), channel_id=1, source_target_pairs={{0,1},{1,0},{2,3},{3,2},{4,5},{5,4},{6,7},{7,6},{8,9},{9,8},{10,11... | collective-permute-start | bytes 1572872 | tf_op jit(solution)/shard_map/ppermute | solution.py:390
  54.0 0.4 collective-permute-start.7
  54.3 3.1 %collective-permute-start.8 = (bf16[128,2048]{1,0:T(8,128)(2,1)S(1)}, bf16[128,2048]{1,0:T(8,128)(2,1)S(1)}, u32[]{:S(2)}, u32[]{:S(2)}) collective-permute-start(bf16[128,2048]{1,0:T(8,128)(2,1)S(1)} %get-tuple-element.55), channel_id=1, source_target_pairs={{0,4},{1,5},{2,6},{3,7},{4,0},{5,1},{6,2},{7,3},{8,12},{9,13},{10,... | collective-permute-start | bytes 1572872 | tf_op jit(solution)/shard_map/ppermute | solution.py:380
  57.4 0.3 collective-permute-start.9
  57.7 14.9 %all_to_all.10.gains_ref = f32[32,2,128]{2,1,0:T(2,128)S(1)} all-to-all(f32[32,2,128]{2,1,0:T(2,128)S(1)} %get-tuple-element.61), channel_id=1, replica_groups={{0,1,8,9,16,17,24,25,32,33,40,41,48,49,56,57,64,65,72,73,80,81,88,89,96..., dimensions={0} | all-to-all | bytes 65536 | tf_op jit(solution)/shard_map/all_to_all | solution.py:440
  72.7 0.0 collective-permute-done.10.far_ref
  72.7 0.5 shard_map.125
  73.2 1.3 %collective-permute-start.11 = (bf16[144,512]{1,0:T(8,128)(2,1)S(1)}, bf16[144,512]{1,0:T(8,128)(2,1)S(1)}, u32[]{:S(2)}, u32[]{:S(2)}) collective-permute-start(bf16[144,512]{1,0:T(8,128)(2,1)S(1)} %get-tuple-element.63), channel_id=1, source_target_pairs={{0,2},{1,3},{2,4},{3,5},{4,6},{5,7},{6,0},{7,1},{8,10},{9,11},{10,... | collective-permute-start | bytes 442376 | tf_op jit(solution)/shard_map/ppermute | solution.py:380
  74.5 1.7 %collective-permute-start.12 = (bf16[144,512]{1,0:T(8,128)(2,1)S(1)}, bf16[144,512]{1,0:T(8,128)(2,1)S(1)}, u32[]{:S(2)}, u32[]{:S(2)}) collective-permute-start(bf16[144,512]{1,0:T(8,128)(2,1)S(1)} %get-tuple-element.64), channel_id=1, source_target_pairs={{0,4},{1,5},{2,6},{3,7},{4,0},{5,1},{6,2},{7,3},{8,12},{9,13},{10,... | collective-permute-start | bytes 442376 | tf_op jit(solution)/shard_map/ppermute | solution.py:380
  76.1 0.0 collective-permute-done.7.refs_1_
  76.2 1.2 %collective-permute-start.13 = (bf16[144,512]{1,0:T(8,128)(2,1)S(1)}, bf16[144,512]{1,0:T(8,128)(2,1)S(1)}, u32[]{:S(2)}, u32[]{:S(2)}) collective-permute-start(bf16[144,512]{1,0:T(8,128)(2,1)S(1)} %get-tuple-element.65), channel_id=1, source_target_pairs={{0,6},{1,7},{2,0},{3,1},{4,2},{5,3},{6,4},{7,5},{8,14},{9,15},{10,... | collective-permute-start | bytes 442376 | tf_op jit(solution)/shard_map/ppermute | solution.py:380
  77.4 0.0 collective-permute-done.8.refs_2_
  77.4 0.0 collective-permute-done.9.refs_3_
  77.4 1.4 %shard_map.124 = (bf16[128,4096]{1,0:T(8,128)(2,1)}, bf16[128,4096]{1,0:T(8,128)(2,1)}) custom-call(bf16[128,2048]{1,0:T(8,128)(2,1)S(1)} %get-tuple-element.53.refs_0_, bf16[128,2048]{1,0:T(8,128)(2,1)S(1)} %collective-permute-done.7.refs_1_, bf16[128,2048]{1,0:T(8,128)(2,1)S(1)} %collective-permute-done.8.refs_2_, ...), custom_call_target="tpu_custom_call" | custom-call | tf_op jit(solution)/shard_map/pallas_call | solution.py:452
  78.8 4.4 %collective-permute-done.11.refs_1_ = bf16[144,512]{1,0:T(8,128)(2,1)S(1)} collective-permute-done((bf16[144,512]{1,0:T(8,128)(2,1)S(1)}, bf16[144,512]{1,0:T(8,128)(2,1)S(1)}, u32[]{:S(2)}, u32[]{:S(2)}) %collective-permute-start.11) | collective-permute-done | bytes 147488 | tf_op jit(solution)/shard_map/ppermute | solution.py:380
  83.2 0.0 collective-permute-done.12.refs_2_
  83.2 0.6 collective-permute-done.13.refs_3_
  83.8 1.4 %shard_map.126 = (bf16[128,1024]{1,0:T(8,128)(2,1)}, bf16[128,1024]{1,0:T(8,128)(2,1)}, f32[1,128]{1,0:T(1,128)}, f32[1,128]{1,0:T(1,128)}) custom-call(bf16[144,512]{1,0:T(8,128)(2,1)S(1)} %get-tuple-element.62.refs_0_, bf16[144,512]{1,0:T(8,128)(2,1)S(1)} %collective-permute-done.11.refs_1_, bf16[144,512]{1,0:T(8,128)(2,1)S(1)} %collective-permute-done.12.refs_2_, ...), custom_call_target="tpu_custom_call" | custom-call | tf_op jit(solution)/shard_map/pallas_call | solution.py:462
  (11 shorter events, 0.1 us)
Async XLA Ops:
  2.6 6.9 %collective-permute-start = (bf16[128,512]{1,0:T(8,128)(2,1)}, bf16[128,512]{1,0:T(8,128)(2,1)S(1)}, u32[]{:S(2)}, u32[]{:S(2)}) collective-permute-start(bf16[128,512]{1,0:T(8,128)(2,1)} %get-tuple-element.39), channel_id=1, source_target_pairs={{0,2},{1,3},{2,4},{3,5},{4,6},{5,7},{6,0},{7,1},{8,10},{9,11},{10,... | collective-permute-start | bytes 393224 | tf_op jit(solution)/shard_map/ppermute | solution.py:380
  4.3 9.1 %collective-permute-start.1 = (bf16[128,512]{1,0:T(8,128)(2,1)}, bf16[128,512]{1,0:T(8,128)(2,1)S(1)}, u32[]{:S(2)}, u32[]{:S(2)}) collective-permute-start(bf16[128,512]{1,0:T(8,128)(2,1)} %get-tuple-element.40), channel_id=1, source_target_pairs={{0,4},{1,5},{2,6},{3,7},{4,0},{5,1},{6,2},{7,3},{8,12},{9,13},{10,... | collective-permute-start | bytes 393224 | tf_op jit(solution)/shard_map/ppermute | solution.py:380
  7.2 6.2 %collective-permute-start.2 = (bf16[128,512]{1,0:T(8,128)(2,1)}, bf16[128,512]{1,0:T(8,128)(2,1)S(1)}, u32[]{:S(2)}, u32[]{:S(2)}) collective-permute-start(bf16[128,512]{1,0:T(8,128)(2,1)} %get-tuple-element.41), channel_id=1, source_target_pairs={{0,6},{1,7},{2,0},{3,1},{4,2},{5,3},{6,4},{7,5},{8,14},{9,15},{10,... | collective-permute-start | bytes 393224 | tf_op jit(solution)/shard_map/ppermute | solution.py:380
  9.5 1.2 %copy-start.1 = (bf16[128,4096]{1,0:T(8,128)(2,1)S(1)}, bf16[128,4096]{1,0:T(8,128)(2,1)}, u32[]{:S(2)}) copy-start(bf16[128,4096]{1,0:T(8,128)(2,1)} %q_ref.1) | copy-start | bytes 3145732
  10.7 1.2 %copy-start.2 = (bf16[128,4096]{1,0:T(8,128)(2,1)S(1)}, bf16[128,4096]{1,0:T(8,128)(2,1)}, u32[]{:S(2)}) copy-start(bf16[128,4096]{1,0:T(8,128)(2,1)} %g_ref.1) | copy-start | bytes 3145732
  11.9 1.5 %copy-start.3 = (bf16[128,512]{1,0:T(8,128)(2,1)S(1)}, bf16[128,512]{1,0:T(8,128)(2,1)}, u32[]{:S(2)}) copy-start(bf16[128,512]{1,0:T(8,128)(2,1)} %get-tuple-element.38.refs_0_) | copy-start | bytes 393220
  12.4 1.0 %copy-start = (bf16[4,128,1024]{2,1,0:T(8,128)(2,1)}, bf16[4,128,1024]{2,1,0:T(8,128)(2,1)S(1)}, u32[]{:S(2)}) copy-start(bf16[4,128,1024]{2,1,0:T(8,128)(2,1)S(1)} %get-tuple-element.48.refs_0_) | copy-start | bytes 3145732
  13.4 0.7 copy-start.6
  13.4 0.7 copy-start.7
  14.2 0.6 copy-start.4
  14.7 22.6 %all-to-all-start = ((bf16[4,128,1024]{2,1,0:T(8,128)(2,1)}), bf16[4,128,1024]{2,1,0:T(8,128)(2,1)S(1)}, u32[]{:S(2)}, u32[]{:S(2)}) async-start(bf16[4,128,1024]{2,1,0:T(8,128)(2,1)} %shard_map.121), calls=%async_computation | async-start | bytes 2097152 | tf_op jit(solution)/shard_map/all_to_all | solution.py:428
  20.7 9.2 %copy-start.8 = (s32[16,8]{0,1:T(8,128)S(1)}, s32[16,8]{0,1:T(8,128)}, u32[]{:S(2)}) copy-start(s32[16,8]{0,1:T(8,128)} %param.13) | copy-start | bytes 1540
  20.7 12.1 %collective-permute-start.3 = (bf16[512,512]{1,0:T(8,128)(2,1)S(1)}, bf16[512,512]{1,0:T(8,128)(2,1)S(1)}, u32[]{:S(2)}, u32[]{:S(2)}) collective-permute-start(bf16[512,512]{1,0:T(8,128)(2,1)S(1)} %get-tuple-element.43.refs_2_.kv_ref), channel_id=1, source_target_pairs={{0,1},{1,0},{2,3},{3,2},{4,5},{5,4},{6,7},{7,6},{8,9},{9,8},{10,11... | collective-permute-start | bytes 1572872 | tf_op jit(solution)/shard_map/ppermute | solution.py:390
  23.7 19.5 %collective-permute-start.4 = (bf16[128,1024]{1,0:T(8,128)(2,1)S(1)}, bf16[128,1024]{1,0:T(8,128)(2,1)S(1)}, u32[]{:S(2)}, u32[]{:S(2)}) collective-permute-start(bf16[128,1024]{1,0:T(8,128)(2,1)S(1)} %get-tuple-element.45), channel_id=1, source_target_pairs={{0,2},{1,3},{2,4},{3,5},{4,6},{5,7},{6,0},{7,1},{8,10},{9,11},{10,... | collective-permute-start | bytes 786440 | tf_op jit(solution)/shard_map/ppermute | solution.py:380
  25.7 18.5 %collective-permute-start.5 = (bf16[128,1024]{1,0:T(8,128)(2,1)S(1)}, bf16[128,1024]{1,0:T(8,128)(2,1)}, u32[]{:S(2)}, u32[]{:S(2)}) collective-permute-start(bf16[128,1024]{1,0:T(8,128)(2,1)S(1)} %get-tuple-element.46), channel_id=1, source_target_pairs={{0,4},{1,5},{2,6},{3,7},{4,0},{5,1},{6,2},{7,3},{8,12},{9,13},{10,... | collective-permute-start | bytes 786440 | tf_op jit(solution)/shard_map/ppermute | solution.py:380
  28.4 15.9 %collective-permute-start.6 = (bf16[128,1024]{1,0:T(8,128)(2,1)S(1)}, bf16[128,1024]{1,0:T(8,128)(2,1)}, u32[]{:S(2)}, u32[]{:S(2)}) collective-permute-start(bf16[128,1024]{1,0:T(8,128)(2,1)S(1)} %get-tuple-element.47), channel_id=1, source_target_pairs={{0,6},{1,7},{2,0},{3,1},{4,2},{5,3},{6,4},{7,5},{8,14},{9,15},{10,... | collective-permute-start | bytes 786440 | tf_op jit(solution)/shard_map/ppermute | solution.py:380
  29.9 7.4 %copy-start.5 = (f32[2,128]{1,0:T(2,128)S(1)}, f32[2,128]{1,0:T(2,128)}, u32[]{:S(2)}) copy-start(f32[2,128]{1,0:T(2,128)} %copy-done.4) | copy-start | bytes 3076
  51.1 21.5 %collective-permute-start.10 = (bf16[512,512]{1,0:T(8,128)(2,1)S(1)}, bf16[512,512]{1,0:T(8,128)(2,1)S(1)}, u32[]{:S(2)}, u32[]{:S(2)}) collective-permute-start(bf16[512,512]{1,0:T(8,128)(2,1)S(1)} %get-tuple-element.60), channel_id=1, source_target_pairs={{0,1},{1,0},{2,3},{3,2},{4,5},{5,4},{6,7},{7,6},{8,9},{9,8},{10,11... | collective-permute-start | bytes 1572872 | tf_op jit(solution)/shard_map/ppermute | solution.py:390
  54.0 22.2 %collective-permute-start.7 = (bf16[128,2048]{1,0:T(8,128)(2,1)S(1)}, bf16[128,2048]{1,0:T(8,128)(2,1)S(1)}, u32[]{:S(2)}, u32[]{:S(2)}) collective-permute-start(bf16[128,2048]{1,0:T(8,128)(2,1)S(1)} %get-tuple-element.54), channel_id=1, source_target_pairs={{0,2},{1,3},{2,4},{3,5},{4,6},{5,7},{6,0},{7,1},{8,10},{9,11},{10,... | collective-permute-start | bytes 1572872 | tf_op jit(solution)/shard_map/ppermute | solution.py:380
  54.3 23.0 %collective-permute-start.8 = (bf16[128,2048]{1,0:T(8,128)(2,1)S(1)}, bf16[128,2048]{1,0:T(8,128)(2,1)S(1)}, u32[]{:S(2)}, u32[]{:S(2)}) collective-permute-start(bf16[128,2048]{1,0:T(8,128)(2,1)S(1)} %get-tuple-element.55), channel_id=1, source_target_pairs={{0,4},{1,5},{2,6},{3,7},{4,0},{5,1},{6,2},{7,3},{8,12},{9,13},{10,... | collective-permute-start | bytes 1572872 | tf_op jit(solution)/shard_map/ppermute | solution.py:380
  57.4 19.9 %collective-permute-start.9 = (bf16[128,2048]{1,0:T(8,128)(2,1)S(1)}, bf16[128,2048]{1,0:T(8,128)(2,1)S(1)}, u32[]{:S(2)}, u32[]{:S(2)}) collective-permute-start(bf16[128,2048]{1,0:T(8,128)(2,1)S(1)} %get-tuple-element.56), channel_id=1, source_target_pairs={{0,6},{1,7},{2,0},{3,1},{4,2},{5,3},{6,4},{7,5},{8,14},{9,15},{10,... | collective-permute-start | bytes 1572872 | tf_op jit(solution)/shard_map/ppermute | solution.py:380
  73.2 10.0 %collective-permute-start.11 = (bf16[144,512]{1,0:T(8,128)(2,1)S(1)}, bf16[144,512]{1,0:T(8,128)(2,1)S(1)}, u32[]{:S(2)}, u32[]{:S(2)}) collective-permute-start(bf16[144,512]{1,0:T(8,128)(2,1)S(1)} %get-tuple-element.63), channel_id=1, source_target_pairs={{0,2},{1,3},{2,4},{3,5},{4,6},{5,7},{6,0},{7,1},{8,10},{9,11},{10,... | collective-permute-start | bytes 442376 | tf_op jit(solution)/shard_map/ppermute | solution.py:380
  74.5 8.7 %collective-permute-start.12 = (bf16[144,512]{1,0:T(8,128)(2,1)S(1)}, bf16[144,512]{1,0:T(8,128)(2,1)S(1)}, u32[]{:S(2)}, u32[]{:S(2)}) collective-permute-start(bf16[144,512]{1,0:T(8,128)(2,1)S(1)} %get-tuple-element.64), channel_id=1, source_target_pairs={{0,4},{1,5},{2,6},{3,7},{4,0},{5,1},{6,2},{7,3},{8,12},{9,13},{10,... | collective-permute-start | bytes 442376 | tf_op jit(solution)/shard_map/ppermute | solution.py:380
  76.2 7.6 %collective-permute-start.13 = (bf16[144,512]{1,0:T(8,128)(2,1)S(1)}, bf16[144,512]{1,0:T(8,128)(2,1)S(1)}, u32[]{:S(2)}, u32[]{:S(2)}) collective-permute-start(bf16[144,512]{1,0:T(8,128)(2,1)S(1)} %get-tuple-element.65), channel_id=1, source_target_pairs={{0,6},{1,7},{2,0},{3,1},{4,2},{5,3},{6,4},{7,5},{8,14},{9,15},{10,... | collective-permute-start | bytes 442376 | tf_op jit(solution)/shard_map/ppermute | solution.py:380

commit v3 on v2

--- a/solution.py
+++ b/solution.py
@@ -134,18 +134,16 @@
     lengths_ref, both_gains_ref, own_ref, far_ref = refs[:4]
     del refs[:4]
     if part == 0:
-        qg_ref, y_ref, far_out, own_out, gains_ref = refs[:5]
-        del refs[:5]
+        qg_ref = refs.pop(0)
+        arrived = [(j, qg_ref.at[j * BLK : (j + 1) * BLK]) for j in range(YS)]
     else:
-        pieces = refs[:YS]
-        y_before, far_before, own_before, gains_before = refs[YS : YS + 4]
-        del refs[: YS + 4]
-        outs = refs[:YS]
-        far_out, own_out, gains_ref = refs[YS : YS + 3]
-        del refs[: YS + 3]
-        qg_ref = refs.pop()
-        y_ref = refs.pop()
-    kn_ref, v_ref, dk_ref, dv_ref, unit_ref, inv_ref, qn_ref, g_ref, dq_ref = refs
+        arrived = [(behind(step), refs[step]) for step in range(YS)]
+        y_before = refs[YS : 2 * YS]
+        far_before, own_before, gains_before = refs[2 * YS : 2 * YS + 3]
+        del refs[: 2 * YS + 3]
+    outs = refs[:YS]
+    far_out, own_out, gains_ref = refs[YS : YS + 3]
+    kn_ref, v_ref, dk_ref, dv_ref, unit_ref, inv_ref, qn_ref, g_ref, dq_ref, out_ref = refs[YS + 3 :]
     replica = lax.axis_index("dp")
     column = lax.rem(lax.axis_index("head"), 2)
     q_gain = both_gains_ref[0:1, :]
@@ -159,21 +157,16 @@
             unit, _ = unit_of(ref[local, k_at])
             kn_ref[place, :] = (unit * k_gain).astype(BF16)
             v_ref[place, :] = ref[local, v_at]
-    if part > 0:
-        for step in range(YS):
-            qg_ref[block_rows(behind(step)), :] = pieces[step][...]
     dk_ref[...] = jnp.zeros_like(dk_ref)
     dv_ref[...] = jnp.zeros_like(dv_ref)
-    for h in range(GROUP):
-        unit, inverse = unit_of(qg_ref[:, h * HD : (h + 1) * HD])
-        unit_ref[h] = unit
-        inv_ref[h] = jnp.broadcast_to(inverse, unit.shape)
-        normed = (unit * q_gain).astype(BF16)
-        g = qg_ref[:, WIDTH + h * HD : WIDTH + (h + 1) * HD]
-        for j in range(YS):
-            to = slice(j * WIDTH + h * BLK, j * WIDTH + (h + 1) * BLK)
-            qn_ref[to, :] = normed[j * BLK : (j + 1) * BLK]
-            g_ref[to, :] = g[j * BLK : (j + 1) * BLK]
+    for j, piece in arrived:
+        for h in range(GROUP):
+            to = block_rows(j * GROUP + h)
+            unit, inverse = unit_of(piece[:, h * HD : (h + 1) * HD])
+            unit_ref[to, :] = unit
+            inv_ref[to, :] = jnp.broadcast_to(inverse, unit.shape)
+            qn_ref[to, :] = (unit * q_gain).astype(BF16)
+            g_ref[to, :] = piece[:, WIDTH + h * HD : WIDTH + (h + 1) * HD]
     ends = []
     total = jnp.int32(0)
     for d in range(lengths_ref.shape[1]):
@@ -230,13 +223,11 @@
             dscores = [
                 (w * (dw - d) * FACTOR).astype(BF16) for w, dw, d in zip(weights, dweights, delta)
             ]
-            for n, (j, _) in enumerate(blocks):
+            for n in range(len(blocks)):
                 dq_ref[rows[n], :] = dot(dscores[n], kn[n], (1, 0))
                 dv_ref[n, windows[n], :] += dot(rounded[n], g[n], (0, 0))
                 dk_ref[n, windows[n], :] += dot(dscores[n], qn[n], (0, 0))
-                here = block_rows(j)
-                for h in range(GROUP):
-                    y_ref[here, h * HD : (h + 1) * HD] = out[n][h * BLK : (h + 1) * BLK, :].astype(BF16)
+                out_ref[rows[n], :] = out[n].astype(BF16)
 
         for tiles in range(1, WINDOWS + 1):
 
@@ -250,13 +241,16 @@
 
     lax.fori_loop(0, YS // PAIR, pair, 0)
     q_sum = jnp.zeros((8, HD), F32)
-    for h in range(GROUP):
-        for j in range(YS):
-            local = slice(j * BLK, (j + 1) * BLK)
-            unit = unit_ref[h, local, :]
-            dq = dq_ref[j * WIDTH + h * BLK : j * WIDTH + (h + 1) * BLK, :]
-            back = norm_back(dq, unit, inv_ref[h, local, :], q_gain)
-            y_ref[local, WIDTH + h * HD : WIDTH + (h + 1) * HD] = back.astype(BF16)
+    for step in range(YS):
+        for h in range(GROUP):
+            turn = block_rows(ahead(step) * GROUP + h)
+            unit = unit_ref[turn, :]
+            dq = dq_ref[turn, :]
+            back = norm_back(dq, unit, inv_ref[turn, :], q_gain)
+            first = part * WIDTH + h * HD
+            outs[step][:, first : first + HD] = out_ref[turn, :]
+            first += (part + 1) * WIDTH
+            outs[step][:, first : first + HD] = back.astype(BF16)
             q_sum = q_sum + fold(dq * unit)
     k_sum = jnp.zeros((8, HD), F32)
     for j in range(YS):
@@ -283,10 +277,8 @@
     else:
         gains_ref[...] = jnp.broadcast_to((gains_before[...] + sums)[None], gains_ref.shape)
         for step in range(YS):
-            rows = block_rows(ahead(step))
-            for p, ref in enumerate((y_before, y_ref)):
-                outs[step][:, p * WIDTH : (p + 1) * WIDTH] = ref[rows, :WIDTH]
-                outs[step][:, (PARTS + p) * WIDTH : (PARTS + p + 1) * WIDTH] = ref[rows, WIDTH:]
+            outs[step][:, :WIDTH] = y_before[step][:, :WIDTH]
+            outs[step][:, PARTS * WIDTH : (PARTS + 1) * WIDTH] = y_before[step][:, WIDTH:]
 
 
 def attend(part, lengths, both_gains, own, far, pieces, before, others):
@@ -295,7 +287,7 @@
     half = own.shape[0]
     sums = [shape(half, 2 * PARTS * HD), shape(half, 2 * PARTS * HD, F32)]
     if part == 0:
-        out_shape = [shape(half, 2 * WIDTH), *sums, shape(2, HD, F32)]
+        out_shape = [shape(BLK, 2 * WIDTH)] * YS + [*sums, shape(2, HD, F32)]
     else:
         out_shape = [shape(BLK, 2 * PARTS * WIDTH)] * YS + sums
         out_shape += [jax.ShapeDtypeStruct((others, 2, HD), F32)]
@@ -304,14 +296,13 @@
         pltpu.VMEM((span, HD), BF16),
         pltpu.VMEM((PAIR, span, HD), F32),
         pltpu.VMEM((PAIR, span, HD), F32),
-        pltpu.VMEM((GROUP, half, HD), F32),
-        pltpu.VMEM((GROUP, half, HD), F32),
+        pltpu.VMEM((GROUP * half, HD), F32),
+        pltpu.VMEM((GROUP * half, HD), F32),
         pltpu.VMEM((GROUP * half, HD), BF16),
         pltpu.VMEM((GROUP * half, HD), BF16),
         pltpu.VMEM((GROUP * half, HD), F32),
     ]
-    if part > 0:
-        scratch += [pltpu.VMEM((half, 2 * WIDTH), BF16)] * 2
+    scratch += [pltpu.VMEM((GROUP * half, HD), BF16)]
     return pl.pallas_call(
         functools.partial(attend_kernel, part),
         out_shape=out_shape,

time: 85.7 us -> 85.9 us (level)
  starting transfers between devices: 31.9 us -> 33.5 us
  Pallas kernels: 18.4 us -> 17.1 us
    pallas_call x2, Pallas kernels: 12.7 us -> 11.3 us  [attend(): pl.pallas_call(functools.partial(attend_kernel, part), out_shape=out_shap...]
    ppermute x2, starting transfers between devices: 5.87 us -> 6.88 us  [over_x(): return lax.ppermute(x, 'head', [(i, i ^ 1) for i in range(2 * YS)])]
  transfers between devices with their start and end apart: 15 -> 15, of which waited for: 7 -> 7; matrix products, arithmetic and copies ran while one was open for 0% -> 0% of each run, Pallas kernels for 10% -> 9%
where the time goes in v3:
time: 85.9 us; the launch traced here: 84.8 us
  starting transfers between devices  33.5 us (39%)
  Pallas kernels  17.1 us (20%)
  waiting for transfers between devices  14.6 us (17%)
  blocking collectives  14.1 us (16%)
  local copies, waits for them, and re-layouts  4.72 us (5%)
  between operations  0.92 us (1%)
    ppermute x12, starting transfers between devices, over_y(): lax.ppermute(pieces[step], 'head', [(2 * y + c, 2 * ((y + step) % YS) + c...  20.7 us
    all_to_all x1, blocking collectives, on_device(): lax.all_to_all(gains, ('dp', 'head'), split_axis=0, concat_axis=0, tiled=...  14.1 us
    pallas_call x2, Pallas kernels, attend(): pl.pallas_call(functools.partial(attend_kernel, part), out_shape=out_shap...  11.3 us
    ppermute x12, waiting for transfers between devices, over_y(): lax.ppermute(pieces[step], 'head', [(2 * y + c, 2 * ((y + step) % YS) + c...  7.14 us
    ppermute x2, starting transfers between devices, over_x(): return lax.ppermute(x, 'head', [(i, i ^ 1) for i in range(2 * YS)])  6.88 us
    all_to_all x1, starting transfers between devices, on_device(): lax.all_to_all(soon, 'head', split_axis=0, concat_axis=0, tiled=True, axi...  5.93 us
    unnamed x19, local copies, waits for them, and re-layouts  4.72 us
    all_to_all x1, waiting for transfers between devices, on_device(): lax.all_to_all(soon, 'head', split_axis=0, concat_axis=0, tiled=True, axi...  4.59 us
  transfers between devices with their start and end apart: 15, of which 7 were waited for; matrix products, arithmetic and copies ran while one was open for 0% of the time, Pallas kernels for 9%

profile of v3, /device:TPU:0, one launch (start us, length us, event | category | flops | bytes accessed | tf_op | source)
XLA Modules:
  0.0 84.8 jit_solution(6433609308785904717)
XLA Ops:
  0.6 1.9 %shard_map.118 = (bf16[128,512]{1,0:T(8,128)(2,1)}, bf16[128,512]{1,0:T(8,128)(2,1)}, bf16[128,512]{1,0:T(8,128)(2,1)}, bf16[128,512]{1,0:T(8,128)(2,1)}) custom-call(bf16[128,1024]{1,0:T(8,128)(2,1)} %k_ref.1, bf16[128,1024]{1,0:T(8,128)(2,1)} %v_ref.1), custom_call_target="tpu_custom_call" | custom-call | tf_op jit(solution)/shard_map/pallas_call | solution.py:391
  2.6 1.7 %collective-permute-start = (bf16[128,512]{1,0:T(8,128)(2,1)}, bf16[128,512]{1,0:T(8,128)(2,1)S(1)}, u32[]{:S(2)}, u32[]{:S(2)}) collective-permute-start(bf16[128,512]{1,0:T(8,128)(2,1)} %get-tuple-element.42), channel_id=1, source_target_pairs={{0,2},{1,3},{2,4},{3,5},{4,6},{5,7},{6,0},{7,1},{8,10},{9,11},{10,... | collective-permute-start | bytes 393224 | tf_op jit(solution)/shard_map/ppermute | solution.py:371
  4.3 2.9 %collective-permute-start.1 = (bf16[128,512]{1,0:T(8,128)(2,1)}, bf16[128,512]{1,0:T(8,128)(2,1)S(1)}, u32[]{:S(2)}, u32[]{:S(2)}) collective-permute-start(bf16[128,512]{1,0:T(8,128)(2,1)} %get-tuple-element.43), channel_id=1, source_target_pairs={{0,4},{1,5},{2,6},{3,7},{4,0},{5,1},{6,2},{7,3},{8,12},{9,13},{10,... | collective-permute-start | bytes 393224 | tf_op jit(solution)/shard_map/ppermute | solution.py:371
  7.2 1.3 %collective-permute-start.2 = (bf16[128,512]{1,0:T(8,128)(2,1)}, bf16[128,512]{1,0:T(8,128)(2,1)S(1)}, u32[]{:S(2)}, u32[]{:S(2)}) collective-permute-start(bf16[128,512]{1,0:T(8,128)(2,1)} %get-tuple-element.44), channel_id=1, source_target_pairs={{0,6},{1,7},{2,0},{3,1},{4,2},{5,3},{6,4},{7,5},{8,14},{9,15},{10,... | collective-permute-start | bytes 393224 | tf_op jit(solution)/shard_map/ppermute | solution.py:371
  8.6 0.9 %collective-permute-done.refs_1_._ = bf16[128,512]{1,0:T(8,128)(2,1)S(1)} collective-permute-done((bf16[128,512]{1,0:T(8,128)(2,1)}, bf16[128,512]{1,0:T(8,128)(2,1)S(1)}, u32[]{:S(2)}, u32[]{:S(2)}) %collective-permute-start) | collective-permute-done | bytes 131104 | tf_op jit(solution)/shard_map/ppermute | solution.py:371
  9.5 1.2 %copy-done.1 = bf16[128,4096]{1,0:T(8,128)(2,1)S(1)} copy-done((bf16[128,4096]{1,0:T(8,128)(2,1)S(1)}, bf16[128,4096]{1,0:T(8,128)(2,1)}, u32[]{:S(2)}) %copy-start.1) | copy-done | bytes 1048600
  10.7 1.2 %copy-done.2 = bf16[128,4096]{1,0:T(8,128)(2,1)S(1)} copy-done((bf16[128,4096]{1,0:T(8,128)(2,1)S(1)}, bf16[128,4096]{1,0:T(8,128)(2,1)}, u32[]{:S(2)}) %copy-start.2) | copy-done | bytes 1048600
  11.9 0.5 shard_map.120
  12.4 0.0 copy-start
  12.4 1.0 %copy-done = bf16[4,128,1024]{2,1,0:T(8,128)(2,1)} copy-done((bf16[4,128,1024]{2,1,0:T(8,128)(2,1)}, bf16[4,128,1024]{2,1,0:T(8,128)(2,1)S(1)}, u32[]{:S(2)}) %copy-start) | copy-done | bytes 1048600
  13.4 0.1 collective-permute-done.1.refs_2_
  13.4 0.0 collective-permute-done.2.refs_3_
  13.4 0.0 copy-done.3
  13.5 0.6 copy-done.6
  14.1 0.0 copy-done.7
  14.2 0.0 copy-start.4
  14.2 0.6 copy-done.4
  14.7 5.9 %all-to-all-start = ((bf16[4,128,1024]{2,1,0:T(8,128)(2,1)}), bf16[4,128,1024]{2,1,0:T(8,128)(2,1)S(1)}, u32[]{:S(2)}, u32[]{:S(2)}) async-start(bf16[4,128,1024]{2,1,0:T(8,128)(2,1)} %shard_map.121), calls=%async_computation | async-start | bytes 2097152 | tf_op jit(solution)/shard_map/all_to_all | solution.py:419
  20.7 3.0 %collective-permute-start.3 = (bf16[512,512]{1,0:T(8,128)(2,1)S(1)}, bf16[512,512]{1,0:T(8,128)(2,1)S(1)}, u32[]{:S(2)}, u32[]{:S(2)}) collective-permute-start(bf16[512,512]{1,0:T(8,128)(2,1)S(1)} %get-tuple-element.46.refs_2_.kv_ref), channel_id=1, source_target_pairs={{0,1},{1,0},{2,3},{3,2},{4,5},{5,4},{6,7},{7,6},{8,9},{9,8},{10,11... | collective-permute-start | bytes 1572872 | tf_op jit(solution)/shard_map/ppermute | solution.py:381
  23.7 2.0 %collective-permute-start.4 = (bf16[128,1024]{1,0:T(8,128)(2,1)S(1)}, bf16[128,1024]{1,0:T(8,128)(2,1)S(1)}, u32[]{:S(2)}, u32[]{:S(2)}) collective-permute-start(bf16[128,1024]{1,0:T(8,128)(2,1)S(1)} %get-tuple-element.48), channel_id=1, source_target_pairs={{0,2},{1,3},{2,4},{3,5},{4,6},{5,7},{6,0},{7,1},{8,10},{9,11},{10,... | collective-permute-start | bytes 786440 | tf_op jit(solution)/shard_map/ppermute | solution.py:371
  25.7 2.7 %collective-permute-start.5 = (bf16[128,1024]{1,0:T(8,128)(2,1)S(1)}, bf16[128,1024]{1,0:T(8,128)(2,1)}, u32[]{:S(2)}, u32[]{:S(2)}) collective-permute-start(bf16[128,1024]{1,0:T(8,128)(2,1)S(1)} %get-tuple-element.49), channel_id=1, source_target_pairs={{0,4},{1,5},{2,6},{3,7},{4,0},{5,1},{6,2},{7,3},{8,12},{9,13},{10,... | collective-permute-start | bytes 786440 | tf_op jit(solution)/shard_map/ppermute | solution.py:371
  28.4 1.5 %collective-permute-start.6 = (bf16[128,1024]{1,0:T(8,128)(2,1)S(1)}, bf16[128,1024]{1,0:T(8,128)(2,1)}, u32[]{:S(2)}, u32[]{:S(2)}) collective-permute-start(bf16[128,1024]{1,0:T(8,128)(2,1)S(1)} %get-tuple-element.50), channel_id=1, source_target_pairs={{0,6},{1,7},{2,0},{3,1},{4,2},{5,3},{6,4},{7,5},{8,14},{9,15},{10,... | collective-permute-start | bytes 786440 | tf_op jit(solution)/shard_map/ppermute | solution.py:371
  29.9 0.1 copy.15.refs_0_
  29.9 2.8 %collective-permute-done.3.refs_3_ = bf16[512,512]{1,0:T(8,128)(2,1)S(1)} collective-permute-done((bf16[512,512]{1,0:T(8,128)(2,1)S(1)}, bf16[512,512]{1,0:T(8,128)(2,1)S(1)}, u32[]{:S(2)}, u32[]{:S(2)}) %collective-permute-start.3) | collective-permute-done | bytes 524320 | tf_op jit(solution)/shard_map/ppermute | solution.py:381
  32.8 4.6 %all-to-all-done = bf16[4,128,1024]{2,1,0:T(8,128)(2,1)S(1)} async-done(((bf16[4,128,1024]{2,1,0:T(8,128)(2,1)}), bf16[4,128,1024]{2,1,0:T(8,128)(2,1)S(1)}, u32[]{:S(2)}, u32[]{:S(2)}) %all-to-all-start) | async-done | bytes 1048608 | tf_op jit(solution)/shard_map/all_to_all | solution.py:419
  37.3 5.3 %shard_map.122 = (bf16[128,1024]{1,0:T(8,128)(2,1)S(1)}, bf16[128,1024]{1,0:T(8,128)(2,1)S(1)}, bf16[128,1024]{1,0:T(8,128)(2,1)S(1)}, bf16[128,1024]{1,0:T(8,12...) custom-call(s32[16,8]{1,0:T(8,128)S(1)} %copy.15.refs_0_, ...), custom_call_target="tpu_custom_call" | custom-call | flops 2013265920 | bytes 4194304 | tf_op jit(solution)/shard_map/pallas_call | solution.py:306
  42.6 0.0 collective-permute-done.4.refs_5_
  42.6 1.6 %collective-permute-done.5.refs_6_ = bf16[128,1024]{1,0:T(8,128)(2,1)} collective-permute-done((bf16[128,1024]{1,0:T(8,128)(2,1)S(1)}, bf16[128,1024]{1,0:T(8,128)(2,1)}, u32[]{:S(2)}, u32[]{:S(2)}) %collective-permute-start.5) | collective-permute-done | bytes 262176 | tf_op jit(solution)/shard_map/ppermute | solution.py:371
  44.3 0.0 collective-permute-done.6.refs_7_
  44.3 6.0 %shard_map.123 = (bf16[128,2048]{1,0:T(8,128)(2,1)S(1)}, bf16[128,2048]{1,0:T(8,128)(2,1)S(1)}, bf16[128,2048]{1,0:T(8,128)(2,1)S(1)}, bf16[128,2048]{1,0:T(8,12...) custom-call(s32[16,8]{1,0:T(8,128)S(1)} %copy.15.refs_0_, ...), custom_call_target="tpu_custom_call" | custom-call | flops 2013265920 | bytes 4194304 | tf_op jit(solution)/shard_map/pallas_call | solution.py:306
  50.3 3.9 %collective-permute-start.10 = (bf16[512,512]{1,0:T(8,128)(2,1)S(1)}, bf16[512,512]{1,0:T(8,128)(2,1)S(1)}, u32[]{:S(2)}, u32[]{:S(2)}) collective-permute-start(bf16[512,512]{1,0:T(8,128)(2,1)S(1)} %get-tuple-element.66), channel_id=1, source_target_pairs={{0,1},{1,0},{2,3},{3,2},{4,5},{5,4},{6,7},{7,6},{8,9},{9,8},{10,11... | collective-permute-start | bytes 1572872 | tf_op jit(solution)/shard_map/ppermute | solution.py:381
  54.2 0.8 collective-permute-start.7
  55.0 3.1 %collective-permute-start.8 = (bf16[128,2048]{1,0:T(8,128)(2,1)S(1)}, bf16[128,2048]{1,0:T(8,128)(2,1)S(1)}, u32[]{:S(2)}, u32[]{:S(2)}) collective-permute-start(bf16[128,2048]{1,0:T(8,128)(2,1)S(1)} %get-tuple-element.61), channel_id=1, source_target_pairs={{0,4},{1,5},{2,6},{3,7},{4,0},{5,1},{6,2},{7,3},{8,12},{9,13},{10,... | collective-permute-start | bytes 1572872 | tf_op jit(solution)/shard_map/ppermute | solution.py:371
  58.1 0.0 collective-permute-start.9
  58.1 14.1 %all_to_all.10.gains_ref = f32[32,2,128]{2,1,0:T(2,128)S(1)} all-to-all(f32[32,2,128]{2,1,0:T(2,128)S(1)} %get-tuple-element.67), channel_id=1, replica_groups={{0,1,8,9,16,17,24,25,32,33,40,41,48,49,56,57,64,65,72,73,80,81,88,89,96..., dimensions={0} | all-to-all | bytes 65536 | tf_op jit(solution)/shard_map/all_to_all | solution.py:431
  72.2 0.0 collective-permute-done.10.far_ref
  72.2 0.5 shard_map.125
  72.7 1.9 %collective-permute-start.11 = (bf16[144,512]{1,0:T(8,128)(2,1)S(1)}, bf16[144,512]{1,0:T(8,128)(2,1)S(1)}, u32[]{:S(2)}, u32[]{:S(2)}) collective-permute-start(bf16[144,512]{1,0:T(8,128)(2,1)S(1)} %get-tuple-element.69), channel_id=1, source_target_pairs={{0,2},{1,3},{2,4},{3,5},{4,6},{5,7},{6,0},{7,1},{8,10},{9,11},{10,... | collective-permute-start | bytes 442376 | tf_op jit(solution)/shard_map/ppermute | solution.py:371
  74.6 1.1 %collective-permute-start.12 = (bf16[144,512]{1,0:T(8,128)(2,1)S(1)}, bf16[144,512]{1,0:T(8,128)(2,1)S(1)}, u32[]{:S(2)}, u32[]{:S(2)}) collective-permute-start(bf16[144,512]{1,0:T(8,128)(2,1)S(1)} %get-tuple-element.70), channel_id=1, source_target_pairs={{0,4},{1,5},{2,6},{3,7},{4,0},{5,1},{6,2},{7,3},{8,12},{9,13},{10,... | collective-permute-start | bytes 442376 | tf_op jit(solution)/shard_map/ppermute | solution.py:371
  75.7 0.0 collective-permute-done.7.refs_1_
  75.7 1.7 %collective-permute-start.13 = (bf16[144,512]{1,0:T(8,128)(2,1)S(1)}, bf16[144,512]{1,0:T(8,128)(2,1)S(1)}, u32[]{:S(2)}, u32[]{:S(2)}) collective-permute-start(bf16[144,512]{1,0:T(8,128)(2,1)S(1)} %get-tuple-element.71), channel_id=1, source_target_pairs={{0,6},{1,7},{2,0},{3,1},{4,2},{5,3},{6,4},{7,5},{8,14},{9,15},{10,... | collective-permute-start | bytes 442376 | tf_op jit(solution)/shard_map/ppermute | solution.py:371
  77.3 0.0 collective-permute-done.8.refs_2_
  77.3 0.0 collective-permute-done.9.refs_3_
  77.3 1.4 %shard_map.124 = (bf16[128,4096]{1,0:T(8,128)(2,1)}, bf16[128,4096]{1,0:T(8,128)(2,1)}) custom-call(bf16[128,2048]{1,0:T(8,128)(2,1)S(1)} %get-tuple-element.59.refs_0_, bf16[128,2048]{1,0:T(8,128)(2,1)S(1)} %collective-permute-done.7.refs_1_, bf16[128,2048]{1,0:T(8,128)(2,1)S(1)} %collective-permute-done.8.refs_2_, ...), custom_call_target="tpu_custom_call" | custom-call | tf_op jit(solution)/shard_map/pallas_call | solution.py:443
  78.7 4.2 %collective-permute-done.11.refs_1_ = bf16[144,512]{1,0:T(8,128)(2,1)S(1)} collective-permute-done((bf16[144,512]{1,0:T(8,128)(2,1)S(1)}, bf16[144,512]{1,0:T(8,128)(2,1)S(1)}, u32[]{:S(2)}, u32[]{:S(2)}) %collective-permute-start.11) | collective-permute-done | bytes 147488 | tf_op jit(solution)/shard_map/ppermute | solution.py:371
  82.9 0.0 collective-permute-done.12.refs_2_
  82.9 0.3 collective-permute-done.13.refs_3_
  83.3 1.4 %shard_map.126 = (bf16[128,1024]{1,0:T(8,128)(2,1)}, bf16[128,1024]{1,0:T(8,128)(2,1)}, f32[1,128]{1,0:T(1,128)}, f32[1,128]{1,0:T(1,128)}) custom-call(bf16[144,512]{1,0:T(8,128)(2,1)S(1)} %get-tuple-element.68.refs_0_, bf16[144,512]{1,0:T(8,128)(2,1)S(1)} %collective-permute-done.11.refs_1_, bf16[144,512]{1,0:T(8,128)(2,1)S(1)} %collective-permute-done.12.refs_2_, ...), custom_call_target="tpu_custom_call" | custom-call | tf_op jit(solution)/shard_map/pallas_call | solution.py:453
  (11 shorter events, 0.1 us)
Async XLA Ops:
  2.6 6.9 %collective-permute-start = (bf16[128,512]{1,0:T(8,128)(2,1)}, bf16[128,512]{1,0:T(8,128)(2,1)S(1)}, u32[]{:S(2)}, u32[]{:S(2)}) collective-permute-start(bf16[128,512]{1,0:T(8,128)(2,1)} %get-tuple-element.42), channel_id=1, source_target_pairs={{0,2},{1,3},{2,4},{3,5},{4,6},{5,7},{6,0},{7,1},{8,10},{9,11},{10,... | collective-permute-start | bytes 393224 | tf_op jit(solution)/shard_map/ppermute | solution.py:371
  4.3 9.1 %collective-permute-start.1 = (bf16[128,512]{1,0:T(8,128)(2,1)}, bf16[128,512]{1,0:T(8,128)(2,1)S(1)}, u32[]{:S(2)}, u32[]{:S(2)}) collective-permute-start(bf16[128,512]{1,0:T(8,128)(2,1)} %get-tuple-element.43), channel_id=1, source_target_pairs={{0,4},{1,5},{2,6},{3,7},{4,0},{5,1},{6,2},{7,3},{8,12},{9,13},{10,... | collective-permute-start | bytes 393224 | tf_op jit(solution)/shard_map/ppermute | solution.py:371
  7.2 6.2 %collective-permute-start.2 = (bf16[128,512]{1,0:T(8,128)(2,1)}, bf16[128,512]{1,0:T(8,128)(2,1)S(1)}, u32[]{:S(2)}, u32[]{:S(2)}) collective-permute-start(bf16[128,512]{1,0:T(8,128)(2,1)} %get-tuple-element.44), channel_id=1, source_target_pairs={{0,6},{1,7},{2,0},{3,1},{4,2},{5,3},{6,4},{7,5},{8,14},{9,15},{10,... | collective-permute-start | bytes 393224 | tf_op jit(solution)/shard_map/ppermute | solution.py:371
  9.5 1.2 %copy-start.1 = (bf16[128,4096]{1,0:T(8,128)(2,1)S(1)}, bf16[128,4096]{1,0:T(8,128)(2,1)}, u32[]{:S(2)}) copy-start(bf16[128,4096]{1,0:T(8,128)(2,1)} %q_ref.1) | copy-start | bytes 3145732
  10.7 1.2 %copy-start.2 = (bf16[128,4096]{1,0:T(8,128)(2,1)S(1)}, bf16[128,4096]{1,0:T(8,128)(2,1)}, u32[]{:S(2)}) copy-start(bf16[128,4096]{1,0:T(8,128)(2,1)} %g_ref.1) | copy-start | bytes 3145732
  11.9 1.5 %copy-start.3 = (bf16[128,512]{1,0:T(8,128)(2,1)S(1)}, bf16[128,512]{1,0:T(8,128)(2,1)}, u32[]{:S(2)}) copy-start(bf16[128,512]{1,0:T(8,128)(2,1)} %get-tuple-element.41.refs_0_) | copy-start | bytes 393220
  12.4 1.0 %copy-start = (bf16[4,128,1024]{2,1,0:T(8,128)(2,1)}, bf16[4,128,1024]{2,1,0:T(8,128)(2,1)S(1)}, u32[]{:S(2)}) copy-start(bf16[4,128,1024]{2,1,0:T(8,128)(2,1)S(1)} %get-tuple-element.51.refs_0_) | copy-start | bytes 3145732
  13.4 0.7 copy-start.6
  13.4 0.7 copy-start.7
  14.2 0.6 copy-start.4
  14.7 22.6 %all-to-all-start = ((bf16[4,128,1024]{2,1,0:T(8,128)(2,1)}), bf16[4,128,1024]{2,1,0:T(8,128)(2,1)S(1)}, u32[]{:S(2)}, u32[]{:S(2)}) async-start(bf16[4,128,1024]{2,1,0:T(8,128)(2,1)} %shard_map.121), calls=%async_computation | async-start | bytes 2097152 | tf_op jit(solution)/shard_map/all_to_all | solution.py:419
  20.7 9.2 %copy-start.8 = (s32[16,8]{0,1:T(8,128)S(1)}, s32[16,8]{0,1:T(8,128)}, u32[]{:S(2)}) copy-start(s32[16,8]{0,1:T(8,128)} %param.13) | copy-start | bytes 1540
  20.7 12.1 %collective-permute-start.3 = (bf16[512,512]{1,0:T(8,128)(2,1)S(1)}, bf16[512,512]{1,0:T(8,128)(2,1)S(1)}, u32[]{:S(2)}, u32[]{:S(2)}) collective-permute-start(bf16[512,512]{1,0:T(8,128)(2,1)S(1)} %get-tuple-element.46.refs_2_.kv_ref), channel_id=1, source_target_pairs={{0,1},{1,0},{2,3},{3,2},{4,5},{5,4},{6,7},{7,6},{8,9},{9,8},{10,11... | collective-permute-start | bytes 1572872 | tf_op jit(solution)/shard_map/ppermute | solution.py:381
  23.7 18.9 %collective-permute-start.4 = (bf16[128,1024]{1,0:T(8,128)(2,1)S(1)}, bf16[128,1024]{1,0:T(8,128)(2,1)S(1)}, u32[]{:S(2)}, u32[]{:S(2)}) collective-permute-start(bf16[128,1024]{1,0:T(8,128)(2,1)S(1)} %get-tuple-element.48), channel_id=1, source_target_pairs={{0,2},{1,3},{2,4},{3,5},{4,6},{5,7},{6,0},{7,1},{8,10},{9,11},{10,... | collective-permute-start | bytes 786440 | tf_op jit(solution)/shard_map/ppermute | solution.py:371
  25.7 18.5 %collective-permute-start.5 = (bf16[128,1024]{1,0:T(8,128)(2,1)S(1)}, bf16[128,1024]{1,0:T(8,128)(2,1)}, u32[]{:S(2)}, u32[]{:S(2)}) collective-permute-start(bf16[128,1024]{1,0:T(8,128)(2,1)S(1)} %get-tuple-element.49), channel_id=1, source_target_pairs={{0,4},{1,5},{2,6},{3,7},{4,0},{5,1},{6,2},{7,3},{8,12},{9,13},{10,... | collective-permute-start | bytes 786440 | tf_op jit(solution)/shard_map/ppermute | solution.py:371
  28.4 15.9 %collective-permute-start.6 = (bf16[128,1024]{1,0:T(8,128)(2,1)S(1)}, bf16[128,1024]{1,0:T(8,128)(2,1)}, u32[]{:S(2)}, u32[]{:S(2)}) collective-permute-start(bf16[128,1024]{1,0:T(8,128)(2,1)S(1)} %get-tuple-element.50), channel_id=1, source_target_pairs={{0,6},{1,7},{2,0},{3,1},{4,2},{5,3},{6,4},{7,5},{8,14},{9,15},{10,... | collective-permute-start | bytes 786440 | tf_op jit(solution)/shard_map/ppermute | solution.py:371
  29.9 7.4 %copy-start.5 = (f32[2,128]{1,0:T(2,128)S(1)}, f32[2,128]{1,0:T(2,128)}, u32[]{:S(2)}) copy-start(f32[2,128]{1,0:T(2,128)} %copy-done.4) | copy-start | bytes 3076
  50.3 21.9 %collective-permute-start.10 = (bf16[512,512]{1,0:T(8,128)(2,1)S(1)}, bf16[512,512]{1,0:T(8,128)(2,1)S(1)}, u32[]{:S(2)}, u32[]{:S(2)}) collective-permute-start(bf16[512,512]{1,0:T(8,128)(2,1)S(1)} %get-tuple-element.66), channel_id=1, source_target_pairs={{0,1},{1,0},{2,3},{3,2},{4,5},{5,4},{6,7},{7,6},{8,9},{9,8},{10,11... | collective-permute-start | bytes 1572872 | tf_op jit(solution)/shard_map/ppermute | solution.py:381
  54.2 21.5 %collective-permute-start.7 = (bf16[128,2048]{1,0:T(8,128)(2,1)S(1)}, bf16[128,2048]{1,0:T(8,128)(2,1)S(1)}, u32[]{:S(2)}, u32[]{:S(2)}) collective-permute-start(bf16[128,2048]{1,0:T(8,128)(2,1)S(1)} %get-tuple-element.60), channel_id=1, source_target_pairs={{0,2},{1,3},{2,4},{3,5},{4,6},{5,7},{6,0},{7,1},{8,10},{9,11},{10,... | collective-permute-start | bytes 1572872 | tf_op jit(solution)/shard_map/ppermute | solution.py:371
  55.0 22.4 %collective-permute-start.8 = (bf16[128,2048]{1,0:T(8,128)(2,1)S(1)}, bf16[128,2048]{1,0:T(8,128)(2,1)S(1)}, u32[]{:S(2)}, u32[]{:S(2)}) collective-permute-start(bf16[128,2048]{1,0:T(8,128)(2,1)S(1)} %get-tuple-element.61), channel_id=1, source_target_pairs={{0,4},{1,5},{2,6},{3,7},{4,0},{5,1},{6,2},{7,3},{8,12},{9,13},{10,... | collective-permute-start | bytes 1572872 | tf_op jit(solution)/shard_map/ppermute | solution.py:371
  58.1 19.3 %collective-permute-start.9 = (bf16[128,2048]{1,0:T(8,128)(2,1)S(1)}, bf16[128,2048]{1,0:T(8,128)(2,1)S(1)}, u32[]{:S(2)}, u32[]{:S(2)}) collective-permute-start(bf16[128,2048]{1,0:T(8,128)(2,1)S(1)} %get-tuple-element.62), channel_id=1, source_target_pairs={{0,6},{1,7},{2,0},{3,1},{4,2},{5,3},{6,4},{7,5},{8,14},{9,15},{10,... | collective-permute-start | bytes 1572872 | tf_op jit(solution)/shard_map/ppermute | solution.py:371
  72.7 10.2 %collective-permute-start.11 = (bf16[144,512]{1,0:T(8,128)(2,1)S(1)}, bf16[144,512]{1,0:T(8,128)(2,1)S(1)}, u32[]{:S(2)}, u32[]{:S(2)}) collective-permute-start(bf16[144,512]{1,0:T(8,128)(2,1)S(1)} %get-tuple-element.69), channel_id=1, source_target_pairs={{0,2},{1,3},{2,4},{3,5},{4,6},{5,7},{6,0},{7,1},{8,10},{9,11},{10,... | collective-permute-start | bytes 442376 | tf_op jit(solution)/shard_map/ppermute | solution.py:371
  74.6 8.4 %collective-permute-start.12 = (bf16[144,512]{1,0:T(8,128)(2,1)S(1)}, bf16[144,512]{1,0:T(8,128)(2,1)S(1)}, u32[]{:S(2)}, u32[]{:S(2)}) collective-permute-start(bf16[144,512]{1,0:T(8,128)(2,1)S(1)} %get-tuple-element.70), channel_id=1, source_target_pairs={{0,4},{1,5},{2,6},{3,7},{4,0},{5,1},{6,2},{7,3},{8,12},{9,13},{10,... | collective-permute-start | bytes 442376 | tf_op jit(solution)/shard_map/ppermute | solution.py:371
  75.7 7.6 %collective-permute-start.13 = (bf16[144,512]{1,0:T(8,128)(2,1)S(1)}, bf16[144,512]{1,0:T(8,128)(2,1)S(1)}, u32[]{:S(2)}, u32[]{:S(2)}) collective-permute-start(bf16[144,512]{1,0:T(8,128)(2,1)S(1)} %get-tuple-element.71), channel_id=1, source_target_pairs={{0,6},{1,7},{2,0},{3,1},{4,2},{5,3},{6,4},{7,5},{8,14},{9,15},{10,... | collective-permute-start | bytes 442376 | tf_op jit(solution)/shard_map/ppermute | solution.py:371

commit v4 on v3

--- a/solution.py
+++ b/solution.py
@@ -59,11 +59,15 @@
     return pl.ds(pl.multiple_of(index * BLK, BLK), BLK)
 
 
-def do_copies(moves, sems):
+def start_copies(moves, sems):
     started = [pltpu.make_async_copy(a, b, sems.at[i]) for i, (a, b) in enumerate(moves)]
     for move in started:
         move.start()
-    for move in started:
+    return started
+
+
+def do_copies(moves, sems):
+    for move in start_copies(moves, sems):
         move.wait()
 
 
@@ -139,8 +143,8 @@
     else:
         arrived = [(behind(step), refs[step]) for step in range(YS)]
         y_before = refs[YS : 2 * YS]
-        far_before, own_before, gains_before = refs[2 * YS : 2 * YS + 3]
-        del refs[: 2 * YS + 3]
+        far_before, gains_before = refs[2 * YS : 2 * YS + 2]
+        del refs[: 2 * YS + 2]
     outs = refs[:YS]
     far_out, own_out, gains_ref = refs[YS : YS + 3]
     kn_ref, v_ref, dk_ref, dv_ref, unit_ref, inv_ref, qn_ref, g_ref, dq_ref, out_ref = refs[YS + 3 :]
@@ -261,14 +265,15 @@
             dk = sum(dk_ref[n, place, :] for n in range(PAIR))
             dv = sum(dv_ref[n, place, :] for n in range(PAIR))
             k_sum = k_sum + fold(dk * unit)
-            target = own_out if ref is own_ref else far_out
-            target[local, k_at] = dk.astype(target.dtype)
-            target[local, v_at] = dv.astype(target.dtype)
+            if ref is own_ref:
+                own_out[local, :HD] = dk
+                own_out[local, HD:] = dv
+            else:
+                far_out[local, k_at] = dk.astype(BF16)
+                far_out[local, v_at] = dv.astype(BF16)
     if part > 0:
-        for before, target in ((far_before, far_out), (own_before, own_out)):
-            for p in range(part):
-                for at in (p, PARTS + p):
-                    target[:, at * HD : (at + 1) * HD] = before[:, at * HD : (at + 1) * HD]
+        for at in range(0, 2 * PARTS, PARTS):
+            far_out[:, at * HD : (at + 1) * HD] = far_before[:, at * HD : (at + 1) * HD]
     sums = jnp.concatenate(
         [jnp.sum(q_sum, axis=0, keepdims=True), jnp.sum(k_sum, axis=0, keepdims=True)], axis=0
     )
@@ -285,7 +290,7 @@
     span = 2 * YS * BLK
     args = [lengths, both_gains, own, far, *pieces, *before]
     half = own.shape[0]
-    sums = [shape(half, 2 * PARTS * HD), shape(half, 2 * PARTS * HD, F32)]
+    sums = [shape(half, 2 * PARTS * HD), shape(half, 2 * HD, F32)]
     if part == 0:
         out_shape = [shape(BLK, 2 * WIDTH)] * YS + [*sums, shape(2, HD, F32)]
     else:
@@ -316,7 +321,8 @@
     )(*args)
 
 
-def finish_kv_kernel(both_gains_ref, kv_ref, own_ref, far_ref, gains_ref, *refs):
+def finish_kv_kernel(both_gains_ref, kv_ref, *refs):
+    own, far_ref, gains_ref, refs = refs[:PARTS], refs[PARTS], refs[PARTS + 1], refs[PARTS + 2 :]
     outs = refs[:YS]
     y_ref = refs[YS]
     k_gain = both_gains_ref[1:2, :]
@@ -324,9 +330,9 @@
         k_at = slice(p * HD, (p + 1) * HD)
         v_at = slice((PARTS + p) * HD, (PARTS + p + 1) * HD)
         unit, inverse = unit_of(kv_ref[:, k_at])
-        dk = own_ref[:, k_at] + far_ref[:, k_at].astype(F32)
+        dk = own[p][:, :HD] + far_ref[:, k_at].astype(F32)
         y_ref[:, k_at] = norm_back(dk, unit, inverse, k_gain).astype(BF16)
-        y_ref[:, v_at] = (own_ref[:, v_at] + far_ref[:, v_at].astype(F32)).astype(BF16)
+        y_ref[:, v_at] = (own[p][:, HD:] + far_ref[:, v_at].astype(F32)).astype(BF16)
     rest = jnp.concatenate([jnp.sum(gains_ref[...], axis=0), jnp.zeros((TAIL - 2, HD), F32)], axis=0)
     for step in range(YS):
         outs[step][:BLK, :] = y_ref[block_rows(ahead(step)), :]
@@ -354,6 +360,7 @@
 def unpack_kv_kernel(scales, *refs):
     pieces = refs[:YS]
     dk_ref, dv_ref, q_ref, k_ref, sums_ref, sems = refs[YS:]
+    started = start_copies(unpack_moves(PARTS * HD, pieces, (dk_ref, dv_ref)), sems)
     for step in range(YS):
         tail = pieces[step][BLK:, :].astype(F32)
         whole = (tail[:, :HD] + tail[:, HD : 2 * HD]) + tail[:, 2 * HD : 3 * HD]
@@ -361,7 +368,8 @@
     total = (sums_ref[0] + sums_ref[1]) + (sums_ref[2] + sums_ref[3])
     q_ref[...] = total[0:1] * scales[0]
     k_ref[...] = total[1:2] * scales[1]
-    do_copies(unpack_moves(PARTS * HD, pieces, (dk_ref, dv_ref)), sems)
+    for move in started:
+        move.wait()
 
 
 def over_y(pieces):
@@ -420,11 +428,13 @@
     qg_parts = [[soon.reshape(half, 2 * WIDTH)], qg_moved]
 
     before = ()
+    own_sums = []
     for part in range(PARTS):
-        before = attend(
+        *outs, far_sum, own_sum, gains = attend(
             part, doc_lengths, both_gains, own, far, qg_parts[part], before, 2 * replicas
         )
-    *outs, far_sum, own_sum, gains = before
+        before = (*outs, far_sum, gains)
+        own_sums.append(own_sum)
     far_back = over_x(far_sum)
     outs = over_y(outs)
     same_y = [[d * members + 2 * y + c for d in range(replicas) for c in range(2)] for y in range(YS)]
@@ -434,11 +444,11 @@
     kv_back = pl.pallas_call(
         finish_kv_kernel,
         out_shape=[shape(rows + TAIL, wide)] * YS,
-        in_specs=specs([VMEM] * 5),
+        in_specs=specs([VMEM] * (4 + PARTS)),
         out_specs=specs([VMEM] * YS),
         scratch_shapes=[pltpu.VMEM((half, wide), BF16)],
         compiler_params=LIMIT,
-    )(both_gains, own, own_sum, far_back, gains)
+    )(both_gains, own, *own_sums, far_back, gains)
     kv_back = over_y(kv_back)
     out, dq = pl.pallas_call(
         unpack_qg_kernel,

time: 85.9 us -> 86 us (level); the launches traced: 84.8 us -> 85.9 us
  starting transfers between devices: 33.5 us -> 31.1 us
  blocking collectives: 14.1 us -> 15.8 us
  Pallas kernels: 17.1 us -> 18.7 us
    pallas_call x2, Pallas kernels: 11.3 us -> 13 us  [attend(): pl.pallas_call(functools.partial(attend_kernel, part), out_shape=out_shap...]
    all_to_all x1, blocking collectives: 14.1 us -> 15.8 us  [on_device(): lax.all_to_all(gains, ('dp', 'head'), split_axis=0, concat_axis=0, tiled=...]
    ppermute x2, starting transfers between devices: 6.88 us -> 5.59 us  [over_x(): return lax.ppermute(x, 'head', [(i, i ^ 1) for i in range(2 * YS)])]
    ppermute x12, starting transfers between devices: 20.7 us -> 19.6 us  [over_y(): lax.ppermute(pieces[step], 'head', [(2 * y + c, 2 * ((y + step) % YS) + c...]
  transfers between devices with their start and end apart: 15 -> 15, of which waited for: 7 -> 7; matrix products, arithmetic and copies ran while one was open for 0% -> 0% of each run, Pallas kernels for 9% -> 10%
where the time goes in v4:
time: 86 us; the launch traced here: 85.9 us
  starting transfers between devices  31.1 us (36%)
  Pallas kernels  18.7 us (22%)
  blocking collectives  15.8 us (18%)
  waiting for transfers between devices  14.6 us (17%)
  local copies, waits for them, and re-layouts  4.72 us (5%)
  between operations  0.92 us (1%)
    ppermute x12, starting transfers between devices, over_y(): lax.ppermute(pieces[step], 'head', [(2 * y + c, 2 * ((y + step) % YS) + c...  19.6 us
    all_to_all x1, blocking collectives, on_device(): lax.all_to_all(gains, ('dp', 'head'), split_axis=0, concat_axis=0, tiled=...  15.8 us
    pallas_call x2, Pallas kernels, attend(): pl.pallas_call(functools.partial(attend_kernel, part), out_shape=out_shap...  13 us
    ppermute x12, waiting for transfers between devices, over_y(): lax.ppermute(pieces[step], 'head', [(2 * y + c, 2 * ((y + step) % YS) + c...  7.23 us
    all_to_all x1, starting transfers between devices, on_device(): lax.all_to_all(soon, 'head', split_axis=0, concat_axis=0, tiled=True, axi...  5.93 us
    ppermute x2, starting transfers between devices, over_x(): return lax.ppermute(x, 'head', [(i, i ^ 1) for i in range(2 * YS)])  5.59 us
    unnamed x19, local copies, waits for them, and re-layouts  4.72 us
    all_to_all x1, waiting for transfers between devices, on_device(): lax.all_to_all(soon, 'head', split_axis=0, concat_axis=0, tiled=True, axi...  4.59 us
  transfers between devices with their start and end apart: 15, of which 7 were waited for; matrix products, arithmetic and copies ran while one was open for 0% of the time, Pallas kernels for 10%

profile of v4, /device:TPU:0, one launch (start us, length us, event | category | flops | bytes accessed | tf_op | source)
XLA Modules:
  0.0 85.9 jit_solution(7508187892340354346)
XLA Ops:
  0.6 1.9 %shard_map.118 = (bf16[128,512]{1,0:T(8,128)(2,1)}, bf16[128,512]{1,0:T(8,128)(2,1)}, bf16[128,512]{1,0:T(8,128)(2,1)}, bf16[128,512]{1,0:T(8,128)(2,1)}) custom-call(bf16[128,1024]{1,0:T(8,128)(2,1)} %k_ref.1, bf16[128,1024]{1,0:T(8,128)(2,1)} %v_ref.1), custom_call_target="tpu_custom_call" | custom-call | tf_op jit(solution)/shard_map/pallas_call | solution.py:399
  2.6 1.7 %collective-permute-start = (bf16[128,512]{1,0:T(8,128)(2,1)}, bf16[128,512]{1,0:T(8,128)(2,1)S(1)}, u32[]{:S(2)}, u32[]{:S(2)}) collective-permute-start(bf16[128,512]{1,0:T(8,128)(2,1)} %get-tuple-element.42), channel_id=1, source_target_pairs={{0,2},{1,3},{2,4},{3,5},{4,6},{5,7},{6,0},{7,1},{8,10},{9,11},{10,... | collective-permute-start | bytes 393224 | tf_op jit(solution)/shard_map/ppermute | solution.py:379
  4.3 2.9 %collective-permute-start.1 = (bf16[128,512]{1,0:T(8,128)(2,1)}, bf16[128,512]{1,0:T(8,128)(2,1)S(1)}, u32[]{:S(2)}, u32[]{:S(2)}) collective-permute-start(bf16[128,512]{1,0:T(8,128)(2,1)} %get-tuple-element.43), channel_id=1, source_target_pairs={{0,4},{1,5},{2,6},{3,7},{4,0},{5,1},{6,2},{7,3},{8,12},{9,13},{10,... | collective-permute-start | bytes 393224 | tf_op jit(solution)/shard_map/ppermute | solution.py:379
  7.2 1.3 %collective-permute-start.2 = (bf16[128,512]{1,0:T(8,128)(2,1)}, bf16[128,512]{1,0:T(8,128)(2,1)S(1)}, u32[]{:S(2)}, u32[]{:S(2)}) collective-permute-start(bf16[128,512]{1,0:T(8,128)(2,1)} %get-tuple-element.44), channel_id=1, source_target_pairs={{0,6},{1,7},{2,0},{3,1},{4,2},{5,3},{6,4},{7,5},{8,14},{9,15},{10,... | collective-permute-start | bytes 393224 | tf_op jit(solution)/shard_map/ppermute | solution.py:379
  8.6 0.9 %collective-permute-done.refs_1_._ = bf16[128,512]{1,0:T(8,128)(2,1)S(1)} collective-permute-done((bf16[128,512]{1,0:T(8,128)(2,1)}, bf16[128,512]{1,0:T(8,128)(2,1)S(1)}, u32[]{:S(2)}, u32[]{:S(2)}) %collective-permute-start) | collective-permute-done | bytes 131104 | tf_op jit(solution)/shard_map/ppermute | solution.py:379
  9.5 1.2 %copy-done.1 = bf16[128,4096]{1,0:T(8,128)(2,1)S(1)} copy-done((bf16[128,4096]{1,0:T(8,128)(2,1)S(1)}, bf16[128,4096]{1,0:T(8,128)(2,1)}, u32[]{:S(2)}) %copy-start.1) | copy-done | bytes 1048600
  10.7 1.2 %copy-done.2 = bf16[128,4096]{1,0:T(8,128)(2,1)S(1)} copy-done((bf16[128,4096]{1,0:T(8,128)(2,1)S(1)}, bf16[128,4096]{1,0:T(8,128)(2,1)}, u32[]{:S(2)}) %copy-start.2) | copy-done | bytes 1048600
  11.9 0.5 shard_map.120
  12.4 0.0 copy-start
  12.4 1.0 %copy-done = bf16[4,128,1024]{2,1,0:T(8,128)(2,1)} copy-done((bf16[4,128,1024]{2,1,0:T(8,128)(2,1)}, bf16[4,128,1024]{2,1,0:T(8,128)(2,1)S(1)}, u32[]{:S(2)}) %copy-start) | copy-done | bytes 1048600
  13.4 0.1 collective-permute-done.1.refs_2_
  13.4 0.0 collective-permute-done.2.refs_3_
  13.4 0.0 copy-done.3
  13.5 0.6 copy-done.6
  14.1 0.0 copy-done.7
  14.2 0.0 copy-start.4
  14.2 0.6 copy-done.4
  14.7 5.9 %all-to-all-start = ((bf16[4,128,1024]{2,1,0:T(8,128)(2,1)}), bf16[4,128,1024]{2,1,0:T(8,128)(2,1)S(1)}, u32[]{:S(2)}, u32[]{:S(2)}) async-start(bf16[4,128,1024]{2,1,0:T(8,128)(2,1)} %shard_map.121), calls=%async_computation | async-start | bytes 2097152 | tf_op jit(solution)/shard_map/all_to_all | solution.py:427
  20.7 3.0 %collective-permute-start.3 = (bf16[512,512]{1,0:T(8,128)(2,1)S(1)}, bf16[512,512]{1,0:T(8,128)(2,1)S(1)}, u32[]{:S(2)}, u32[]{:S(2)}) collective-permute-start(bf16[512,512]{1,0:T(8,128)(2,1)S(1)} %get-tuple-element.46.refs_2_.kv_ref), channel_id=1, source_target_pairs={{0,1},{1,0},{2,3},{3,2},{4,5},{5,4},{6,7},{7,6},{8,9},{9,8},{10,11... | collective-permute-start | bytes 1572872 | tf_op jit(solution)/shard_map/ppermute | solution.py:389
  23.7 2.0 %collective-permute-start.4 = (bf16[128,1024]{1,0:T(8,128)(2,1)S(1)}, bf16[128,1024]{1,0:T(8,128)(2,1)S(1)}, u32[]{:S(2)}, u32[]{:S(2)}) collective-permute-start(bf16[128,1024]{1,0:T(8,128)(2,1)S(1)} %get-tuple-element.48), channel_id=1, source_target_pairs={{0,2},{1,3},{2,4},{3,5},{4,6},{5,7},{6,0},{7,1},{8,10},{9,11},{10,... | collective-permute-start | bytes 786440 | tf_op jit(solution)/shard_map/ppermute | solution.py:379
  25.7 2.7 %collective-permute-start.5 = (bf16[128,1024]{1,0:T(8,128)(2,1)S(1)}, bf16[128,1024]{1,0:T(8,128)(2,1)}, u32[]{:S(2)}, u32[]{:S(2)}) collective-permute-start(bf16[128,1024]{1,0:T(8,128)(2,1)S(1)} %get-tuple-element.49), channel_id=1, source_target_pairs={{0,4},{1,5},{2,6},{3,7},{4,0},{5,1},{6,2},{7,3},{8,12},{9,13},{10,... | collective-permute-start | bytes 786440 | tf_op jit(solution)/shard_map/ppermute | solution.py:379
  28.4 1.5 %collective-permute-start.6 = (bf16[128,1024]{1,0:T(8,128)(2,1)S(1)}, bf16[128,1024]{1,0:T(8,128)(2,1)}, u32[]{:S(2)}, u32[]{:S(2)}) collective-permute-start(bf16[128,1024]{1,0:T(8,128)(2,1)S(1)} %get-tuple-element.50), channel_id=1, source_target_pairs={{0,6},{1,7},{2,0},{3,1},{4,2},{5,3},{6,4},{7,5},{8,14},{9,15},{10,... | collective-permute-start | bytes 786440 | tf_op jit(solution)/shard_map/ppermute | solution.py:379
  29.9 0.1 copy.15.refs_0_
  29.9 2.8 %collective-permute-done.3.refs_3_ = bf16[512,512]{1,0:T(8,128)(2,1)S(1)} collective-permute-done((bf16[512,512]{1,0:T(8,128)(2,1)S(1)}, bf16[512,512]{1,0:T(8,128)(2,1)S(1)}, u32[]{:S(2)}, u32[]{:S(2)}) %collective-permute-start.3) | collective-permute-done | bytes 524320 | tf_op jit(solution)/shard_map/ppermute | solution.py:389
  32.8 4.6 %all-to-all-done = bf16[4,128,1024]{2,1,0:T(8,128)(2,1)S(1)} async-done(((bf16[4,128,1024]{2,1,0:T(8,128)(2,1)}), bf16[4,128,1024]{2,1,0:T(8,128)(2,1)S(1)}, u32[]{:S(2)}, u32[]{:S(2)}) %all-to-all-start) | async-done | bytes 1048608 | tf_op jit(solution)/shard_map/all_to_all | solution.py:427
  37.3 6.1 %shard_map.122 = (bf16[128,1024]{1,0:T(8,128)(2,1)S(1)}, bf16[128,1024]{1,0:T(8,128)(2,1)S(1)}, bf16[128,1024]{1,0:T(8,128)(2,1)S(1)}, bf16[128,1024]{1,0:T(8,12...) custom-call(s32[16,8]{1,0:T(8,128)S(1)} %copy.15.refs_0_, ...), custom_call_target="tpu_custom_call" | custom-call | flops 2013265920 | bytes 4194304 | tf_op jit(solution)/shard_map/pallas_call | solution.py:311
  43.5 0.0 collective-permute-done.4.refs_5_
  43.5 0.7 collective-permute-done.5.refs_6_
  44.3 0.0 collective-permute-done.6.refs_7_
  44.3 6.9 %shard_map.123 = (bf16[128,2048]{1,0:T(8,128)(2,1)S(1)}, bf16[128,2048]{1,0:T(8,128)(2,1)S(1)}, bf16[128,2048]{1,0:T(8,128)(2,1)S(1)}, bf16[128,2048]{1,0:T(8,12...) custom-call(s32[16,8]{1,0:T(8,128)S(1)} %copy.15.refs_0_, ...), custom_call_target="tpu_custom_call" | custom-call | flops 2013265920 | bytes 4194304 | tf_op jit(solution)/shard_map/pallas_call | solution.py:311
  51.2 2.6 %collective-permute-start.10 = (bf16[512,512]{1,0:T(8,128)(2,1)S(1)}, bf16[512,512]{1,0:T(8,128)(2,1)S(1)}, u32[]{:S(2)}, u32[]{:S(2)}) collective-permute-start(bf16[512,512]{1,0:T(8,128)(2,1)S(1)} %get-tuple-element.66), channel_id=1, source_target_pairs={{0,1},{1,0},{2,3},{3,2},{4,5},{5,4},{6,7},{7,6},{8,9},{9,8},{10,11... | collective-permute-start | bytes 1572872 | tf_op jit(solution)/shard_map/ppermute | solution.py:389
  53.7 0.4 collective-permute-start.7
  54.1 3.1 %collective-permute-start.8 = (bf16[128,2048]{1,0:T(8,128)(2,1)S(1)}, bf16[128,2048]{1,0:T(8,128)(2,1)S(1)}, u32[]{:S(2)}, u32[]{:S(2)}) collective-permute-start(bf16[128,2048]{1,0:T(8,128)(2,1)S(1)} %get-tuple-element.60), channel_id=1, source_target_pairs={{0,4},{1,5},{2,6},{3,7},{4,0},{5,1},{6,2},{7,3},{8,12},{9,13},{10,... | collective-permute-start | bytes 1572872 | tf_op jit(solution)/shard_map/ppermute | solution.py:379
  57.2 0.3 collective-permute-start.9
  57.5 15.8 %all_to_all.10.refs_3_ = f32[32,2,128]{2,1,0:T(2,128)S(1)} all-to-all(f32[32,2,128]{2,1,0:T(2,128)S(1)} %get-tuple-element.67), channel_id=1, replica_groups={{0,1,8,9,16,17,24,25,32,33,40,41,48,49,56,57,64,65,72,73,80,81,88,89,96..., dimensions={0} | all-to-all | bytes 65536 | tf_op jit(solution)/shard_map/all_to_all | solution.py:441
  73.3 0.0 collective-permute-done.10.refs_2_
  73.3 0.5 shard_map.125
  73.8 0.6 collective-permute-start.11
  74.3 2.4 %collective-permute-start.12 = (bf16[144,512]{1,0:T(8,128)(2,1)S(1)}, bf16[144,512]{1,0:T(8,128)(2,1)S(1)}, u32[]{:S(2)}, u32[]{:S(2)}) collective-permute-start(bf16[144,512]{1,0:T(8,128)(2,1)S(1)} %get-tuple-element.70), channel_id=1, source_target_pairs={{0,4},{1,5},{2,6},{3,7},{4,0},{5,1},{6,2},{7,3},{8,12},{9,13},{10,... | collective-permute-start | bytes 442376 | tf_op jit(solution)/shard_map/ppermute | solution.py:379
  76.7 0.0 collective-permute-done.7.refs_1_
  76.7 0.8 collective-permute-start.13
  77.5 0.0 collective-permute-done.8.refs_2_
  77.5 0.0 collective-permute-done.9.refs_3_
  77.5 1.4 %shard_map.124 = (bf16[128,4096]{1,0:T(8,128)(2,1)}, bf16[128,4096]{1,0:T(8,128)(2,1)}) custom-call(bf16[128,2048]{1,0:T(8,128)(2,1)S(1)} %get-tuple-element.58.refs_0_, bf16[128,2048]{1,0:T(8,128)(2,1)S(1)} %collective-permute-done.7.refs_1_, bf16[128,2048]{1,0:T(8,128)(2,1)S(1)} %collective-permute-done.8.refs_2_, ...), custom_call_target="tpu_custom_call" | custom-call | tf_op jit(solution)/shard_map/pallas_call | solution.py:453
  78.9 4.9 %collective-permute-done.11.refs_1_ = bf16[144,512]{1,0:T(8,128)(2,1)S(1)} collective-permute-done((bf16[144,512]{1,0:T(8,128)(2,1)S(1)}, bf16[144,512]{1,0:T(8,128)(2,1)S(1)}, u32[]{:S(2)}, u32[]{:S(2)}) %collective-permute-start.11) | collective-permute-done | bytes 147488 | tf_op jit(solution)/shard_map/ppermute | solution.py:379
  83.8 0.0 collective-permute-done.12.refs_2_
  83.8 0.6 collective-permute-done.13.refs_3_
  84.4 1.4 %shard_map.126 = (bf16[128,1024]{1,0:T(8,128)(2,1)}, bf16[128,1024]{1,0:T(8,128)(2,1)}, f32[1,128]{1,0:T(1,128)}, f32[1,128]{1,0:T(1,128)}) custom-call(bf16[144,512]{1,0:T(8,128)(2,1)S(1)} %get-tuple-element.68.refs_0_, bf16[144,512]{1,0:T(8,128)(2,1)S(1)} %collective-permute-done.11.refs_1_, bf16[144,512]{1,0:T(8,128)(2,1)S(1)} %collective-permute-done.12.refs_2_, ...), custom_call_target="tpu_custom_call" | custom-call | tf_op jit(solution)/shard_map/pallas_call | solution.py:463
  (11 shorter events, 0.1 us)
Async XLA Ops:
  2.6 6.9 %collective-permute-start = (bf16[128,512]{1,0:T(8,128)(2,1)}, bf16[128,512]{1,0:T(8,128)(2,1)S(1)}, u32[]{:S(2)}, u32[]{:S(2)}) collective-permute-start(bf16[128,512]{1,0:T(8,128)(2,1)} %get-tuple-element.42), channel_id=1, source_target_pairs={{0,2},{1,3},{2,4},{3,5},{4,6},{5,7},{6,0},{7,1},{8,10},{9,11},{10,... | collective-permute-start | bytes 393224 | tf_op jit(solution)/shard_map/ppermute | solution.py:379
  4.3 9.1 %collective-permute-start.1 = (bf16[128,512]{1,0:T(8,128)(2,1)}, bf16[128,512]{1,0:T(8,128)(2,1)S(1)}, u32[]{:S(2)}, u32[]{:S(2)}) collective-permute-start(bf16[128,512]{1,0:T(8,128)(2,1)} %get-tuple-element.43), channel_id=1, source_target_pairs={{0,4},{1,5},{2,6},{3,7},{4,0},{5,1},{6,2},{7,3},{8,12},{9,13},{10,... | collective-permute-start | bytes 393224 | tf_op jit(solution)/shard_map/ppermute | solution.py:379
  7.2 6.2 %collective-permute-start.2 = (bf16[128,512]{1,0:T(8,128)(2,1)}, bf16[128,512]{1,0:T(8,128)(2,1)S(1)}, u32[]{:S(2)}, u32[]{:S(2)}) collective-permute-start(bf16[128,512]{1,0:T(8,128)(2,1)} %get-tuple-element.44), channel_id=1, source_target_pairs={{0,6},{1,7},{2,0},{3,1},{4,2},{5,3},{6,4},{7,5},{8,14},{9,15},{10,... | collective-permute-start | bytes 393224 | tf_op jit(solution)/shard_map/ppermute | solution.py:379
  9.5 1.2 %copy-start.1 = (bf16[128,4096]{1,0:T(8,128)(2,1)S(1)}, bf16[128,4096]{1,0:T(8,128)(2,1)}, u32[]{:S(2)}) copy-start(bf16[128,4096]{1,0:T(8,128)(2,1)} %q_ref.1) | copy-start | bytes 3145732
  10.7 1.2 %copy-start.2 = (bf16[128,4096]{1,0:T(8,128)(2,1)S(1)}, bf16[128,4096]{1,0:T(8,128)(2,1)}, u32[]{:S(2)}) copy-start(bf16[128,4096]{1,0:T(8,128)(2,1)} %g_ref.1) | copy-start | bytes 3145732
  11.9 1.5 %copy-start.3 = (bf16[128,512]{1,0:T(8,128)(2,1)S(1)}, bf16[128,512]{1,0:T(8,128)(2,1)}, u32[]{:S(2)}) copy-start(bf16[128,512]{1,0:T(8,128)(2,1)} %get-tuple-element.41.refs_0_) | copy-start | bytes 393220
  12.4 1.0 %copy-start = (bf16[4,128,1024]{2,1,0:T(8,128)(2,1)}, bf16[4,128,1024]{2,1,0:T(8,128)(2,1)S(1)}, u32[]{:S(2)}) copy-start(bf16[4,128,1024]{2,1,0:T(8,128)(2,1)S(1)} %get-tuple-element.51.refs_0_) | copy-start | bytes 3145732
  13.4 0.7 copy-start.6
  13.4 0.7 copy-start.7
  14.2 0.6 copy-start.4
  14.7 22.6 %all-to-all-start = ((bf16[4,128,1024]{2,1,0:T(8,128)(2,1)}), bf16[4,128,1024]{2,1,0:T(8,128)(2,1)S(1)}, u32[]{:S(2)}, u32[]{:S(2)}) async-start(bf16[4,128,1024]{2,1,0:T(8,128)(2,1)} %shard_map.121), calls=%async_computation | async-start | bytes 2097152 | tf_op jit(solution)/shard_map/all_to_all | solution.py:427
  20.7 9.2 %copy-start.8 = (s32[16,8]{0,1:T(8,128)S(1)}, s32[16,8]{0,1:T(8,128)}, u32[]{:S(2)}) copy-start(s32[16,8]{0,1:T(8,128)} %param.13) | copy-start | bytes 1540
  20.7 12.1 %collective-permute-start.3 = (bf16[512,512]{1,0:T(8,128)(2,1)S(1)}, bf16[512,512]{1,0:T(8,128)(2,1)S(1)}, u32[]{:S(2)}, u32[]{:S(2)}) collective-permute-start(bf16[512,512]{1,0:T(8,128)(2,1)S(1)} %get-tuple-element.46.refs_2_.kv_ref), channel_id=1, source_target_pairs={{0,1},{1,0},{2,3},{3,2},{4,5},{5,4},{6,7},{7,6},{8,9},{9,8},{10,11... | collective-permute-start | bytes 1572872 | tf_op jit(solution)/shard_map/ppermute | solution.py:389
  23.7 19.8 %collective-permute-start.4 = (bf16[128,1024]{1,0:T(8,128)(2,1)S(1)}, bf16[128,1024]{1,0:T(8,128)(2,1)S(1)}, u32[]{:S(2)}, u32[]{:S(2)}) collective-permute-start(bf16[128,1024]{1,0:T(8,128)(2,1)S(1)} %get-tuple-element.48), channel_id=1, source_target_pairs={{0,2},{1,3},{2,4},{3,5},{4,6},{5,7},{6,0},{7,1},{8,10},{9,11},{10,... | collective-permute-start | bytes 786440 | tf_op jit(solution)/shard_map/ppermute | solution.py:379
  25.7 18.5 %collective-permute-start.5 = (bf16[128,1024]{1,0:T(8,128)(2,1)S(1)}, bf16[128,1024]{1,0:T(8,128)(2,1)}, u32[]{:S(2)}, u32[]{:S(2)}) collective-permute-start(bf16[128,1024]{1,0:T(8,128)(2,1)S(1)} %get-tuple-element.49), channel_id=1, source_target_pairs={{0,4},{1,5},{2,6},{3,7},{4,0},{5,1},{6,2},{7,3},{8,12},{9,13},{10,... | collective-permute-start | bytes 786440 | tf_op jit(solution)/shard_map/ppermute | solution.py:379
  28.4 15.9 %collective-permute-start.6 = (bf16[128,1024]{1,0:T(8,128)(2,1)S(1)}, bf16[128,1024]{1,0:T(8,128)(2,1)}, u32[]{:S(2)}, u32[]{:S(2)}) collective-permute-start(bf16[128,1024]{1,0:T(8,128)(2,1)S(1)} %get-tuple-element.50), channel_id=1, source_target_pairs={{0,6},{1,7},{2,0},{3,1},{4,2},{5,3},{6,4},{7,5},{8,14},{9,15},{10,... | collective-permute-start | bytes 786440 | tf_op jit(solution)/shard_map/ppermute | solution.py:379
  29.9 7.4 %copy-start.5 = (f32[2,128]{1,0:T(2,128)S(1)}, f32[2,128]{1,0:T(2,128)}, u32[]{:S(2)}) copy-start(f32[2,128]{1,0:T(2,128)} %copy-done.4) | copy-start | bytes 3076
  51.2 22.1 %collective-permute-start.10 = (bf16[512,512]{1,0:T(8,128)(2,1)S(1)}, bf16[512,512]{1,0:T(8,128)(2,1)S(1)}, u32[]{:S(2)}, u32[]{:S(2)}) collective-permute-start(bf16[512,512]{1,0:T(8,128)(2,1)S(1)} %get-tuple-element.66), channel_id=1, source_target_pairs={{0,1},{1,0},{2,3},{3,2},{4,5},{5,4},{6,7},{7,6},{8,9},{9,8},{10,11... | collective-permute-start | bytes 1572872 | tf_op jit(solution)/shard_map/ppermute | solution.py:389
  53.7 23.0 %collective-permute-start.7 = (bf16[128,2048]{1,0:T(8,128)(2,1)S(1)}, bf16[128,2048]{1,0:T(8,128)(2,1)S(1)}, u32[]{:S(2)}, u32[]{:S(2)}) collective-permute-start(bf16[128,2048]{1,0:T(8,128)(2,1)S(1)} %get-tuple-element.59), channel_id=1, source_target_pairs={{0,2},{1,3},{2,4},{3,5},{4,6},{5,7},{6,0},{7,1},{8,10},{9,11},{10,... | collective-permute-start | bytes 1572872 | tf_op jit(solution)/shard_map/ppermute | solution.py:379
  54.1 23.4 %collective-permute-start.8 = (bf16[128,2048]{1,0:T(8,128)(2,1)S(1)}, bf16[128,2048]{1,0:T(8,128)(2,1)S(1)}, u32[]{:S(2)}, u32[]{:S(2)}) collective-permute-start(bf16[128,2048]{1,0:T(8,128)(2,1)S(1)} %get-tuple-element.60), channel_id=1, source_target_pairs={{0,4},{1,5},{2,6},{3,7},{4,0},{5,1},{6,2},{7,3},{8,12},{9,13},{10,... | collective-permute-start | bytes 1572872 | tf_op jit(solution)/shard_map/ppermute | solution.py:379
  57.2 20.3 %collective-permute-start.9 = (bf16[128,2048]{1,0:T(8,128)(2,1)S(1)}, bf16[128,2048]{1,0:T(8,128)(2,1)S(1)}, u32[]{:S(2)}, u32[]{:S(2)}) collective-permute-start(bf16[128,2048]{1,0:T(8,128)(2,1)S(1)} %get-tuple-element.61), channel_id=1, source_target_pairs={{0,6},{1,7},{2,0},{3,1},{4,2},{5,3},{6,4},{7,5},{8,14},{9,15},{10,... | collective-permute-start | bytes 1572872 | tf_op jit(solution)/shard_map/ppermute | solution.py:379
  73.8 10.0 %collective-permute-start.11 = (bf16[144,512]{1,0:T(8,128)(2,1)S(1)}, bf16[144,512]{1,0:T(8,128)(2,1)S(1)}, u32[]{:S(2)}, u32[]{:S(2)}) collective-permute-start(bf16[144,512]{1,0:T(8,128)(2,1)S(1)} %get-tuple-element.69), channel_id=1, source_target_pairs={{0,2},{1,3},{2,4},{3,5},{4,6},{5,7},{6,0},{7,1},{8,10},{9,11},{10,... | collective-permute-start | bytes 442376 | tf_op jit(solution)/shard_map/ppermute | solution.py:379
  74.3 9.4 %collective-permute-start.12 = (bf16[144,512]{1,0:T(8,128)(2,1)S(1)}, bf16[144,512]{1,0:T(8,128)(2,1)S(1)}, u32[]{:S(2)}, u32[]{:S(2)}) collective-permute-start(bf16[144,512]{1,0:T(8,128)(2,1)S(1)} %get-tuple-element.70), channel_id=1, source_target_pairs={{0,4},{1,5},{2,6},{3,7},{4,0},{5,1},{6,2},{7,3},{8,12},{9,13},{10,... | collective-permute-start | bytes 442376 | tf_op jit(solution)/shard_map/ppermute | solution.py:379
  76.7 7.7 %collective-permute-start.13 = (bf16[144,512]{1,0:T(8,128)(2,1)S(1)}, bf16[144,512]{1,0:T(8,128)(2,1)S(1)}, u32[]{:S(2)}, u32[]{:S(2)}) collective-permute-start(bf16[144,512]{1,0:T(8,128)(2,1)S(1)} %get-tuple-element.71), channel_id=1, source_target_pairs={{0,6},{1,7},{2,0},{3,1},{4,2},{5,3},{6,4},{7,5},{8,14},{9,15},{10,... | collective-permute-start | bytes 442376 | tf_op jit(solution)/shard_map/ppermute | solution.py:379
